TPU v7x, 32 devices: a whole 2x2x4 slice. The times are simulated.
32 devices in a mesh: dp: 16 (over z, y, x), mp: 2 (over core).
Axes of the slice: x: 2, y: 2, z: 4, core: 2. Of those that a mesh axis runs over, the one named last changes fastest.
Arguments:
- dec_input: bfloat16 [16, 512, 768], P('dp'), may hold values from -6 to 6
- out_grad: bfloat16 [16, 512, 768], P('dp'), may hold values from -8 to 8
- enc_feats: bfloat16 [16, 2, 16, 128, 768], P('dp', 'mp'), may hold values from -16 to 16
- mem_lengths: int32 [16], replicated, may hold values from 256 to 4096, as said below
- dec_lengths: int32 [16], replicated, may hold values from 128 to 512, as said below
- doc_owner: int32 [16], replicated, may hold values from 0 to 15, each once
- group_gain: float32 [768], replicated, may hold values from 0.5 to 1.5
- group_bias: float32 [768], replicated, may hold values from -3 to 3
- conv_weight: bfloat16 [768, 768], replicated, may hold values from -0.21875 to 0.21875
- cross_kv: bfloat16 [768, 2, 768], replicated, may hold values from -0.21875 to 0.21875
- self_gain: float32 [768], replicated, may hold values from 0.5 to 1.5
- self_qkv: bfloat16 [768, 3, 768], P(None, None, 'mp'), may hold values from -0.21875 to 0.21875
- self_out: bfloat16 [768, 768], P('mp'), may hold values from -2 to 2
- cross_gain: float32 [768], replicated, may hold values from 0.5 to 1.5
- cross_query: bfloat16 [768, 768], P(None, 'mp'), may hold values from -0.21875 to 0.21875
- cross_out: bfloat16 [768, 768], P('mp'), may hold values from -6 to 6
- ffn_gain: float32 [768], replicated, may hold values from 0.5 to 1.5
- ffn_in: bfloat16 [768, 3072], P(None, 'mp'), may hold values from -0.21875 to 0.21875
- ffn_out: bfloat16 [3072, 768], P('mp'), may hold values from -0.109375 to 0.109375
Outputs:
- layer_out: bfloat16 [16, 512, 768], P('dp')
- input_grad: float32 [16, 512, 768], P('dp')
- memory_grad: float32 [16, 2, 16, 128, 768], P('dp', 'mp')
- group_gain_grad: float32 [768], P('dp')
- group_bias_grad: float32 [768], P('dp')
- conv_grad: float32 [768, 768], P('dp')
- cross_kv_grad: float32 [768, 2, 768], P('dp')
- self_gain_grad: float32 [768], P('dp')
- self_qkv_grad: float32 [768, 3, 768], P('dp', None, 'mp')
- self_out_grad: float32 [768, 768], P('mp', 'dp')
- cross_gain_grad: float32 [768], P('dp')
- cross_query_grad: float32 [768, 768], P('dp', 'mp')
- cross_out_grad: float32 [768, 768], P('mp', 'dp')
- ffn_gain_grad: float32 [768], P('dp')
- ffn_in_grad: float32 [768, 3072], P('dp', 'mp')
- ffn_out_grad: float32 [3072, 768], P('mp', 'dp')
Inputs may be any that keep to these rules, and one draw needn't show every extreme that they name: `mem_lengths`: one document, drawn from the seed, has exactly 4096 memory tokens. `dec_lengths`: one slot, drawn from the seed, has exactly 512 decoder tokens. `doc_owner`: each document is read by exactly one decoder slot.
All inputs are finite; a program needn't handle non-finite values.
Results may differ from a plain program's by a relative error of at most 0.015.
Values may be sent and summed in bfloat16 or wider, within the bound.
No kernel may reach another device: no remote copies, remote signals or barrier semaphores. Data moves between devices by JAX's collectives and lax.ppermute only.
A program may use at most 256 MiB of HBM per device.

v0:
```python
from functools import partial

import jax
import jax.numpy as jnp
from jax import lax
from jax.experimental import pallas as pl
from jax.experimental.pallas import tpu as pltpu
from jax.sharding import PartitionSpec as P

HD = 64
GROUPS = 32
DEC = 512


norm_eps = 1e-06
group_eps = 1e-05
masked_fill = -1000000000.0
largest_sum = 1e17
vmem_budget = 16 * 1024 * 1024
vmem_large = 48 * 1024 * 1024


def room(chips):
    return vmem_budget if chips <= 16 else vmem_large


heavy = pl.CostEstimate(flops=10**10, bytes_accessed=10**7, transcendentals=10**7)
low_type = jnp.bfloat16
wide_type = jnp.float32


def dot_wide(left, right):
    return jnp.dot(left, right, preferred_element_type=wide_type)


def dot_rows(left, right):
    return lax.dot_general(left, right, (((0,), (0,)), ((), ())), preferred_element_type=wide_type)


def dot_columns(left, right):
    return lax.dot_general(left, right, (((1,), (1,)), ((), ())), preferred_element_type=wide_type)


def norm_rows(values, gain):
    factor = lax.rsqrt(jnp.mean(values * values, axis=-1, keepdims=True) + norm_eps)
    return (values * factor * gain, factor)


def norm_rows_back(values, factor, gain, incoming):
    scaled = incoming * gain
    inward = factor * scaled - values * factor * factor * factor * jnp.mean(
        scaled * values, axis=-1, keepdims=True
    )
    gain_grad = jnp.sum(incoming * values * factor, axis=0)
    return (inward, gain_grad)


def other_core(values):
    return lax.ppermute(values, "mp", [(0, 1), (1, 0)])


def core_total(partial_sum):
    return partial_sum + other_core(partial_sum)


tie = lax.optimization_barrier


class ScatterSums:
    def __init__(self, arrays, orders, chip_index):
        chips = arrays[0].shape[0]
        self.chip_index = chip_index
        self.bits = chips.bit_length() - 1
        self.orders = [list(order) for order in orders]
        self.left = [list(range(self.bits - 1, -1, -1)) for _ in arrays]
        self.current = [array.reshape((2,) * self.bits + array.shape[1:]) for array in arrays]
        self.kept = self.sent = self.came = None

    def copied(self):
        other = object.__new__(ScatterSums)
        other.chip_index, other.bits = self.chip_index, self.bits
        other.orders = [list(order) for order in self.orders]
        other.left = [list(left) for left in self.left]
        other.current, other.kept, other.sent, other.came = self.current, self.kept, self.sent, self.came
        return other

    def begin(self):
        self.kept, self.sent = [], []
        for number, order in enumerate(self.orders):
            axis = self.left[number].index(order[0])
            mine = (self.chip_index >> order[0]) & 1
            self.sent.append(lax.dynamic_index_in_dim(self.current[number], 1 - mine, axis, False))
            self.kept.append(lax.dynamic_index_in_dim(self.current[number], mine, axis, False))
            self.left[number].pop(axis)

    def ahead_of(self, value):
        self.sent, value = tie((self.sent, value))
        return value

    def send(self):
        chips = 1 << self.bits
        self.came = [
            lax.ppermute(sent, "dp", [(chip, chip ^ (1 << order[0])) for chip in range(chips)])
            for sent, order in zip(self.sent, self.orders)
        ]

    def behind(self, value):
        self.came, value = tie((self.came, value))
        return value

    def merge(self):
        merged = []
        for number, order in enumerate(self.orders):
            total = self.kept[number].astype(wide_type) + self.came[number].astype(wide_type)
            order.pop(0)
            merged.append(total.astype(self.current[number].dtype) if order else total)
        self.current = merged

    def step(self):
        self.begin()
        self.send()
        self.merge()

    def finish(self):
        while self.orders[0]:
            self.step()
        return self.current


def merge_kernel(facts, *refs, plans):
    count = len(plans)
    outs = list(refs[2 * count :])
    for plan, kept, came in zip(plans, refs[:count], refs[count : 2 * count]):
        entries, after, turn = plan["entries"], plan["after"], plan["turn"]

        def total(entry, kept=kept, came=came, after=after):
            own = kept[entry] if after is None else kept[entry >> after, 0, entry & ((1 << after) - 1)]
            return own.astype(wide_type) + came[entry].astype(wide_type)

        if turn is None:
            outs.pop(0)[...] = total(0)
            continue
        sent_out, kept_out = outs.pop(0), outs.pop(0)
        bit, behind = turn
        mine = (facts[0] >> bit) & 1
        for place in range(entries // 2):
            base = (place >> behind << (behind + 1)) | (place & ((1 << behind) - 1))
            kept_out[place] = total(base + (mine << behind)).astype(low_type)
            sent_out[place] = total(base + ((1 - mine) << behind)).astype(low_type)


class Part:
    def __init__(self, array, order):
        self.kept, self.order = array, order
        self.sent = self.came = self.total = None
        self.step = 0
        self.left = tuple(range(len(order) - 1, -1, -1))

    def copied(self):
        other = object.__new__(Part)
        other.__dict__.update(self.__dict__)
        return other


class Sums:
    def __init__(self, parts, chip_index):
        self.parts, self.chip_index = parts, chip_index

    @staticmethod
    def of(arrays, orders, chip_index):
        return Sums([Part(array, order) for array, order in zip(arrays, orders)], chip_index)

    def copied(self):
        return Sums([part.copied() for part in self.parts], self.chip_index)

    def joined(self, *others):
        return Sums([part for sums in (self, *others) for part in sums.parts], self.chip_index)

    def state(self):
        return [(part.kept, part.came) for part in self.parts]

    def stepped(self):
        other = self.copied()
        for part in other.parts:
            part.left = tuple(bit for bit in part.left if bit != part.order[part.step])
            part.step += 1
        return other

    def with_state(self, state):
        other = self.copied()
        for part, (kept, came) in zip(other.parts, state):
            part.kept, part.came = kept, came
        return other

    @property
    def going(self):
        return [part for part in self.parts if part.total is None]

    @property
    def totals(self):
        return [part.total for part in self.parts]

    def start(self, value):
        for part in self.parts:
            chips = part.kept.shape[0]
            behind = part.order[0]
            ahead = len(part.order) - 1 - behind
            view = part.kept.reshape((1 << ahead, 2, 1 << behind) + part.kept.shape[1:])
            mine = (self.chip_index >> behind) & 1
            sent = lax.dynamic_index_in_dim(view, 1 - mine, 1, False)
            part.sent = sent.reshape((chips // 2,) + part.kept.shape[1:])
            part.kept = view
        return self.leave(self.parts, value)

    def leave(self, parts, value):
        sent, value = tie(([part.sent for part in parts], value))
        for part, leaving in zip(parts, sent):
            chips = 1 << len(part.order)
            bit = part.order[part.step]
            part.came = lax.ppermute(leaving, "dp", [(chip, chip ^ (1 << bit)) for chip in range(chips)])
        return value

    def round(self, value):
        parts = self.going
        came, value = tie(([part.came for part in parts], value))
        plans, in_specs, out_specs, out_shape = [], [], [], []
        for part, arrived in zip(parts, came):
            part.came = arrived
            entries, rows, columns = arrived.shape
            kept, bit = part.kept, part.order[part.step]
            if part.step == 0:
                in_specs.append(
                    pl.BlockSpec(
                        (kept.shape[0], 1) + kept.shape[2:],
                        lambda j, facts, bit=bit: (0, (facts[0] >> bit) & 1, 0, 0, 0),
                    )
                )
            else:
                in_specs.append(whole(kept.shape))
            plan = {"entries": entries, "after": bit if part.step == 0 else None, "turn": None}
            part.left = tuple(other for other in part.left if other != bit)
            if part.left:
                following = part.order[part.step + 1]
                plan["turn"] = (following, len(part.left) - 1 - part.left.index(following))
                half = (entries // 2, rows, columns)
                out_specs += [whole(half)] * 2
                out_shape += [jax.ShapeDtypeStruct(half, low_type)] * 2
            else:
                out_specs.append(whole((rows, columns)))
                out_shape.append(jax.ShapeDtypeStruct((rows, columns), wide_type))
            plans.append(plan)
        in_specs += [whole(part.came.shape) for part in parts]
        made = pl.pallas_call(
            partial(merge_kernel, plans=plans),
            grid_spec=pltpu.PrefetchScalarGridSpec(
                num_scalar_prefetch=1, grid=(1,), in_specs=in_specs, out_specs=out_specs
            ),
            out_shape=out_shape,
            compiler_params=pltpu.CompilerParams(vmem_limit_bytes=room(1 << len(parts[0].order))),
            cost_estimate=heavy,
            name="merge_sums",
        )(
            self.chip_index[None].astype(jnp.int32),
            *[part.kept for part in parts],
            *[part.came for part in parts],
        )
        made = list(made)
        for part in parts:
            part.step += 1
            if part.left:
                part.sent, part.kept = made.pop(0), made.pop(0)
            else:
                part.total = made.pop(0)
        parts = [part for part in parts if part.left]
        return self.leave(parts, value) if parts else value


def nothing_like(work):
    def nothing():
        return jax.tree.map(lambda leaf: jnp.zeros(leaf.shape, leaf.dtype), jax.eval_shape(work))

    return nothing


def gather_kernel(owner, rows, out, held, came, gone, *, docs):
    loads = [pltpu.make_async_copy(rows.at[owner[slot]], held.at[slot], came.at[slot]) for slot in range(docs)]
    stores = [pltpu.make_async_copy(held.at[slot], out.at[slot], gone.at[slot]) for slot in range(docs)]
    for load in loads:
        load.start()
    for load, store in zip(loads, stores):
        load.wait()
        store.start()
    for store in stores:
        store.wait()


def gather_docs(memory_in, doc_owner):
    docs = memory_in.shape[0]
    return pl.pallas_call(
        partial(gather_kernel, docs=docs),
        grid_spec=pltpu.PrefetchScalarGridSpec(
            num_scalar_prefetch=1,
            grid=(),
            in_specs=[pl.BlockSpec(memory_space=pl.ANY)],
            out_specs=pl.BlockSpec(memory_space=pltpu.HBM),
            scratch_shapes=[
                pltpu.VMEM(memory_in.shape, low_type),
                pltpu.SemaphoreType.DMA((docs,)),
                pltpu.SemaphoreType.DMA((docs,)),
            ],
        ),
        out_shape=jax.ShapeDtypeStruct(memory_in.shape, low_type),
        compiler_params=pltpu.CompilerParams(vmem_limit_bytes=vmem_large),
        cost_estimate=heavy,
        name="gather_docs",
    )(doc_owner, memory_in)


def prepare_kernel(cross_kv, pair):
    width = cross_kv.shape[0]
    for side in range(2):
        pair[:, side * width : side * width + width] = cross_kv[:, side, :]


def prepare_weights(cross_kv):
    width = cross_kv.shape[0]
    return pl.pallas_call(
        prepare_kernel,
        out_shape=jax.ShapeDtypeStruct((width, 2 * width), low_type),
        compiler_params=pltpu.CompilerParams(vmem_limit_bytes=vmem_budget),
        cost_estimate=heavy,
        name="prepare_weights",
    )(cross_kv)


def moved_kernel(owner, facts, features, groups, out, stats, *, chips, count):
    step = pl.program_id(0)
    sub, width = features.shape[1:]

    @pl.when(step == 0)
    def _():
        own_group = (
            lax.broadcasted_iota(jnp.int32, (128, width), 1) // (width // GROUPS)
            == lax.broadcasted_iota(jnp.int32, (128, width), 0)
        ).astype(wide_type)
        stats[...] = jnp.dot(
            groups[0:chips].reshape(chips * 8, 128), own_group, precision=lax.Precision.HIGHEST
        ).reshape(chips, 8, width)

    position = (lax.broadcasted_iota(jnp.int32, (sub, 1), 0) * 2 + facts[1]) * chips + facts[0]

    def one(place, carry):
        slot = step * count + place
        document = owner[slot]
        normed = (features[document].astype(wide_type) - stats[slot, 0:1, :]) * stats[slot, 1:2, :]
        moved = stats[slot, 1:2, :] * (stats[slot, 2:3, :] + normed * stats[slot, 3:4, :])
        out[place] = jnp.where(position < facts[2 + document], moved, 0.0).astype(low_type)
        return carry

    lax.fori_loop(0, count, one, 0)


def moved_rows(doc_owner, facts, features, groups):
    docs, sub, width = features.shape
    count = max(docs // 4, 1)
    return pl.pallas_call(
        partial(moved_kernel, chips=docs, count=count),
        grid_spec=pltpu.PrefetchScalarGridSpec(
            num_scalar_prefetch=2,
            grid=(docs // count,),
            in_specs=[
                pl.BlockSpec(features.shape, lambda j, owner, facts: (0, 0, 0)),
                pl.BlockSpec(groups.shape, lambda j, owner, facts: (0, 0, 0)),
            ],
            out_specs=pl.BlockSpec((count, sub, width), lambda j, owner, facts: (j, 0, 0)),
            scratch_shapes=[pltpu.VMEM((docs, 8, width), wide_type)],
        ),
        out_shape=jax.ShapeDtypeStruct(features.shape, low_type),
        compiler_params=pltpu.CompilerParams(vmem_limit_bytes=room(docs)),
        cost_estimate=heavy,
        name="moved_rows",
    )(doc_owner, facts, features, groups)


def spread_kernel(owner, *refs, docs, pieces):
    rows = refs[:pieces]
    moved, out, held, taken, wide, came, also, gone = refs[pieces:]
    each = rows[0].shape[1]
    loads = [
        [
            pltpu.make_async_copy(
                piece.at[slot], held.at[slot, pl.ds(number * each, each)], came.at[slot * pieces + number]
            )
            for number, piece in enumerate(rows)
        ]
        for slot in range(docs)
    ]
    takes = [pltpu.make_async_copy(moved.at[slot], taken.at[slot], also.at[slot]) for slot in range(docs)]
    stores = [pltpu.make_async_copy(wide.at[slot], out.at[owner[slot]], gone.at[slot]) for slot in range(docs)]
    for slot in range(docs):
        for load in loads[slot]:
            load.start()
        takes[slot].start()
    for slot in range(docs):
        for load in loads[slot]:
            load.wait()
        takes[slot].wait()
        wide[slot] = held[slot].astype(wide_type) - taken[slot].astype(wide_type)
        stores[slot].start()
    for store in stores:
        store.wait()


def spread_docs(rows, moved, doc_owner):
    docs = moved.shape[0]
    pieces = len(rows)
    return pl.pallas_call(
        partial(spread_kernel, docs=docs, pieces=pieces),
        grid_spec=pltpu.PrefetchScalarGridSpec(
            num_scalar_prefetch=1,
            grid=(),
            in_specs=[pl.BlockSpec(memory_space=pl.ANY)] * (pieces + 1),
            out_specs=pl.BlockSpec(memory_space=pl.ANY),
            scratch_shapes=[
                pltpu.VMEM(moved.shape, low_type),
                pltpu.VMEM(moved.shape, low_type),
                pltpu.VMEM(moved.shape, wide_type),
                pltpu.SemaphoreType.DMA((docs * pieces,)),
                pltpu.SemaphoreType.DMA((docs,)),
                pltpu.SemaphoreType.DMA((docs,)),
            ],
        ),
        out_shape=jax.ShapeDtypeStruct(moved.shape, wide_type),
        compiler_params=pltpu.CompilerParams(vmem_limit_bytes=vmem_large),
        cost_estimate=heavy,
        name="spread_docs",
    )(doc_owner, *rows, moved)


def chunk_of(chips, sub):
    return min(sub, max(16, 512 // chips))


def live_rows(facts, start, chips, span):
    row = lax.broadcasted_iota(jnp.int32, (chips * span, 1), 0)
    chip, step = row // span, row % span
    return ((start + step) * 2 + facts[1]) * chips + chip < facts[0]


def in_branches(facts, start, chips, span, work, dead=None):
    first = (start * 2 + facts[1]) * chips
    last = ((start + span - 1) * 2 + facts[1]) * chips + chips - 1
    full = last < facts[0]
    none = first >= facts[0]

    @pl.when(full)
    def _():
        work(None)

    @pl.when(jnp.logical_not(full) & jnp.logical_not(none))
    def _():
        work(live_rows(facts, start, chips, span))

    if dead is not None:
        pl.when(none)(dead)


def whole(shape):
    return pl.BlockSpec(shape, lambda j, facts: (0,) * len(shape))


def slab(shape, span, first=0):
    return pl.BlockSpec((shape[0], span, shape[2]), lambda j, facts: (0, j + first, 0))


def memory_forward_kernel(facts, rows, stats, weight, out, *, chips, span):
    width = rows.shape[-1]
    wide = rows[...].reshape(chips * span, width).astype(wide_type)
    drive = (wide - stats[0:1, :]) * stats[1:2, :] * stats[2:3, :] + stats[3:4, :]
    hidden = (drive * (0.5 + 0.5 * jnp.tanh(0.5 * drive))).astype(low_type)
    made = wide + dot_wide(hidden, weight[...])
    out[...] = made.astype(low_type).reshape(chips, span, width)


def memory_forward(facts, rows, stats, weight):
    chips, sub, width = rows.shape
    span = chunk_of(chips, sub)
    return pl.pallas_call(
        partial(memory_forward_kernel, chips=chips, span=span),
        grid_spec=pltpu.PrefetchScalarGridSpec(
            num_scalar_prefetch=1,
            grid=(sub // span,),
            in_specs=[slab(rows.shape, span), whole(stats.shape), whole(weight.shape)],
            out_specs=slab(rows.shape, span),
        ),
        out_shape=jax.ShapeDtypeStruct(rows.shape, low_type),
        compiler_params=pltpu.CompilerParams(vmem_limit_bytes=room(chips)),
        cost_estimate=heavy,
        name="memory_forward",
    )(facts, rows, stats, weight)


def memory_backward_kernel(
    facts, rows, own, came, stats, weight, sums_in, grad_out, hidden_out, base_out, sums, groups, *, chips, span, steps
):
    step = pl.program_id(0)
    width = rows.shape[-1]
    count = chips * span

    @pl.when(step == 0)
    def _():
        sums[...] = sums_in[...]

    wide = rows[...].reshape(count, width).astype(wide_type)
    normed = (wide - stats[0:1, :]) * stats[1:2, :]
    drive = normed * stats[2:3, :] + stats[3:4, :]
    gate = 0.5 + 0.5 * jnp.tanh(0.5 * drive)
    hidden_out[...] = (drive * gate).astype(low_type).reshape(chips, span, width)
    grad = (own[...].reshape(count, width) + came[...].reshape(count, width).astype(wide_type)).astype(low_type)
    grad_out[...] = grad.reshape(chips, span, width)
    grad_act = dot_columns(grad, weight[...]) * (gate * (1.0 + drive * (1.0 - gate)))
    sums[0:1, :] += jnp.sum(grad_act, axis=0, keepdims=True)
    sums[1:2, :] += jnp.sum(grad_act * normed, axis=0, keepdims=True)
    base = grad.astype(wide_type) + grad_act * (stats[1:2, :] * stats[2:3, :])
    base_out[...] = base.astype(low_type).reshape(chips, span, width)

    @pl.when(step == steps - 1)
    def _():
        per_group = width // GROUPS
        group_of = (
            lax.broadcasted_iota(jnp.int32, (width, 128), 0) // per_group
            == lax.broadcasted_iota(jnp.int32, (width, 128), 1)
        ).astype(wide_type)
        entries = (facts[0] * per_group).astype(wide_type)
        rows_of = jnp.concatenate(
            (
                stats[0:2, :] * (0.5 / per_group),
                sums[0:2, :] * stats[2:3, :] / entries,
                jnp.zeros((4, width), wide_type),
            )
        )
        groups[...] = jnp.dot(rows_of, group_of, precision=lax.Precision.HIGHEST)


def memory_backward(facts, rows, own, came, stats, weight, sums_in, first):
    chips, sub, width = own.shape
    span = chunk_of(chips, rows.shape[1])
    block = slab(own.shape, span)
    return pl.pallas_call(
        partial(memory_backward_kernel, chips=chips, span=span, steps=sub // span),
        grid_spec=pltpu.PrefetchScalarGridSpec(
            num_scalar_prefetch=1,
            grid=(sub // span,),
            in_specs=[
                slab(rows.shape, span, first),
                block,
                block,
                whole(stats.shape),
                whole(weight.shape),
                whole(sums_in.shape),
            ],
            out_specs=[block, block, block, whole(stats.shape), whole((8, 128))],
        ),
        out_shape=[
            jax.ShapeDtypeStruct(own.shape, low_type),
            jax.ShapeDtypeStruct(own.shape, low_type),
            pltpu.HBM(own.shape, low_type),
            jax.ShapeDtypeStruct(stats.shape, wide_type),
            jax.ShapeDtypeStruct((8, 128), wide_type),
        ],
        compiler_params=pltpu.CompilerParams(vmem_limit_bytes=room(chips)),
        cost_estimate=heavy,
        name="memory_backward",
    )(facts, rows, own, came, stats, weight, sums_in)


def cross_forward_kernel(
    facts, query_t, rows, key_weight, value_weight, top_in, total_in, sum_in, pairs, top, total, gathered,
    total_here, sum_here, held, *, chips, span
):
    step = pl.program_id(0)
    half = key_weight.shape[1]
    width = rows.shape[-1]

    @pl.when(step == 0)
    def _():
        top[...] = top_in[...]
        total[...] = total_in[...]
        gathered[...] = sum_in[...]

    def work(live):
        block = rows[...].reshape(chips * span, width)
        keys = dot_wide(block, key_weight[...]).astype(low_type)
        values = dot_wide(block, value_weight[...]).astype(low_type)
        pairs[:, :, :half] = keys.reshape(chips, span, half)
        pairs[:, :, half:] = values.reshape(chips, span, half)
        heads = half // HD

        def score(head):
            made = dot_wide(keys[:, head // 2 * 128 : head // 2 * 128 + 128], query_t[head])
            return made if live is None else jnp.where(live, made, masked_fill)

        def part_of(head, weights):
            part = dot_rows(values[:, head // 2 * 128 : head // 2 * 128 + 128], weights.astype(low_type))
            return part[head % 2 * HD : head % 2 * HD + HD, :]

        def plain():
            following = score(0)
            for head in range(heads):
                scores = following
                if head + 1 < heads:
                    following = score(head + 1)
                weights = jnp.exp(scores - top[head : head + 1, :])
                total_here[head : head + 1, :] = jnp.sum(weights, axis=0, keepdims=True)
                sum_here[head * HD : head * HD + HD, :] = part_of(head, weights)

        def shifted():
            following = score(0)
            for head in range(heads):
                scores = following
                if head + 1 < heads:
                    following = score(head + 1)
                old_top = top[head : head + 1, :]
                new_top = jnp.maximum(old_top, jnp.max(scores, axis=0, keepdims=True))
                weights = jnp.exp(scores - new_top)
                shrink = jnp.exp(old_top - new_top)
                total[head : head + 1, :] = total[head : head + 1, :] * shrink + jnp.sum(
                    weights, axis=0, keepdims=True
                )
                rows_of = slice(head * HD, head * HD + HD)
                gathered[rows_of, :] = gathered[rows_of, :] * shrink + part_of(head, weights)
                top[head : head + 1, :] = new_top

        fresh = (facts[3] == 1) & (step == 0)
        held[0] = jnp.where(fresh, 1, 0)

        @pl.when(jnp.logical_not(fresh))
        def _():
            plain()
            small = jnp.max(total_here[0:heads, :]) < largest_sum
            held[0] = jnp.where(small, 0, 1)

            @pl.when(small)
            def _():
                total[0:heads, :] += total_here[0:heads, :]
                gathered[...] += sum_here[...]

        pl.when(held[0] == 1)(shifted)

    def dead():
        pairs[...] = jnp.zeros_like(pairs)

    in_branches(facts, step * span, chips, span, work, dead)


def cross_forward(facts, query_t, rows, weight, carry):
    chips, sub, width = rows.shape
    heads, _, queries = query_t.shape
    half = heads * HD
    span = chunk_of(chips, sub)
    stat = (8, queries)
    summed = (half, queries)
    return pl.pallas_call(
        partial(cross_forward_kernel, chips=chips, span=span),
        grid_spec=pltpu.PrefetchScalarGridSpec(
            num_scalar_prefetch=1,
            grid=(sub // span,),
            in_specs=[
                whole(query_t.shape),
                slab(rows.shape, span),
                pl.BlockSpec((width, half), lambda j, facts: (0, facts[2])),
                pl.BlockSpec((width, half), lambda j, facts: (0, 2 + facts[2])),
                whole(stat),
                whole(stat),
                whole(summed),
            ],
            out_specs=[slab((chips, sub, 2 * half), span), whole(stat), whole(stat), whole(summed)],
            scratch_shapes=[
                pltpu.VMEM(stat, wide_type),
                pltpu.VMEM(summed, wide_type),
                pltpu.SMEM((1,), jnp.int32),
            ],
        ),
        out_shape=[
            jax.ShapeDtypeStruct((chips, sub, 2 * half), low_type),
            jax.ShapeDtypeStruct(stat, wide_type),
            jax.ShapeDtypeStruct(stat, wide_type),
            jax.ShapeDtypeStruct(summed, wide_type),
        ],
        compiler_params=pltpu.CompilerParams(vmem_limit_bytes=room(chips)),
        cost_estimate=heavy,
        name="cross_forward",
    )(facts, query_t, rows, weight, weight, *carry)


def cross_close_kernel(gathered, top, total, weight, crossed, crossed_t, log_total, part, *, heads):
    log_total[...] = top[...] + jnp.log(jnp.maximum(total[...], 1e-30))
    for head in range(heads):
        rows = slice(head * HD, head * HD + HD)
        crossed_t[rows, :] = gathered[rows, :] / total[head : head + 1, :]
    low = crossed_t[...].T.astype(low_type)
    crossed[...] = low
    part[...] = dot_wide(low, weight[...])


def cross_close(gathered, top, total, weight):
    half, queries = gathered.shape
    return pl.pallas_call(
        partial(cross_close_kernel, heads=half // HD),
        out_shape=[
            jax.ShapeDtypeStruct((queries, half), low_type),
            jax.ShapeDtypeStruct((half, queries), wide_type),
            jax.ShapeDtypeStruct(top.shape, wide_type),
            jax.ShapeDtypeStruct((queries, weight.shape[1]), wide_type),
        ],
        compiler_params=pltpu.CompilerParams(vmem_limit_bytes=vmem_budget),
        cost_estimate=heavy,
        name="cross_close",
    )(gathered, top, total, weight)


gelu_scale = 0.7978845608028654
gelu_cubic = 0.044715


def feed_forward_kernel(
    first, own, came, gain, weight, grad_active, second, normed, both_grad, both_active, grad_normed
):
    step = pl.program_id(0)

    @pl.when(step == 0)
    def _():
        total = first[...] + (own[...] + came[...])
        second[...] = total
        factor = lax.rsqrt(jnp.mean(total * total, axis=-1, keepdims=True) + norm_eps)
        normed[...] = (total * factor * gain[...]).astype(low_type)
        grad_normed[...] = jnp.zeros_like(grad_normed)

    lifted = dot_wide(normed[...], weight[...])
    square = lifted * lifted
    bent = jnp.tanh(gelu_scale * (lifted * (1.0 + gelu_cubic * square)))
    half_up = 0.5 * (1.0 + bent)
    both_active[...] = (lifted * half_up).astype(low_type)
    slope = half_up + (0.5 * gelu_scale) * lifted * (1.0 - bent * bent) * (1.0 + 3.0 * gelu_cubic * square)
    grad_lifted = (grad_active[...].astype(wide_type) * slope).astype(low_type)
    both_grad[...] = grad_lifted
    grad_normed[...] += dot_columns(grad_lifted, weight[...])


def feed_forward(first, own, came, gain, weight, grad_active):
    rows, width = first.shape
    hidden = weight.shape[1]
    block = 512
    still = pl.BlockSpec((rows, width), lambda j: (0, 0))
    moving = pl.BlockSpec((rows, block), lambda j: (0, j))
    return pl.pallas_call(
        feed_forward_kernel,
        grid=(hidden // block,),
        in_specs=[
            still,
            still,
            still,
            pl.BlockSpec((1, width), lambda j: (0, 0)),
            pl.BlockSpec((width, block), lambda j: (0, j)),
            moving,
        ],
        out_specs=[still, still, moving, moving, still],
        out_shape=[
            jax.ShapeDtypeStruct((rows, width), wide_type),
            jax.ShapeDtypeStruct((rows, width), low_type),
            jax.ShapeDtypeStruct((rows, hidden), low_type),
            jax.ShapeDtypeStruct((rows, hidden), low_type),
            jax.ShapeDtypeStruct((rows, width), wide_type),
        ],
        compiler_params=pltpu.CompilerParams(vmem_limit_bytes=vmem_budget),
        cost_estimate=heavy,
        name="feed_forward",
    )(first, own, came, gain, weight, grad_active)


def feed_close_kernel(
    second, own, came, gain, grad_out, weight, crossed_t, grad_second, gain_grad, grad_cross, heads_out,
    heads_out_t, inner, *, heads,
):
    values = second[...]
    incoming = (own[...] + came[...]).astype(low_type).astype(wide_type)
    factor = lax.rsqrt(jnp.mean(values * values, axis=-1, keepdims=True) + norm_eps)
    scaled = incoming * gain[...]
    inward = factor * scaled - values * (factor * factor * factor) * jnp.mean(
        scaled * values, axis=-1, keepdims=True
    )
    gain_grad[...] = jnp.broadcast_to(
        jnp.sum(incoming * values * factor, axis=0, keepdims=True), gain_grad.shape
    )
    total = inward + grad_out[...].astype(wide_type)
    grad_second[...] = total
    low = total.astype(low_type)
    grad_cross[...] = low
    made = dot_columns(low, weight[...])
    made_low = made.astype(low_type)
    made_t = made_low.astype(wide_type).T
    low_t = made_t.astype(low_type)
    left = lax.broadcasted_iota(jnp.int32, (made.shape[0], 128), 1) < HD
    inner[...] = jnp.zeros_like(inner)
    for head in range(heads):
        pair = made_low[:, head // 2 * 128 : head // 2 * 128 + 128]
        keep = left if head % 2 == 0 else jnp.logical_not(left)
        heads_out[head] = jnp.where(keep, pair, jnp.zeros_like(pair))
        rows = slice(head * HD, head * HD + HD)
        own_rows = slice(head % 2 * HD, head % 2 * HD + HD)
        other_rows = slice((1 - head % 2) * HD, (1 - head % 2) * HD + HD)
        heads_out_t[head, own_rows, :] = low_t[rows, :]
        heads_out_t[head, other_rows, :] = jnp.zeros_like(low_t[rows, :])
        inner[head : head + 1, :] = jnp.sum(made_t[rows, :] * crossed_t[rows, :], axis=0, keepdims=True)


def feed_close(second, own, came, gain, grad_out, weight, crossed_t):
    rows, width = second.shape
    half = weight.shape[0]
    heads = half // HD
    return pl.pallas_call(
        partial(feed_close_kernel, heads=heads),
        out_shape=[
            jax.ShapeDtypeStruct((rows, width), wide_type),
            jax.ShapeDtypeStruct((8, width), wide_type),
            jax.ShapeDtypeStruct((rows, width), low_type),
            jax.ShapeDtypeStruct((heads, rows, 128), low_type),
            jax.ShapeDtypeStruct((heads, 128, rows), low_type),
            jax.ShapeDtypeStruct((8, rows), wide_type),
        ],
        compiler_params=pltpu.CompilerParams(vmem_limit_bytes=vmem_budget),
        cost_estimate=heavy,
        name="feed_close",
    )(second, own, came, gain, grad_out, weight, crossed_t)


def feed_weights_kernel(
    normed, grad_out, grad_cross, both_grad, both_active, crossed, left, middle, right, turned, *, steps
):
    step = pl.program_id(0)
    third = (2 * steps + 1) // 3

    @pl.when(step == 0)
    def _():
        turned[...] = normed[...].T

    @pl.when(step == steps)
    def _():
        turned[...] = grad_out[...].T

    @pl.when(step == 2 * steps)
    def _():
        turned[...] = grad_cross[...].T

    for number, out in enumerate((left, middle, right)):
        inside = (step >= number * third) & (step < number * third + third)

        @pl.when(inside & (step < steps))
        def _(out=out):
            out[...] = dot_wide(turned[...], both_grad[...]).astype(low_type)

        @pl.when(inside & (step >= steps) & (step < 2 * steps))
        def _(out=out):
            out[...] = dot_wide(turned[...], both_active[...]).astype(low_type)

        @pl.when(inside & (step == 2 * steps))
        def _(out=out):
            out[...] = dot_wide(turned[...], crossed[...]).astype(low_type)


def feed_weights(normed, grad_out, grad_cross, grad_lifted, active, crossed):
    rows, width = normed.shape
    hidden = active.shape[1]
    block = crossed.shape[1]
    steps = hidden // block
    third = (2 * steps + 1) // 3

    def piece(number):
        return pl.BlockSpec((width, block), lambda j: (0, jnp.clip(j - number * third, 0, third - 1)))

    still = pl.BlockSpec((rows, width), lambda j: (0, 0))
    return pl.pallas_call(
        partial(feed_weights_kernel, steps=steps),
        grid=(2 * steps + 1,),
        in_specs=[
            still,
            still,
            still,
            pl.BlockSpec((rows, block), lambda j: (0, jnp.minimum(j, steps - 1))),
            pl.BlockSpec((rows, block), lambda j: (0, jnp.clip(j - steps, 0, steps - 1))),
            pl.BlockSpec((rows, block), lambda j: (0, 0)),
        ],
        out_specs=[piece(number) for number in range(3)],
        out_shape=[jax.ShapeDtypeStruct((width, third * block), low_type)] * 3,
        scratch_shapes=[pltpu.VMEM((width, rows), low_type)],
        compiler_params=pltpu.CompilerParams(vmem_limit_bytes=vmem_budget),
        cost_estimate=heavy,
        name="feed_weights",
    )(normed, grad_out, grad_cross, grad_lifted, active, crossed)


def cross_backward_kernel(
    facts, query, query_t, grad, grad_t, log_total, inner, pairs, key_weight, value_weight, pair_grads,
    row_grads, query_grad, held, *, chips, span, first
):
    step = pl.program_id(0)
    width, half = key_weight.shape

    @pl.when(step == 0)
    def _():
        query_grad[...] = jnp.zeros_like(query_grad)

    def work(live):
        block = pairs[...].reshape(chips * span, 2 * half)
        heads = half // HD

        def lanes(head, shift=0):
            return block[:, shift + head // 2 * 128 : shift + head // 2 * 128 + 128]

        def products(head):
            scores = dot_wide(lanes(head), query_t[head])
            if live is not None:
                scores = jnp.where(live, scores, masked_fill)
            return scores, dot_wide(lanes(head, half), grad_t[head])

        following = products(0)
        for pair in range(heads // 2):
            lows, low_grads = [], []
            for side in range(2):
                head = pair * 2 + side
                scores, grad_probs = following
                if head + 1 < heads:
                    following = products(head + 1)
                probs = jnp.exp(scores - log_total[head : head + 1, :])
                low_grads.append((probs * (grad_probs - inner[head : head + 1, :])).astype(low_type))
                lows.append(probs.astype(low_type))
                part = dot_rows(lanes(head), low_grads[-1])
                query_grad[head * HD : head * HD + HD, :] += part[side * HD : side * HD + HD, :]
            at = pair * 128
            both = slice(pair * 2, pair * 2 + 2)
            queries = query.shape[1]
            held[:, at : at + 128] = dot_wide(
                jnp.concatenate(low_grads, axis=1), query[both].reshape(2 * queries, 128)
            ).astype(low_type)
            held[:, half + at : half + at + 128] = dot_wide(
                jnp.concatenate(lows, axis=1), grad[both].reshape(2 * queries, 128)
            ).astype(low_type)
        made = held[...]
        pair_grads[...] = made.reshape(chips, span, 2 * half)
        back = dot_columns(made[:, :half], key_weight[...]) + dot_columns(made[:, half:], value_weight[...])
        row_grads[...] = back.astype(row_grads.dtype).reshape(chips, span, width)

    def dead():
        pair_grads[...] = jnp.zeros_like(pair_grads)
        row_grads[...] = jnp.zeros_like(row_grads)

    in_branches(facts, (step + first) * span, chips, span, work, dead)


def cross_backward(facts, query, query_t, grad, grad_t, log_total, inner, pairs, weight, grad_type, first, steps):
    chips, sub, both = pairs.shape
    width = weight.shape[0]
    heads, _, queries = query_t.shape
    span = chunk_of(chips, sub)
    half = both // 2
    rows = steps * span
    pair_block = slab((chips, rows, both), span)
    row_block = slab((chips, rows, width), span)
    return pl.pallas_call(
        partial(cross_backward_kernel, chips=chips, span=span, first=first),
        grid_spec=pltpu.PrefetchScalarGridSpec(
            num_scalar_prefetch=1,
            grid=(steps,),
            in_specs=[
                whole(query.shape),
                whole(query_t.shape),
                whole(grad.shape),
                whole(grad_t.shape),
                whole(log_total.shape),
                whole(inner.shape),
                slab(pairs.shape, span, first),
                pl.BlockSpec((width, half), lambda j, facts: (0, facts[2])),
                pl.BlockSpec((width, half), lambda j, facts: (0, 2 + facts[2])),
            ],
            out_specs=[pair_block, row_block, whole((heads * HD, queries))],
            scratch_shapes=[pltpu.VMEM((chips * span, both), low_type)],
        ),
        out_shape=[
            jax.ShapeDtypeStruct((chips, rows, both), low_type),
            jax.ShapeDtypeStruct((chips, rows, width), grad_type),
            jax.ShapeDtypeStruct((heads * HD, queries), wide_type),
        ],
        compiler_params=pltpu.CompilerParams(vmem_limit_bytes=room(chips)),
        cost_estimate=heavy,
        name="cross_backward",
    )(facts, query, query_t, grad, grad_t, log_total, inner, pairs, weight, weight)


def query_back_kernel(*refs):
    *parts, weight, grad, part = refs
    total = parts[0][...]
    for other in parts[1:]:
        total = total + other[...]
    low = (total * 0.125).T.astype(low_type)
    grad[...] = low
    part[...] = dot_columns(low, weight[...])


def query_back(parts, weight):
    half, rows = parts[0].shape
    return pl.pallas_call(
        query_back_kernel,
        out_shape=[
            jax.ShapeDtypeStruct((rows, half), low_type),
            jax.ShapeDtypeStruct((rows, weight.shape[0]), wide_type),
        ],
        compiler_params=pltpu.CompilerParams(vmem_limit_bytes=vmem_budget),
        cost_estimate=heavy,
        name="query_back",
    )(*parts, weight)


def memory_weights_kernel(facts, *refs, pieces, chips, span, steps):
    rows, other = refs[:2]
    sets = [refs[2 + 4 * piece : 6 + 4 * piece] for piece in range(pieces)]
    pair_out, keep_out, send_out, pair_sum, conv_sum = refs[2 + 4 * pieces :]
    step = pl.program_id(0)
    count = chips * span
    each = steps // pieces

    def flat(ref):
        return ref[...].reshape(count, ref.shape[-1])

    @pl.when(step == 0)
    def _():
        pair_sum[...] = jnp.zeros_like(pair_sum)
        conv_sum[...] = jnp.zeros_like(conv_sum)

    for piece, (hidden, pair_grads, row_grads, other_grads) in enumerate(sets):

        @pl.when((step >= piece * each) & (step < piece * each + each))
        def _(hidden=hidden, pair_grads=pair_grads, row_grads=row_grads, other_grads=other_grads):
            pair_sum[...] += dot_rows(flat(rows), flat(pair_grads)) + dot_rows(flat(other), flat(other_grads))
            conv_sum[...] += dot_rows(flat(hidden), flat(row_grads))

    @pl.when(step == steps - 1)
    def _():
        pair_out[...] = pair_sum[...].astype(low_type)
        half = keep_out.shape[1]
        first = facts[1] == 0
        keep_out[...] = jnp.where(first, conv_sum[:, :half], conv_sum[:, half:])
        send_out[...] = jnp.where(first, conv_sum[:, half:], conv_sum[:, :half]).astype(low_type)


def memory_weights(facts, rows, other, sets):
    chips, sub, width = rows.shape
    span = chunk_of(chips, sub)
    both = sets[0][1].shape[2]
    steps = sub // span
    pieces = len(sets)
    each = steps // pieces

    def piece_block(piece, columns):
        return pl.BlockSpec(
            (chips, span, columns), lambda j, facts: (0, jnp.clip(j - piece * each, 0, each - 1), 0)
        )

    in_specs = [slab(rows.shape, span), slab(other.shape, span)]
    for piece, arrays in enumerate(sets):
        in_specs += [piece_block(piece, array.shape[2]) for array in arrays]
    outs = (((width, both), low_type), ((width, width // 2), wide_type), ((width, width // 2), low_type))
    return pl.pallas_call(
        partial(memory_weights_kernel, pieces=pieces, chips=chips, span=span, steps=steps),
        grid_spec=pltpu.PrefetchScalarGridSpec(
            num_scalar_prefetch=1,
            grid=(steps,),
            in_specs=in_specs,
            out_specs=[whole(shape) for shape, _ in outs],
            scratch_shapes=[pltpu.VMEM((width, both), wide_type), pltpu.VMEM((width, width), wide_type)],
        ),
        out_shape=[jax.ShapeDtypeStruct(shape, kind) for shape, kind in outs],
        compiler_params=pltpu.CompilerParams(vmem_limit_bytes=room(chips)),
        cost_estimate=heavy,
        name="memory_weights",
    )(facts, rows, other, *[array for arrays in sets for array in arrays])


def side_weights_kernel(normed_one, grad_qkv, normed_two, grad_cq, grad_self, attended, first, second):
    half = attended.shape[1]
    cut = first.shape[1]
    first[...] = dot_rows(normed_one[...], grad_qkv[:, :cut]).astype(low_type)
    rest = 3 * half - cut
    second[:, :rest] = dot_rows(normed_one[...], grad_qkv[:, cut:]).astype(low_type)
    second[:, rest : rest + half] = dot_rows(normed_two[...], grad_cq[...]).astype(low_type)
    second[:, rest + half :] = dot_rows(grad_self[...], attended[...]).astype(low_type)


def side_weights(*args):
    width = args[0].shape[1]
    half = args[-1].shape[1]
    cut = 3 * half - 128
    return pl.pallas_call(
        side_weights_kernel,
        out_shape=[
            jax.ShapeDtypeStruct((width, cut), low_type),
            jax.ShapeDtypeStruct((width, 5 * half - cut), low_type),
        ],
        compiler_params=pltpu.CompilerParams(vmem_limit_bytes=vmem_budget),
        cost_estimate=heavy,
        name="side_weights",
    )(*args)


def product_kernel(left, right, out):
    @pl.when(pl.program_id(0) == 0)
    def _():
        out[...] = jnp.zeros_like(out)

    out[...] += dot_wide(left[...], right[...])


def product(left, right):
    rows, depth = left.shape
    width = right.shape[1]
    block = 512
    return pl.pallas_call(
        product_kernel,
        grid=(depth // block,),
        in_specs=[
            pl.BlockSpec((rows, block), lambda j: (0, j)),
            pl.BlockSpec((block, width), lambda j: (j, 0)),
        ],
        out_specs=pl.BlockSpec((rows, width), lambda j: (0, 0)),
        out_shape=jax.ShapeDtypeStruct((rows, width), wide_type),
        compiler_params=pltpu.CompilerParams(vmem_limit_bytes=vmem_budget),
        cost_estimate=heavy,
        name="product",
    )(left, right)


def back_through_norm(values, incoming, gain):
    factor = lax.rsqrt(jnp.mean(values * values, axis=-1, keepdims=True) + norm_eps)
    scaled = incoming * gain
    inward = factor * scaled - values * (factor * factor * factor) * jnp.mean(
        scaled * values, axis=-1, keepdims=True
    )
    return inward, jnp.sum(incoming * values * factor, axis=0, keepdims=True)


def self_forward_kernel(
    facts, rows_in, gain, weight, out_weight, normed_out, triple, attended, log_total, part, *, heads
):
    values = rows_in[...].astype(wide_type)
    factor = lax.rsqrt(jnp.mean(values * values, axis=-1, keepdims=True) + norm_eps)
    normed = (values * factor * gain[...]).astype(low_type)
    normed_out[...] = normed
    rows = values.shape[0]
    half = heads * HD
    for side in range(3):
        triple[:, side * half : side * half + half] = dot_wide(normed, weight[side]).astype(low_type)
    key_pos = lax.broadcasted_iota(jnp.int32, (rows, rows), 0)
    query_pos = lax.broadcasted_iota(jnp.int32, (rows, rows), 1)
    allowed = (key_pos <= query_pos) & (key_pos < facts[0])
    left = lax.broadcasted_iota(jnp.int32, (rows, 128), 1) < HD
    log_total[...] = jnp.zeros_like(log_total)
    for pair in range(heads // 2):
        lanes = slice(pair * 128, pair * 128 + 128)
        query_pair = triple[:, lanes]
        key_pair = triple[:, half + pair * 128 : half + pair * 128 + 128]
        value_pair = triple[:, 2 * half + pair * 128 : 2 * half + pair * 128 + 128]
        parts = []
        for side in range(2):
            head = pair * 2 + side
            keep = left if side == 0 else jnp.logical_not(left)
            query = jnp.where(keep, query_pair, jnp.zeros_like(query_pair))
            scores = jnp.where(allowed, dot_columns(key_pair, query) * 0.125, masked_fill)
            top = jnp.max(scores, axis=0, keepdims=True)
            weights = jnp.exp(scores - top)
            total = jnp.sum(weights, axis=0, keepdims=True)
            log_total[head : head + 1, :] = top + jnp.log(total)
            made = dot_rows(value_pair, (weights / total).astype(low_type))
            parts.append(made[side * HD : side * HD + HD, :])
        attended[:, lanes] = jnp.concatenate(parts).T.astype(low_type)
    part[...] = dot_wide(attended[...], out_weight[...])


def self_forward(facts, rows_in, gain, weight, out_weight):
    rows, width = rows_in.shape
    half = out_weight.shape[0]
    args = (rows_in, gain, weight, out_weight)
    outs = (
        ((rows, width), low_type),
        ((rows, 3 * half), low_type),
        ((rows, half), low_type),
        ((8, rows), wide_type),
        ((rows, width), wide_type),
    )
    return pl.pallas_call(
        partial(self_forward_kernel, heads=half // HD),
        grid_spec=pltpu.PrefetchScalarGridSpec(
            num_scalar_prefetch=1,
            grid=(1,),
            in_specs=[whole(arg.shape) for arg in args],
            out_specs=[whole(shape) for shape, _ in outs],
        ),
        out_shape=[jax.ShapeDtypeStruct(shape, kind) for shape, kind in outs],
        compiler_params=pltpu.CompilerParams(vmem_limit_bytes=vmem_budget),
        cost_estimate=heavy,
        name="self_forward",
    )(facts, *args)


def query_forward_kernel(rows_in, own, came, gain, weight, first, normed_out, heads_out, heads_out_t, *, heads):
    total = rows_in[...].astype(wide_type) + (own[...] + came[...])
    first[...] = total
    factor = lax.rsqrt(jnp.mean(total * total, axis=-1, keepdims=True) + norm_eps)
    normed = (total * factor * gain[...]).astype(low_type)
    normed_out[...] = normed
    query = (dot_wide(normed, weight[...]).astype(low_type).astype(wide_type) * 0.125).astype(low_type)
    turned = query.T
    left = lax.broadcasted_iota(jnp.int32, (query.shape[0], 128), 1) < HD
    for head in range(heads):
        pair = query[:, head // 2 * 128 : head // 2 * 128 + 128]
        keep = left if head % 2 == 0 else jnp.logical_not(left)
        heads_out[head] = jnp.where(keep, pair, jnp.zeros_like(pair))
        own_rows = slice(head % 2 * HD, head % 2 * HD + HD)
        other_rows = slice((1 - head % 2) * HD, (1 - head % 2) * HD + HD)
        mine = turned[head * HD : head * HD + HD, :]
        heads_out_t[head, own_rows, :] = mine
        heads_out_t[head, other_rows, :] = jnp.zeros_like(mine)


def query_forward(rows_in, own, came, gain, weight):
    rows, width = rows_in.shape
    heads = weight.shape[1] // HD
    outs = (
        ((rows, width), wide_type),
        ((rows, width), low_type),
        ((heads, rows, 128), low_type),
        ((heads, 128, rows), low_type),
    )
    return pl.pallas_call(
        partial(query_forward_kernel, heads=heads),
        out_shape=[jax.ShapeDtypeStruct(shape, kind) for shape, kind in outs],
        compiler_params=pltpu.CompilerParams(vmem_limit_bytes=vmem_budget),
        cost_estimate=heavy,
        name="query_forward",
    )(rows_in, own, came, gain, weight)


def self_backward_kernel(
    facts, values, own, came, gain, grad_second, out_weight, triple, log_total, weight,
    grad_first, grad_low, gain_grad, triple_grad, part, *, heads,
):
    rows = triple.shape[0]
    half = heads * HD
    incoming = (own[...] + came[...]).astype(low_type).astype(wide_type)
    inward, gain_row = back_through_norm(values[...], incoming, gain[...])
    gain_grad[...] = jnp.broadcast_to(gain_row, gain_grad.shape)
    total = inward + grad_second[...]
    grad_first[...] = total
    grad_low[...] = total.astype(low_type)
    grad = dot_columns(grad_low[...], out_weight[...]).astype(low_type)
    key_pos = lax.broadcasted_iota(jnp.int32, (rows, rows), 0)
    query_pos = lax.broadcasted_iota(jnp.int32, (rows, rows), 1)
    allowed = (key_pos <= query_pos) & (key_pos < facts[0])
    left = lax.broadcasted_iota(jnp.int32, (rows, 128), 1) < HD
    for pair in range(heads // 2):
        lanes = slice(pair * 128, pair * 128 + 128)
        query_pair = triple[:, lanes]
        key_pair = triple[:, half + pair * 128 : half + pair * 128 + 128]
        value_pair = triple[:, 2 * half + pair * 128 : 2 * half + pair * 128 + 128]
        grad_pair = grad[:, lanes]
        key_sum, value_sum, query_parts = 0.0, 0.0, []
        for side in range(2):
            head = pair * 2 + side
            keep = left if side == 0 else jnp.logical_not(left)
            query = jnp.where(keep, query_pair, jnp.zeros_like(query_pair))
            grad_head = jnp.where(keep, grad_pair, jnp.zeros_like(grad_pair))
            scores = dot_columns(key_pair, query) * 0.125
            probs = jnp.exp(jnp.where(allowed, scores, masked_fill) - log_total[head : head + 1, :])
            grad_probs = dot_columns(value_pair, grad_head)
            inner = jnp.sum(probs * grad_probs, axis=0, keepdims=True)
            grad_scores = (probs * (grad_probs - inner)).astype(low_type)
            value_sum = value_sum + dot_wide(probs.astype(low_type), grad_head)
            key_sum = key_sum + dot_wide(grad_scores, query)
            query_parts.append(dot_rows(key_pair, grad_scores)[side * HD : side * HD + HD, :])
        triple_grad[:, lanes] = (jnp.concatenate(query_parts) * 0.125).T.astype(low_type)
        triple_grad[:, half + pair * 128 : half + pair * 128 + 128] = (key_sum * 0.125).astype(low_type)
        triple_grad[:, 2 * half + pair * 128 : 2 * half + pair * 128 + 128] = value_sum.astype(low_type)
    part[...] = (
        dot_columns(triple_grad[:, :half], weight[0])
        + dot_columns(triple_grad[:, half : 2 * half], weight[1])
        + dot_columns(triple_grad[:, 2 * half :], weight[2])
    )


def self_backward(facts, values, own, came, gain, grad_second, out_weight, triple, log_total, weight):
    rows, wide = triple.shape
    width = weight.shape[1]
    args = (values, own, came, gain, grad_second, out_weight, triple, log_total, weight)
    outs = (
        ((rows, width), wide_type),
        ((rows, width), low_type),
        ((8, width), wide_type),
        ((rows, wide), low_type),
        ((rows, width), wide_type),
    )
    return pl.pallas_call(
        partial(self_backward_kernel, heads=wide // (3 * HD)),
        grid_spec=pltpu.PrefetchScalarGridSpec(
            num_scalar_prefetch=1,
            grid=(1,),
            in_specs=[whole(arg.shape) for arg in args],
            out_specs=[whole(shape) for shape, _ in outs],
        ),
        out_shape=[jax.ShapeDtypeStruct(shape, kind) for shape, kind in outs],
        compiler_params=pltpu.CompilerParams(vmem_limit_bytes=vmem_budget),
        cost_estimate=heavy,
        name="self_backward",
    )(facts, *args)


def input_back_kernel(
    values, own, came, gain, grad_first, second, result_own, result_came, act_sums, cross_gain_grad,
    ffn_gain_grad, input_grad, layer_out, gains_out,
):
    incoming = (own[...] + came[...]).astype(low_type).astype(wide_type)
    inward, gain_row = back_through_norm(values[...].astype(wide_type), incoming, gain[...])
    input_grad[...] = inward + grad_first[...]
    layer_out[...] = (second[...] + (result_own[...] + result_came[...])).astype(low_type)
    width = values.shape[1]
    gains = jnp.concatenate(
        (
            act_sums[1:2, :],
            act_sums[0:1, :],
            0.5 * gain_row,
            0.5 * cross_gain_grad[0:1, :],
            0.5 * ffn_gain_grad[0:1, :],
            jnp.zeros((3, width), wide_type),
        )
    )
    for tile in range(width // 128):
        gains_out[tile] = gains[:, tile * 128 : tile * 128 + 128]


def input_back(*args):
    rows, width = args[0].shape
    outs = (((rows, width), wide_type), ((rows, width), low_type), ((width // 128, 8, 128), wide_type))
    return pl.pallas_call(
        input_back_kernel,
        out_shape=[jax.ShapeDtypeStruct(shape, kind) for shape, kind in outs],
        compiler_params=pltpu.CompilerParams(vmem_limit_bytes=vmem_budget),
        cost_estimate=heavy,
        name="input_back",
    )(*args)


def assemble_kernel(
    facts, memory, memory_came, own, other, left, middle, right, gains, conv, cross_kv,
    cross_out, self_qkv, cross_query, self_out, ffn_in, ffn_out, *gain_outs,
):
    width = conv.shape[1]
    half = width // 2
    third = left.shape[1]
    hidden = ffn_in.shape[1]
    first = facts[1] == 0
    conv[:, :half] = jnp.where(first, memory[:, width:], memory_came[:, width:])
    conv[:, half:] = jnp.where(first, memory_came[:, width:], memory[:, width:])
    for side in range(2):
        mine = memory[:, side * half : side * half + half]
        theirs = memory_came[:, side * half : side * half + half]
        cross_kv[:, side, :half] = jnp.where(first, mine, theirs)
        cross_kv[:, side, half:] = jnp.where(first, theirs, mine)
    rest = 3 * half - own.shape[1]
    self_qkv[0] = own[:, :half]
    self_qkv[1] = own[:, half : 2 * half]
    self_qkv[2, :, : half - rest] = own[:, 2 * half :]
    self_qkv[2, :, half - rest :] = other[:, :rest]
    cross_query[...] = other[:, rest : rest + half]
    self_out[...] = other[:, rest + half :]
    ffn_in[:, :third] = left[...]
    ffn_in[:, third:] = middle[:, : hidden - third]
    ffn_out[:, : 2 * third - hidden] = middle[:, hidden - third :]
    ffn_out[:, 2 * third - hidden :] = right[:, : 2 * hidden - 2 * third]
    cross_out[...] = right[:, 2 * hidden - 2 * third :]
    share = conv.shape[0]
    picked = (
        lax.broadcasted_iota(jnp.int32, (width, share), 0)
        == lax.broadcasted_iota(jnp.int32, (width, share), 1) + facts[0] * share
    ).astype(wide_type)
    first_tile = gains.shape[0] - width // 128
    rows_of = jnp.concatenate([gains[first_tile + tile] for tile in range(width // 128)], axis=1)
    mine = jnp.dot(rows_of, picked, precision=lax.Precision.HIGHEST)
    for number, out in enumerate(gain_outs):
        out[...] = mine[number : number + 1, :]


def assemble(facts, *args):
    share = args[0].shape[0]
    width = 2 * args[0].shape[1] // 3
    half = width // 2
    hidden = (3 * args[4].shape[1] - half) // 2
    outs = (
        (share, width),
        (share, 2, width),
        (share, half),
        (3, share, half),
        (share, half),
        (share, half),
        (share, hidden),
        (share, hidden),
    ) + ((1, share),) * 5
    return pl.pallas_call(
        assemble_kernel,
        grid_spec=pltpu.PrefetchScalarGridSpec(
            num_scalar_prefetch=1,
            grid=(1,),
            in_specs=[whole(arg.shape) for arg in args],
            out_specs=[whole(shape) for shape in outs],
        ),
        out_shape=[jax.ShapeDtypeStruct(shape, wide_type) for shape in outs],
        compiler_params=pltpu.CompilerParams(vmem_limit_bytes=vmem_budget),
        cost_estimate=heavy,
        name="assemble",
    )(facts, *args)


def shards(
    dec_input,
    out_grad,
    enc_feats,
    mem_lengths,
    dec_lengths,
    doc_owner,
    group_gain,
    group_bias,
    conv_weight,
    cross_kv,
    self_gain,
    self_qkv,
    self_out,
    cross_gain,
    cross_query,
    cross_out,
    ffn_gain,
    ffn_in,
    ffn_out,
):
    chips = lax.axis_size("dp")
    chip_index = lax.axis_index("dp")
    core_index = lax.axis_index("mp")
    memory_in = enc_feats[0, 0]
    docs, sub, width = memory_in.shape
    per_group = width // GROUPS
    half = width // 2
    heads = half // HD
    rows_here = docs * sub
    share = width // chips
    bits = chips.bit_length() - 1
    rest = tuple(range(4, bits))
    order_sets = {
        "stats": (0, 1, 2, 3),
        "left": (2, 3, 0, 1),
        "middle": (0, 2, 3, 1),
        "right": (1, 0, 2, 3),
        "first": (0, 1, 2, 3),
        "second": (1, 0, 2, 3),
        "memory": (1, 2, 3, 0),
    }
    orders = {
        name: order + rest if bits >= 4 else tuple(range(bits)) for name, order in order_sets.items()
    }

    outgoing = gather_docs(memory_in, doc_owner)
    features = lax.all_to_all(outgoing, "dp", split_axis=0, concat_axis=0, tiled=True)
    outgoing, dec_input = tie((outgoing, dec_input))
    dec_rows = DEC
    dec_rows_in = dec_input.reshape(dec_rows, width)
    self_facts = dec_lengths[chip_index][None]
    self_weight = self_qkv.transpose(1, 0, 2)
    normed_one, qkv_self, attended, self_totals, part = self_forward(
        self_facts, dec_rows_in, self_gain[None], self_weight, self_out
    )
    part_came = other_core(part)
    memory_here, part = tie((memory_in, part))
    wide_in = memory_here.astype(wide_type)
    slot_pos = lax.broadcasted_iota(jnp.int32, (docs, sub), 1)
    live_in = ((slot_pos * 2 + core_index) * chips + chip_index < mem_lengths[:, None])[:, :, None]
    masked_in = jnp.where(live_in, wide_in, 0.0)
    channel_sums = jnp.stack((jnp.sum(masked_in, axis=1), jnp.sum(masked_in * wide_in, axis=1)), axis=1)
    group_of = (
        lax.broadcasted_iota(jnp.int32, (width, GROUPS), 0) // per_group
        == lax.broadcasted_iota(jnp.int32, (width, GROUPS), 1)
    ).astype(wide_type)

    def group_sums(channels):
        return jnp.dot(channels, group_of, precision=lax.Precision.HIGHEST)

    def to_channels(groups):
        return jnp.dot(groups, group_of.T, precision=lax.Precision.HIGHEST)

    sums_here = group_sums(channel_sums.reshape(docs * 2, width)).reshape(docs, 2 * GROUPS)
    sums_here = jnp.take(sums_here, doc_owner, axis=0, mode="clip")
    stat_sums = ScatterSums([core_total(sums_here)], [orders["stats"]], chip_index)
    stat_sums.begin()

    def next_step(sums, value):
        value = sums.behind(value)
        sums.merge()
        if sums.orders[0]:
            sums.begin()
            value = sums.ahead_of(value)
            sums.send()
        return value

    part_came = stat_sums.ahead_of(part_came)
    stat_sums.send()
    first_out, normed_two, query_heads, query_heads_t = query_forward(
        dec_rows_in, part, part_came, cross_gain[None], cross_query
    )
    cross_kv, query_heads = next_step(stat_sums, (cross_kv, query_heads))
    pair_weight = prepare_weights(cross_kv)
    pair_weight, query_heads = next_step(stat_sums, (pair_weight, query_heads))
    grad_low, query_heads, pair_weight = tie((out_grad.reshape(DEC, width), query_heads, pair_weight))
    grad_active = dot_columns(grad_low, ffn_out).astype(low_type)
    grad_active, query_heads = tie((grad_active, query_heads))
    while stat_sums.orders[0]:
        query_heads = next_step(stat_sums, query_heads)
    sums_all = stat_sums.current[0]

    document = doc_owner[chip_index]
    length = mem_lengths[document]
    entries = (length * per_group).astype(wide_type)
    center = sums_all[:GROUPS] / entries
    spread = lax.rsqrt(sums_all[GROUPS:] / entries - center * center + group_eps)
    channel_stats = to_channels(jnp.stack((center, spread)))
    stats = jnp.concatenate(
        (channel_stats, group_gain[None], group_bias[None], jnp.zeros((4, width), wide_type))
    )

    facts_own = jnp.stack((length, core_index, core_index, 1)).astype(jnp.int32)
    facts_other = jnp.stack((length, 1 - core_index, core_index, 0)).astype(jnp.int32)
    features, stats, query_heads, query_heads_t = tie((features, stats, query_heads, query_heads_t))
    memory_own = memory_forward(facts_own, features, stats, conv_weight)
    memory_other = other_core(memory_own)

    carry = (
        jnp.full((8, dec_rows), -1e30, wide_type),
        jnp.zeros((8, dec_rows), wide_type),
        jnp.zeros((half, dec_rows), wide_type),
    )
    pairs_own, *carry = cross_forward(
        facts_own, query_heads_t, memory_own, pair_weight, carry
    )
    pairs_other, top, total, gathered = cross_forward(
        facts_other, query_heads_t, memory_other, pair_weight, carry
    )
    crossed, crossed_t, log_total, part = cross_close(gathered, top, total, cross_out)

    second_out, normed_three, grad_lifted, active, part = feed_forward(
        first_out, part, other_core(part), ffn_gain[None], ffn_in, grad_active
    )
    part_came = other_core(part)
    result_part = product(active, ffn_out)
    part_came, result_part = tie((part_came, result_part))
    result_came = other_core(result_part)
    grad_second, ffn_gain_grad, grad_cross, grad_heads, grad_heads_t, inner = feed_close(
        second_out, part, part_came, ffn_gain[None], grad_low, cross_out, crossed_t
    )
    feed_grads = feed_weights(normed_three, grad_low, grad_cross, grad_lifted, active, crossed)
    feed_sums = Sums.of(
        [grad.reshape(chips, share, grad.shape[1]) for grad in feed_grads],
        [orders["left"], orders["middle"], orders["right"]],
        chip_index,
    )
    inner = feed_sums.start(inner)

    steps = sub // chunk_of(chips, sub)
    place = jnp.concatenate((jnp.stack((chip_index, core_index)).astype(jnp.int32), mem_lengths))
    pair_other, row_other, query_other = cross_backward(
        facts_other, query_heads, query_heads_t, grad_heads, grad_heads_t, log_total, inner, pairs_other, pair_weight,
        low_type, 0, steps,
    )
    facts_two, query_other = feed_sums.round((facts_own, query_other))
    row_came = other_core(row_other)
    pair_own, row_own, query_own = cross_backward(
        facts_two, query_heads, query_heads_t, grad_heads, grad_heads_t, log_total, inner, pairs_own, pair_weight,
        wide_type, 0, steps,
    )

    facts_three, query_own = feed_sums.round((facts_own, query_own))
    grad_memory, hidden, base, act_sums, groups = memory_backward(
        facts_three, features, row_own, row_came, stats, conv_weight, jnp.zeros((8, width), wide_type), 0
    )
    queries, sets = (query_other, query_own), [(hidden, pair_own, grad_memory, pair_other)]

    def dp_hop(value, bit):
        return lax.ppermute(value, "dp", [(chip, chip ^ (1 << bit)) for chip in range(chips)])

    feed_came, base, queries = tie(([part.came for part in feed_sums.parts], base, queries))
    for part, arrived in zip(feed_sums.parts, feed_came):
        part.came = arrived
    returned = [lax.all_to_all(base, "dp", split_axis=0, concat_axis=0, tiled=True)]

    def when_live(work):
        return lax.cond(length > 0, work, nothing_like(work))

    def self_work():
        own_slot = lax.broadcasted_iota(jnp.int32, (chips, 1, 1), 0) == chip_index
        document_groups = jnp.where(own_slot, core_total(groups)[None], 0.0)

        grad_cq, part = query_back(queries, cross_query)
        part_came = other_core(part)
        grad_first, grad_self, cross_gain_grad, grad_qkv, part_one = self_backward(
            self_facts, first_out, part, part_came, cross_gain[None], grad_second, self_out, qkv_self, self_totals,
            self_weight,
        )
        part_one_came = other_core(part_one)
        first_part, second_part = side_weights(normed_one, grad_qkv, normed_two, grad_cq, grad_self, attended)
        part_one_came, first_part = tie((part_one_came, first_part))
        return grad_first, cross_gain_grad, part_one, part_one_came, document_groups, (first_part, second_part)

    queries = feed_sums.round(queries)
    early_feed, late_feed = Sums(feed_sums.parts[:2], chip_index), Sums(feed_sums.parts[2:], chip_index)
    grad_first, cross_gain_grad, part_one, part_one_came, document_groups, late_parts = when_live(self_work)
    while early_feed.going:
        document_groups = early_feed.round(document_groups)
    late_sums = Sums.of(
        [part.reshape(chips, share, -1) for part in late_parts], [orders["first"], orders["second"]], chip_index
    )
    document_groups = late_sums.start(document_groups)

    def memory_work():
        pair_part, conv_keep, conv_send = memory_weights(place, memory_own, memory_other, sets)
        conv_came = other_core(conv_send)
        came, conv_keep = tie((part_one_came, conv_keep))
        input_grad, layer_out, gains = input_back(
            dec_rows_in, part_one, came, self_gain[None], grad_first, second_out, result_part, result_came, act_sums,
            cross_gain_grad, ffn_gain_grad,
        )
        gains, conv_came = tie((gains, conv_came))
        conv_part = (conv_keep + conv_came.astype(wide_type)).astype(low_type)
        return input_grad, layer_out, core_total(gains), jnp.concatenate((pair_part, conv_part), axis=1)

    input_grad, layer_out, small, memory_part = when_live(memory_work)

    memory_sums = Sums.of([memory_part.reshape(chips, share, -1)], [orders["memory"]], chip_index)
    small = memory_sums.start(small)
    late_sums = late_sums.joined(memory_sums)
    all_sums = late_feed.joined(late_sums)
    hop = 0
    moved = memory_grad = None
    while all_sums.going:
        small_came = dp_hop(small, hop) if hop < bits else None
        for bit in ((0,), (1, 2), range(3, bits))[hop] if hop < 3 else ():
            document_groups = document_groups + dp_hop(document_groups, bit)
        value = (small_came, document_groups)
        if hop == 2:
            moved = moved_rows(doc_owner, place, memory_in, document_groups)
            value = (small_came, moved)
        if hop == 3:
            memory_grad = spread_docs(returned, moved, doc_owner)
            value = (small_came, memory_grad)
        if hop == 0:
            returned, small_came = tie((returned, small_came))
            value = (small_came, document_groups)
        small_came, value = all_sums.round(value)
        if hop < bits:
            small = small + small_came
        if hop < 2:
            document_groups = value
        elif hop == 2:
            moved = value
        elif hop == 3:
            memory_grad = value
        hop += 1
    while hop < bits:
        small = small + dp_hop(small, hop)
        hop += 1
    if moved is None:
        moved = moved_rows(doc_owner, place, memory_in, document_groups)
    if memory_grad is None:
        memory_grad = spread_docs(returned, moved, doc_owner)
    first_total, second_total, memory_total = late_sums.totals
    memory_came = other_core(memory_total)
    weight_grads = assemble(
        place, memory_total, memory_came, first_total, second_total, *feed_sums.totals, small
    )
    conv_grad, cross_kv_grad, cross_out_grad, self_qkv_grad, cross_query_grad, self_out_grad = weight_grads[:6]
    ffn_in_grad, ffn_out_grad = weight_grads[6:8]
    gains = [gain.reshape(share) for gain in weight_grads[8:]]
    return (
        layer_out.reshape(1, DEC, width),
        input_grad.reshape(1, DEC, width),
        memory_grad.reshape(1, 1, docs, sub, width),
        gains[0],
        gains[1],
        conv_grad,
        cross_kv_grad,
        gains[2],
        self_qkv_grad.transpose(1, 0, 2),
        self_out_grad.T,
        gains[3],
        cross_query_grad,
        cross_out_grad.T,
        gains[4],
        ffn_in_grad,
        ffn_out_grad.T,
    )


def solution(mesh):
    placed = (
        P("dp", None, None),
        P("dp", None, None),
        P("dp", "mp", None, None, None),
        P(),
        P(),
        P(),
        P(),
        P(),
        P(),
        P(),
        P(),
        P(None, None, "mp"),
        P("mp", None),
        P(),
        P(None, "mp"),
        P("mp", None),
        P(),
        P(None, "mp"),
        P("mp", None),
    )
    return jax.shard_map(
        shards,
        mesh=mesh,
        in_specs=placed,
        out_specs=(
            P("dp", None, None),
            P("dp", None, None),
            P("dp", "mp", None, None, None),
            P("dp"),
            P("dp"),
            P("dp", None),
            P("dp", None, None),
            P("dp"),
            P("dp", None, "mp"),
            P("mp", "dp"),
            P("dp"),
            P("dp", "mp"),
            P("mp", "dp"),
            P("dp"),
            P("dp", "mp"),
            P("mp", "dp"),
        ),
        check_vma=False,
    )
```

profile of v0, /device:TPU:0, one launch (start us, length us, event | category | flops | bytes accessed | tf_op | source)
XLA Modules:
  0.0 372.5 jit_solution(14766970154489142547)
XLA Ops:
  1.3 5.8 %gather_docs.1 = bf16[16,128,768]{2,1,0:T(8,128)(2,1)S(1)} custom-call(s32[16]{0:T(128)S(1)} %copy-done.2, bf16[16,128,768]{2,1,0:T(8,128)(2,1)} %bitcast.60), custom_call_target="tpu_custom_call" | custom-call | flops 10000000000 | bytes 10000000 | tf_op jit(solution)/shard_map/gather_docs/pallas_call | solution.py:299
  7.1 1.7 copy-done
  8.8 8.4 %all-to-all-start = ((bf16[16,128,768]{2,1,0:T(8,128)(2,1)}), bf16[16,128,768]{2,1,0:T(8,128)(2,1)S(1)}, u32[]{:S(2)}, u32[]{:S(2)}) async-start(bf16[16,128,768]{2,1,0:T(8,128)(2,1)} %copy-done), calls=%async_computation | async-start | bytes 6291456 | tf_op jit(solution)/shard_map/all_to_all | solution.py:1476
  17.9 9.0 %self_forward.1 = (bf16[512,768]{1,0:T(8,128)(2,1)}, bf16[512,1152]{1,0:T(8,128)(2,1)}, bf16[512,384]{1,0:T(8,128)(2,1)}, f32[8,512]{1,0:T(8,128)}, f32[512,768]{1,0:T(8,128)}) custom-call(s32[1]{0:T(128)} %dynamic_slice.62.facts, bf16[512,768]{1,0:T(8,128)(2,1)} %bitcast.90, f32[1,768]{1,0:T(1,128)S(1)} %broadcast_in_dim.82.gain, ...), custom_call_target="tpu_custom_call" | custom-call | flops 10000000000 | bytes 10000000 | tf_op jit(solution)/shard_map/self_forward/pallas_call | solution.py:1198
  27.0 3.3 select_reduce_fusion
  36.9 2.0 collective-permute-start.7
  38.9 4.0 %query_forward.1 = (f32[512,768]{1,0:T(8,128)}, bf16[512,768]{1,0:T(8,128)(2,1)}, bf16[6,512,128]{2,1,0:T(8,128)(2,1)S(1)}, bf16[6,128,512]{2,1,0:T(8,128)(2,1)S(1)}) custom-call(bf16[512,768]{1,0:T(8,128)(2,1)} %bitcast.91, f32[512,768]{1,0:T(8,128)} %get-tuple-element.380.own, f32[512,768]{1,0:T(8,128)} %collective-permute-done.6.came, ...), custom_call_target="tpu_custom_call" | custom-call | flops 10000000000 | bytes 10000000 | tf_op jit(solution)/shard_map/query_forward/pallas_call | solution.py:1242
  42.9 1.5 collective-permute-start.8
  44.5 5.3 %prepare_weights.1.key_weight.value_weight = bf16[768,1536]{1,0:T(8,128)(2,1)S(1)} custom-call(bf16[768,2,768]{2,1,0:T(2,128)(2,1)S(1)} %copy-done.5), custom_call_target="tpu_custom_call" | custom-call | flops 10000000000 | bytes 10000000 | tf_op jit(solution)/shard_map/prepare_weights/pallas_call | solution.py:327
  49.8 1.4 copy-done.20
  51.2 1.5 collective-permute-start.9
  52.7 2.6 convolution_convert_fusion.grad_active
  55.3 14.0 %collective-permute-done.9 = f32[2,64]{1,0:T(2,128)S(1)} collective-permute-done((f32[2,64]{1,0:T(2,128)S(1)}, f32[2,64]{1,0:T(2,128)S(1)}, u32[]{:S(2)}, u32[]{:S(2)}) %collective-permute-start.9) | collective-permute-done | bytes 544 | tf_op jit(solution)/shard_map/ppermute | solution.py:103
  69.3 3.3 collective-permute-start.10
  72.7 15.1 %collective-permute-done.10 = f32[64]{0:T(128)S(1)} collective-permute-done((f32[64]{0:T(128)S(1)}, f32[64]{0:T(128)S(1)}, u32[]{:S(2)}, u32[]{:S(2)}) %collective-permute-start.10) | collective-permute-done | bytes 288 | tf_op jit(solution)/shard_map/ppermute | solution.py:103
  89.1 1.3 copy-done.9
  90.3 6.2 %memory_forward.1.rows = bf16[16,128,768]{2,1,0:T(8,128)(2,1)} custom-call(s32[4]{0:T(128)S(1)} %pad_add_fusion.1.facts, bf16[16,128,768]{2,1,0:T(8,128)(2,1)S(1)} %all-to-all-done.rows, f32[8,768]{1,0:T(8,128)S(1)} %maximum_maximum_fusion.stats, bf16[768,768]{1,0:T(8,128)(2,1)S(1)} %copy-done.9), custom_call_target="tpu_custom_call" | custom-call | flops 10000000000 | bytes 10000000 | tf_op jit(solution)/shard_map/memory_forward/pallas_call | solution.py:488
  97.4 1.7 copy-done.21
  100.2 14.1 %cross_forward.2 = (bf16[16,128,768]{2,1,0:T(8,128)(2,1)S(1)}, f32[8,512]{1,0:T(8,128)S(1)}, f32[8,512]{1,0:T(8,128)S(1)}, f32[384,512]{1,0:T(8,128)S(1)}) custom-call(s32[4]{0:T(128)S(1)} %pad_add_fusion.1.facts, bf16[6,128,512]{2,1,0:T(8,128)(2,1)S(1)} %copy-done.26, bf16[16,128,768]{2,1,0:T(8,128)(2,1)} %memory_forward.1.rows, ...), custom_call_target="tpu_custom_call" | custom-call | flops 10000000000 | bytes 10000000 | tf_op jit(solution)/shard_map/cross_forward/pallas_call | solution.py:663
  114.3 13.0 %cross_forward.3 = (bf16[16,128,768]{2,1,0:T(8,128)(2,1)S(1)}, f32[8,512]{1,0:T(8,128)S(1)}, f32[8,512]{1,0:T(8,128)S(1)}, f32[384,512]{1,0:T(8,128)S(1)}) custom-call(s32[4]{0:T(128)S(1)} %pad_add_fusion.2.facts, bf16[6,128,512]{2,1,0:T(8,128)(2,1)S(1)} %copy-done.26, bf16[16,128,768]{2,1,0:T(8,128)(2,1)} %collective-permute-done.11.rows, ...), custom_call_target="tpu_custom_call" | custom-call | flops 10000000000 | bytes 10000000 | tf_op jit(solution)/shard_map/cross_forward/pallas_call | solution.py:663
  128.6 3.0 collective-permute-done.12.came
  131.7 5.9 %feed_forward.1 = (f32[512,768]{1,0:T(8,128)S(1)}, bf16[512,768]{1,0:T(8,128)(2,1)S(1)}, bf16[512,1536]{1,0:T(8,128)(2,1)S(1)}, bf16[512,1536]{1,0:T(8,128)(2,1)S(1)}, f32[512,768]{1,0:T(8,128)S(1)}) custom-call(f32[512,768]{1,0:T(8,128)S(1)} %copy-done.64, f32[512,768]{1,0:T(8,128)S(1)} %get-tuple-element.416.own, ...), custom_call_target="tpu_custom_call" | custom-call | flops 10000000000 | bytes 10000000 | tf_op jit(solution)/shard_map/feed_forward/pallas_call | solution.py:756
  138.0 3.1 product.1
  141.2 2.2 feed_close.1
  143.4 7.8 %feed_weights.1 = (bf16[768,1152]{1,0:T(8,128)(2,1)S(1)}, bf16[768,1152]{1,0:T(8,128)(2,1)S(1)}, bf16[768,1152]{1,0:T(8,128)(2,1)S(1)}) custom-call(bf16[512,768]{1,0:T(8,128)(2,1)S(1)} %get-tuple-element.418.normed, bf16[512,768]{1,0:T(8,128)(2,1)S(1)} %bitcast.71, bf16[512,768]{1,0:T(8,128)(2,1)S(1)} %get-tuple-element.424.grad_cross, ...), custom_call_target="tpu_custom_call" | custom-call | flops 10000000000 | bytes 10000000 | tf_op jit(solution)/shard_map/feed_weights/pallas_call | solution.py:882
  151.7 2.0 collective-permute-start.16
  153.6 23.7 %cross_backward.2 = (bf16[16,128,768]{2,1,0:T(8,128)(2,1)}, bf16[16,128,768]{2,1,0:T(8,128)(2,1)S(1)}, f32[384,512]{1,0:T(8,128)}) custom-call(s32[4]{0:T(128)S(1)} %pad_add_fusion.2.facts, bf16[6,512,128]{2,1,0:T(8,128)(2,1)S(1)} %copy-done.24, bf16[6,128,512]{2,1,0:T(8,128)(2,1)S(1)} %copy-done.27, bf16[6,512,128]{2,1,0:T(8,128)(2,1)S(1)} %get-tuple-element.435.grad, ...), custom_call_target="tpu_custom_call" | custom-call | flops 10000000000 | bytes 10000000 | tf_op jit(solution)/shard_map/cross_backward/pallas_call | solution.py:969
  178.4 1.9 collective-permute-start.18
  180.3 23.9 %cross_backward.3 = (bf16[16,128,768]{2,1,0:T(8,128)(2,1)}, f32[16,128,768]{2,1,0:T(8,128)S(1)}, f32[384,512]{1,0:T(8,128)}) custom-call(s32[4]{0:T(128)S(1)} %pad_add_fusion.1.facts, bf16[6,512,128]{2,1,0:T(8,128)(2,1)S(1)} %copy-done.24, bf16[6,128,512]{2,1,0:T(8,128)(2,1)S(1)} %copy-done.27, bf16[6,512,128]{2,1,0:T(8,128)(2,1)S(1)} %get-tuple-element.435.grad, ...), custom_call_target="tpu_custom_call" | custom-call | flops 10000000000 | bytes 10000000 | tf_op jit(solution)/shard_map/cross_backward/pallas_call | solution.py:969
  204.8 2.9 collective-permute-start.23
  207.7 9.8 %memory_backward.1 = (bf16[16,128,768]{2,1,0:T(8,128)(2,1)}, bf16[16,128,768]{2,1,0:T(8,128)(2,1)}, bf16[16,128,768]{2,1,0:T(8,128)(2,1)}, f32[8,768]{1,0:T(8,128)}, f32[8,128]{1,0:T(8,128)S(1)}) custom-call(s32[4]{0:T(128)S(1)} %pad_add_fusion.1.facts, bf16[16,128,768]{2,1,0:T(8,128)(2,1)S(1)} %all-to-all-done.rows, ...), custom_call_target="tpu_custom_call" | custom-call | flops 10000000000 | bytes 10000000 | tf_op jit(solution)/shard_map/memory_backward/pallas_call | solution.py:549
  219.0 4.4 %all-to-all-start.1 = ((bf16[16,128,768]{2,1,0:T(8,128)(2,1)}), bf16[16,128,768]{2,1,0:T(8,128)(2,1)S(1)}, u32[]{:S(2)}, u32[]{:S(2)}) async-start(bf16[16,128,768]{2,1,0:T(8,128)(2,1)} %get-tuple-element.526), calls=%async_computation.1 | async-start | bytes 6291456 | tf_op jit(solution)/shard_map/all_to_all | solution.py:1604
  229.7 1.9 collective-permute-start.26
  233.1 21.1 %conditional.2 = (f32[512,768]{1,0:T(8,128)}, f32[8,768]{1,0:T(8,128)S(1)}, f32[512,768]{1,0:T(8,128)}, f32[512,768]{1,0:T(8,128)}, f32[16,8,128]{2,1,0:T(8,128)...) conditional(s32[]{:T(128)} %bitcast.6, () %tuple.90, (f32[384,512]{1,0:T(8,128)S(1)}, ...), branch_computations={%region_2.3_spmd, %region_3.4_spmd} | conditional | flops 30000017408 | bytes 42687572 | solution.py:1607
  234.4 3.0 collective-permute-done.came
  237.4 9.7 %self_backward.1 = (f32[512,768]{1,0:T(8,128)}, bf16[512,768]{1,0:T(8,128)(2,1)S(1)}, f32[8,768]{1,0:T(8,128)S(1)}, bf16[512,1152]{1,0:T(8,128)(2,1)S(1)}, f32[512,768]{1,0:T(8,128)}) custom-call(s32[1]{0:T(128)} %get-tuple-element.73.facts, f32[512,768]{1,0:T(8,128)S(1)} %get-tuple-element.74.values, f32[512,768]{1,0:T(8,128)S(1)} %get-tuple-element.78.own, ...), custom_call_target="tpu_custom_call" | custom-call | flops 10000000000 | bytes 10000000 | tf_op jit(solution)/shard_map/cond/branch_1_fun/self_backward/pallas_call | solution.py:1309
  247.7 2.9 collective-permute-done.2
  250.7 3.3 side_weights.1
  254.8 18.8 %conditional.3 = (f32[6,8,128]{2,1,0:T(8,128)S(1)}, f32[1,512,768]{2,1,0:T(8,128)}, bf16[1,512,768]{2,1,0:T(8,128)(2,1)}, bf16[4,2,2,48,1152]{4,3,2,1,0:T(8,128)(2,1)S(1)}) conditional(s32[]{:T(128)} %bitcast.6, () %tuple.70, (s32[18]{0:T(128)S(1)}, bf16[16,128,768]{2,1,0:T(8,128)(2,1)}, bf16[16,128,768]{2,1,0:T(8,128)(2,1)}, ...), branch_computations={%region_4.5_spmd, %region_5.6_spmd} | conditional | flops 20004429824 | bytes 50652696 | solution.py:1607
  254.9 12.5 %memory_weights.1 = (bf16[768,768]{1,0:T(8,128)(2,1)S(1)}, f32[768,384]{1,0:T(8,128)S(1)}, bf16[768,384]{1,0:T(8,128)(2,1)S(1)}) custom-call(s32[18]{0:T(128)S(1)} %get-tuple-element.103.facts, bf16[16,128,768]{2,1,0:T(8,128)(2,1)} %get-tuple-element.104.refs_0_, bf16[16,128,768]{2,1,0:T(8,128)(2,1)} %get-tuple-element.105.refs_1_, ...), custom_call_target="tpu_custom_call" | custom-call | flops 10000000000 | bytes 10000000 | tf_op jit(solution)/shard_map/cond/branch_1_fun/memory_weights/pallas_call | solution.py:1072
  267.6 4.8 %input_back.1 = (f32[512,768]{1,0:T(8,128)}, bf16[512,768]{1,0:T(8,128)(2,1)}, f32[6,8,128]{2,1,0:T(8,128)S(1)}) custom-call(bf16[512,768]{1,0:T(8,128)(2,1)S(1)} %copy-done.58, f32[512,768]{1,0:T(8,128)} %get-tuple-element.101.own, f32[512,768]{1,0:T(8,128)} %get-tuple-element.111.came, f32[1,768]{1,0:T(1,128)S(1)} %broadcast_in_dim.48.gain, ...), custom_call_target="tpu_custom_call" | custom-call | flops 10000000000 | bytes 10000000 | tf_op jit(solution)/shard_map/cond/branch_1_fun/input_back/pallas_call | solution.py:1350
  274.6 1.9 collective-permute-start.30
  278.5 1.5 collective-permute-start.28
  279.9 1.3 collective-permute-start.29
  281.3 2.4 collective-permute-start.25
  284.2 20.3 %collective-permute-done.32 = f32[16,8,128]{2,1,0:T(8,128)S(1)} collective-permute-done((f32[16,8,128]{2,1,0:T(8,128)S(1)}, f32[16,8,128]{2,1,0:T(8,128)S(1)}, u32[]{:S(2)}, u32[]{:S(2)}) %collective-permute-start.32) | collective-permute-done | bytes 65568 | tf_op jit(solution)/shard_map/ppermute | solution.py:1599
  305.7 2.6 collective-permute-done.31
  308.3 8.5 %collective-permute-done.29.refs_6_ = bf16[8,48,896]{2,1,0:T(8,128)(2,1)} collective-permute-done((bf16[8,48,896]{2,1,0:T(8,128)(2,1)}, bf16[8,48,896]{2,1,0:T(8,128)(2,1)}, u32[]{:S(2)}, u32[]{:S(2)}) %collective-permute-start.29) | collective-permute-done | bytes 688160 | tf_op jit(solution)/shard_map/ppermute | solution.py:220
  317.8 3.0 merge_sums.11
  321.6 1.5 collective-permute-start.33
  323.1 1.5 collective-permute-start.34
  325.1 8.2 %collective-permute-done.37 = f32[16,8,128]{2,1,0:T(8,128)S(1)} collective-permute-done((f32[16,8,128]{2,1,0:T(8,128)S(1)}, f32[16,8,128]{2,1,0:T(8,128)S(1)}, u32[]{:S(2)}, u32[]{:S(2)}) %collective-permute-start.37) | collective-permute-done | bytes 65568 | tf_op jit(solution)/shard_map/ppermute | solution.py:1599
  333.4 1.7 collective-permute-start.38
  335.4 2.3 collective-permute-done.38
  337.7 1.2 collective-permute-done.36
  339.3 2.3 collective-permute-start.43
  342.0 1.6 collective-permute-start.40
  345.9 2.9 moved_rows.1.refs_1_
  348.8 6.5 %collective-permute-done.42 = f32[6,8,128]{2,1,0:T(8,128)S(1)} collective-permute-done((f32[6,8,128]{2,1,0:T(8,128)S(1)}, f32[6,8,128]{2,1,0:T(8,128)S(1)}, u32[]{:S(2)}, u32[]{:S(2)}) %collective-permute-start.42) | collective-permute-done | bytes 24608 | tf_op jit(solution)/shard_map/ppermute | solution.py:1599
  355.5 1.2 collective-permute-start.44
  356.8 1.7 collective-permute-start.45
  359.5 1.2 collective-permute-start.47
  360.7 7.7 %spread_docs.1 = f32[16,128,768]{2,1,0:T(8,128)} custom-call(s32[16]{0:T(128)S(1)} %copy-done.4, bf16[16,128,768]{2,1,0:T(8,128)(2,1)S(1)} %all-to-all-done.1.refs_0_, bf16[16,128,768]{2,1,0:T(8,128)(2,1)} %copy-done.19), custom_call_target="tpu_custom_call" | custom-call | flops 10000000000 | bytes 10000000 | tf_op jit(solution)/shard_map/spread_docs/pallas_call | solution.py:417
  370.1 1.9 assemble.1
  (288 shorter events, 37.9 us)
Async XLA Ops:
  8.8 80.3 %all-to-all-start = ((bf16[16,128,768]{2,1,0:T(8,128)(2,1)}), bf16[16,128,768]{2,1,0:T(8,128)(2,1)S(1)}, u32[]{:S(2)}, u32[]{:S(2)}) async-start(bf16[16,128,768]{2,1,0:T(8,128)(2,1)} %copy-done), calls=%async_computation | async-start | bytes 6291456 | tf_op jit(solution)/shard_map/all_to_all | solution.py:1476
  26.8 10.0 %collective-permute-start.6 = (f32[512,768]{1,0:T(8,128)}, f32[512,768]{1,0:T(8,128)}, u32[]{:S(2)}, u32[]{:S(2)}) collective-permute-start(f32[512,768]{1,0:T(8,128)} %get-tuple-element.380.own), channel_id=1, source_target_pairs={{0,1},{1,0},{2,3},{3,2},{4,5},{5,4},{6,7},{7,6},{8,9},{9,8},{10,11... | collective-permute-start | bytes 4718600 | tf_op jit(solution)/shard_map/ppermute | solution.py:59
  31.7 5.1 %collective-permute-start.5 = (f32[16,64]{1,0:T(8,128)S(1)}, f32[16,64]{1,0:T(8,128)S(1)}, u32[]{:S(2)}, u32[]{:S(2)}) collective-permute-start(f32[16,64]{1,0:T(8,128)S(1)} %gather_fusion), channel_id=1, source_target_pairs={{0,1},{1,0},{2,3},{3,2},{4,5},{5,4},{6,7},{7,6},{8,9},{9,8},{10,11... | collective-permute-start | bytes 12296 | tf_op jit(solution)/shard_map/ppermute | solution.py:59
  36.9 6.0 %collective-permute-start.7 = (f32[2,2,2,64]{3,2,1,0:T(2,128)S(1)}, f32[2,2,2,64]{3,2,1,0:T(2,128)S(1)}, u32[]{:S(2)}, u32[]{:S(2)}) collective-permute-start(f32[2,2,2,64]{3,2,1,0:T(2,128)S(1)} %bitcast.83), channel_id=1, source_target_pairs={{0,2},{2,0},{4,6},{6,4},{8,10},{10,8},{12,14},{14,12},{16,18},{18,... | collective-permute-start | bytes 6152 | tf_op jit(solution)/shard_map/ppermute | solution.py:103
  42.9 9.8 %copy-start.7 = (bf16[1536,768]{1,0:T(8,128)(2,1)S(1)}, bf16[1536,768]{1,0:T(8,128)(2,1)}, u32[]{:S(2)}) copy-start(bf16[1536,768]{1,0:T(8,128)(2,1)} %right.1) | copy-start | bytes 7077892
  42.9 8.3 %collective-permute-start.8 = (f32[2,2,64]{2,1,0:T(2,128)S(1)}, f32[2,2,64]{2,1,0:T(2,128)S(1)}, u32[]{:S(2)}, u32[]{:S(2)}) collective-permute-start(f32[2,2,64]{2,1,0:T(2,128)S(1)} %bitcast.85), channel_id=1, source_target_pairs={{0,4},{2,6},{4,0},{6,2},{8,12},{10,14},{12,8},{14,10},{16,20},{18,... | collective-permute-start | bytes 3080 | tf_op jit(solution)/shard_map/ppermute | solution.py:103
  51.2 18.1 %collective-permute-start.9 = (f32[2,64]{1,0:T(2,128)S(1)}, f32[2,64]{1,0:T(2,128)S(1)}, u32[]{:S(2)}, u32[]{:S(2)}) collective-permute-start(f32[2,64]{1,0:T(2,128)S(1)} %bitcast.86), channel_id=1, source_target_pairs={{0,8},{2,10},{4,12},{6,14},{8,0},{10,2},{12,4},{14,6},{16,24},{18,... | collective-permute-start | bytes 1544 | tf_op jit(solution)/shard_map/ppermute | solution.py:103
  69.3 18.6 %collective-permute-start.10 = (f32[64]{0:T(128)S(1)}, f32[64]{0:T(128)S(1)}, u32[]{:S(2)}, u32[]{:S(2)}) collective-permute-start(f32[64]{0:T(128)S(1)} %fusion.17), channel_id=1, source_target_pairs={{0,16},{2,18},{4,20},{6,22},{8,24},{10,26},{12,28},{14,30},{16,0},... | collective-permute-start | bytes 776 | tf_op jit(solution)/shard_map/ppermute | solution.py:103
  96.5 17.7 %collective-permute-start.11 = (bf16[16,128,768]{2,1,0:T(8,128)(2,1)}, bf16[16,128,768]{2,1,0:T(8,128)(2,1)}, u32[]{:S(2)}, u32[]{:S(2)}) collective-permute-start(bf16[16,128,768]{2,1,0:T(8,128)(2,1)} %memory_forward.1.rows), channel_id=1, source_target_pairs={{0,1},{1,0},{2,3},{3,2},{4,5},{5,4},{6,7},{7,6},{8,9},{9,8},{10,11... | collective-permute-start | bytes 9437192 | tf_op jit(solution)/shard_map/ppermute | solution.py:59
  114.3 13.0 %copy-start.13 = (bf16[384,768]{1,0:T(8,128)(2,1)S(1)}, bf16[384,768]{1,0:T(8,128)(2,1)}, u32[]{:S(2)}) copy-start(bf16[384,768]{1,0:T(8,128)(2,1)} %weight.10) | copy-start | bytes 1769476
  128.0 3.6 collective-permute-start.12
  137.6 3.6 collective-permute-start.13
  151.5 25.8 %collective-permute-start.14 = (bf16[8,48,1152]{2,1,0:T(8,128)(2,1)S(1)}, bf16[8,48,1152]{2,1,0:T(8,128)(2,1)S(1)}, u32[]{:S(2)}, u32[]{:S(2)}) collective-permute-start(bf16[8,48,1152]{2,1,0:T(8,128)(2,1)S(1)} %bitcast.78), channel_id=1, source_target_pairs={{0,8},{2,10},{4,12},{6,14},{8,0},{10,2},{12,4},{14,6},{16,24},{18,... | collective-permute-start | bytes 2654216 | tf_op jit(solution)/shard_map/ppermute | solution.py:220
  151.6 25.7 %collective-permute-start.15 = (bf16[8,48,1152]{2,1,0:T(8,128)(2,1)S(1)}, bf16[8,48,1152]{2,1,0:T(8,128)(2,1)S(1)}, u32[]{:S(2)}, u32[]{:S(2)}) collective-permute-start(bf16[8,48,1152]{2,1,0:T(8,128)(2,1)S(1)} %dynamic-slice_bitcast_fusion), channel_id=1, source_target_pairs={{0,2},{2,0},{4,6},{6,4},{8,10},{10,8},{12,14},{14,12},{16,18},{18,... | collective-permute-start | bytes 2654216 | tf_op jit(solution)/shard_map/ppermute | solution.py:220
  151.7 25.7 %collective-permute-start.16 = (bf16[8,48,1152]{2,1,0:T(8,128)(2,1)S(1)}, bf16[8,48,1152]{2,1,0:T(8,128)(2,1)S(1)}, u32[]{:S(2)}, u32[]{:S(2)}) collective-permute-start(bf16[8,48,1152]{2,1,0:T(8,128)(2,1)S(1)} %bitcast.77), channel_id=1, source_target_pairs={{0,4},{2,6},{4,0},{6,2},{8,12},{10,14},{12,8},{14,10},{16,20},{18,... | collective-permute-start | bytes 2654216 | tf_op jit(solution)/shard_map/ppermute | solution.py:220
  177.3 30.4 %collective-permute-start.20 = (bf16[16,128,768]{2,1,0:T(8,128)(2,1)S(1)}, bf16[16,128,768]{2,1,0:T(8,128)(2,1)S(1)}, u32[]{:S(2)}, u32[]{:S(2)}) collective-permute-start(bf16[16,128,768]{2,1,0:T(8,128)(2,1)S(1)} %get-tuple-element.468), channel_id=1, source_target_pairs={{0,1},{1,0},{2,3},{3,2},{4,5},{5,4},{6,7},{7,6},{8,9},{9,8},{10,11... | collective-permute-start | bytes 9437192 | tf_op jit(solution)/shard_map/ppermute | solution.py:59
  178.3 26.0 %collective-permute-start.17 = (bf16[4,48,1152]{2,1,0:T(8,128)(2,1)S(1)}, bf16[4,48,1152]{2,1,0:T(8,128)(2,1)S(1)}, u32[]{:S(2)}, u32[]{:S(2)}) collective-permute-start(bf16[4,48,1152]{2,1,0:T(8,128)(2,1)S(1)} %get-tuple-element.452), channel_id=1, source_target_pairs={{0,16},{2,18},{4,20},{6,22},{8,24},{10,26},{12,28},{14,30},{16,0},... | collective-permute-start | bytes 1327112 | tf_op jit(solution)/shard_map/ppermute | solution.py:220
  178.4 25.9 %collective-permute-start.18 = (bf16[4,48,1152]{2,1,0:T(8,128)(2,1)S(1)}, bf16[4,48,1152]{2,1,0:T(8,128)(2,1)S(1)}, u32[]{:S(2)}, u32[]{:S(2)}) collective-permute-start(bf16[4,48,1152]{2,1,0:T(8,128)(2,1)S(1)} %get-tuple-element.453), channel_id=1, source_target_pairs={{0,8},{2,10},{4,12},{6,14},{8,0},{10,2},{12,4},{14,6},{16,24},{18,... | collective-permute-start | bytes 1327112 | tf_op jit(solution)/shard_map/ppermute | solution.py:220
  180.3 24.0 %collective-permute-start.19 = (bf16[4,48,1152]{2,1,0:T(8,128)(2,1)S(1)}, bf16[4,48,1152]{2,1,0:T(8,128)(2,1)S(1)}, u32[]{:S(2)}, u32[]{:S(2)}) collective-permute-start(bf16[4,48,1152]{2,1,0:T(8,128)(2,1)S(1)} %get-tuple-element.454), channel_id=1, source_target_pairs={{0,2},{2,0},{4,6},{6,4},{8,10},{10,8},{12,14},{14,12},{16,18},{18,... | collective-permute-start | bytes 1327112 | tf_op jit(solution)/shard_map/ppermute | solution.py:220
  204.6 12.9 %copy-start.28 = (bf16[2,48,1152]{2,1,0:T(8,128)(2,1)}, bf16[2,48,1152]{2,1,0:T(8,128)(2,1)S(1)}, u32[]{:S(2)}) copy-start(bf16[2,48,1152]{2,1,0:T(8,128)(2,1)S(1)} %get-tuple-element.473.refs_0_) | copy-start | bytes 663556
  204.7 12.9 %copy-start.30 = (bf16[2,48,1152]{2,1,0:T(8,128)(2,1)}, bf16[2,48,1152]{2,1,0:T(8,128)(2,1)S(1)}, u32[]{:S(2)}) copy-start(bf16[2,48,1152]{2,1,0:T(8,128)(2,1)S(1)} %get-tuple-element.474.refs_1_) | copy-start | bytes 663556
  204.7 12.9 %copy-start.32 = (bf16[2,48,1152]{2,1,0:T(8,128)(2,1)}, bf16[2,48,1152]{2,1,0:T(8,128)(2,1)S(1)}, u32[]{:S(2)}) copy-start(bf16[2,48,1152]{2,1,0:T(8,128)(2,1)S(1)} %get-tuple-element.475.refs_2_) | copy-start | bytes 663556
  204.7 12.9 %collective-permute-start.21 = (bf16[2,48,1152]{2,1,0:T(8,128)(2,1)S(1)}, bf16[2,48,1152]{2,1,0:T(8,128)(2,1)S(1)}, u32[]{:S(2)}, u32[]{:S(2)}) collective-permute-start(bf16[2,48,1152]{2,1,0:T(8,128)(2,1)S(1)} %get-tuple-element.476), channel_id=1, source_target_pairs={{0,2},{2,0},{4,6},{6,4},{8,10},{10,8},{12,14},{14,12},{16,18},{18,... | collective-permute-start | bytes 663560 | tf_op jit(solution)/shard_map/ppermute | solution.py:220
  204.8 12.8 %collective-permute-start.22 = (bf16[2,48,1152]{2,1,0:T(8,128)(2,1)S(1)}, bf16[2,48,1152]{2,1,0:T(8,128)(2,1)S(1)}, u32[]{:S(2)}, u32[]{:S(2)}) collective-permute-start(bf16[2,48,1152]{2,1,0:T(8,128)(2,1)S(1)} %get-tuple-element.477), channel_id=1, source_target_pairs={{0,16},{2,18},{4,20},{6,22},{8,24},{10,26},{12,28},{14,30},{16,0},... | collective-permute-start | bytes 663560 | tf_op jit(solution)/shard_map/ppermute | solution.py:220
  204.8 13.4 %collective-permute-start.23 = (bf16[2,48,1152]{2,1,0:T(8,128)(2,1)S(1)}, bf16[2,48,1152]{2,1,0:T(8,128)(2,1)S(1)}, u32[]{:S(2)}, u32[]{:S(2)}) collective-permute-start(bf16[2,48,1152]{2,1,0:T(8,128)(2,1)S(1)} %get-tuple-element.478), channel_id=1, source_target_pairs={{0,8},{2,10},{4,12},{6,14},{8,0},{10,2},{12,4},{14,6},{16,24},{18,... | collective-permute-start | bytes 663560 | tf_op jit(solution)/shard_map/ppermute | solution.py:220
  219.0 89.3 %all-to-all-start.1 = ((bf16[16,128,768]{2,1,0:T(8,128)(2,1)}), bf16[16,128,768]{2,1,0:T(8,128)(2,1)S(1)}, u32[]{:S(2)}, u32[]{:S(2)}) async-start(bf16[16,128,768]{2,1,0:T(8,128)(2,1)} %get-tuple-element.526), calls=%async_computation.1 | async-start | bytes 6291456 | tf_op jit(solution)/shard_map/all_to_all | solution.py:1604
  223.4 30.9 %collective-permute-start.24 = (f32[512,768]{1,0:T(8,128)}, f32[512,768]{1,0:T(8,128)}, u32[]{:S(2)}, u32[]{:S(2)}) collective-permute-start(f32[512,768]{1,0:T(8,128)} %product.1), channel_id=1, source_target_pairs={{0,1},{1,0},{2,3},{3,2},{4,5},{5,4},{6,7},{7,6},{8,9},{9,8},{10,11... | collective-permute-start | bytes 4718600 | tf_op jit(solution)/shard_map/ppermute | solution.py:59
  229.7 48.8 %collective-permute-start.26 = (bf16[1,48,1152]{2,1,0:T(8,128)(2,1)}, bf16[1,48,1152]{2,1,0:T(8,128)(2,1)S(1)}, u32[]{:S(2)}, u32[]{:S(2)}) collective-permute-start(bf16[1,48,1152]{2,1,0:T(8,128)(2,1)} %get-tuple-element.518), channel_id=1, source_target_pairs={{0,4},{2,6},{4,0},{6,2},{8,12},{10,14},{12,8},{14,10},{16,20},{18,... | collective-permute-start | bytes 331784 | tf_op jit(solution)/shard_map/ppermute | solution.py:220
  231.6 46.9 %collective-permute-start.27 = (bf16[1,48,1152]{2,1,0:T(8,128)(2,1)}, bf16[1,48,1152]{2,1,0:T(8,128)(2,1)S(1)}, u32[]{:S(2)}, u32[]{:S(2)}) collective-permute-start(bf16[1,48,1152]{2,1,0:T(8,128)(2,1)} %get-tuple-element.519), channel_id=1, source_target_pairs={{0,4},{2,6},{4,0},{6,2},{8,12},{10,14},{12,8},{14,10},{16,20},{18,... | collective-permute-start | bytes 331784 | tf_op jit(solution)/shard_map/ppermute | solution.py:220
  233.1 21.1 %copy-start.50 = (f32[768]{0:T(1024)S(1)}, f32[768]{0:T(1024)}, u32[]{:S(2)}) copy-start(f32[768]{0:T(1024)} %param.33) | copy-start | bytes 9220
  233.8 3.6 collective-permute-start
  247.1 6.8 %collective-permute-start.1 = (f32[512,768]{1,0:T(8,128)}, f32[512,768]{1,0:T(8,128)}, u32[]{:S(2)}, u32[]{:S(2)}) collective-permute-start(f32[512,768]{1,0:T(8,128)} %get-tuple-element.629), channel_id=1, source_target_pairs={{0,1},{1,0},{2,3},{3,2},{4,5},{5,4},{6,7},{7,6},{8,9},{9,8},{10,11... | collective-permute-start | bytes 4718600 | tf_op jit(solution)/shard_map/cond/branch_1_fun/ppermute | solution.py:59
  247.5 3.0 collective-permute-start.2
  254.8 12.7 %copy-start.43 = (f32[512,768]{1,0:T(8,128)S(1)}, f32[512,768]{1,0:T(8,128)}, u32[]{:S(2)}) copy-start(f32[512,768]{1,0:T(8,128)} %get-tuple-element.113.grad_first) | copy-start | bytes 4718596 | tf_op jit(solution)/shard_map/cond
  254.8 12.7 %copy-start.57 = (f32[512,768]{1,0:T(8,128)S(1)}, f32[512,768]{1,0:T(8,128)}, u32[]{:S(2)}) copy-start(f32[512,768]{1,0:T(8,128)} %get-tuple-element.115.result_own) | copy-start | bytes 4718596 | tf_op jit(solution)/shard_map/cond
  254.9 12.7 %copy-start.58 = (bf16[512,768]{1,0:T(8,128)(2,1)S(1)}, bf16[512,768]{1,0:T(8,128)(2,1)}, u32[]{:S(2)}) copy-start(bf16[512,768]{1,0:T(8,128)(2,1)} %get-tuple-element.100.values) | copy-start | bytes 2359300 | tf_op jit(solution)/shard_map/cond
  254.9 12.7 %copy-start.63 = (f32[512,768]{1,0:T(8,128)S(1)}, f32[512,768]{1,0:T(8,128)}, u32[]{:S(2)}) copy-start(f32[512,768]{1,0:T(8,128)} %get-tuple-element.114.second) | copy-start | bytes 4718596 | tf_op jit(solution)/shard_map/cond
  254.9 12.7 %copy-start.73 = (f32[8,768]{1,0:T(8,128)S(1)}, f32[8,768]{1,0:T(8,128)}, u32[]{:S(2)}) copy-start(f32[8,768]{1,0:T(8,128)} %get-tuple-element.117.act_sums) | copy-start | bytes 73732 | tf_op jit(solution)/shard_map/cond
  254.9 12.7 %copy-start.74 = (f32[8,768]{1,0:T(8,128)S(1)}, f32[8,768]{1,0:T(8,128)}, u32[]{:S(2)}) copy-start(f32[8,768]{1,0:T(8,128)} %get-tuple-element.119.ffn_gain_grad) | copy-start | bytes 73732 | tf_op jit(solution)/shard_map/cond
  267.4 5.0 %collective-permute-start.3 = (bf16[768,384]{1,0:T(8,128)(2,1)S(1)}, bf16[768,384]{1,0:T(8,128)(2,1)S(1)}, u32[]{:S(2)}, u32[]{:S(2)}) collective-permute-start(bf16[768,384]{1,0:T(8,128)(2,1)S(1)} %get-tuple-element.121), channel_id=1, source_target_pairs={{0,1},{1,0},{2,3},{3,2},{4,5},{5,4},{6,7},{7,6},{8,9},{9,8},{10,11... | collective-permute-start | bytes 1769480 | tf_op jit(solution)/shard_map/cond/branch_1_fun/ppermute | solution.py:59
  272.4 1.2 collective-permute-start.4
  273.6 32.1 %copy-start.40 = (bf16[4,2,2,48,1152]{4,3,2,1,0:T(8,128)(2,1)}, bf16[4,2,2,48,1152]{4,3,2,1,0:T(8,128)(2,1)S(1)}, u32[]{:S(2)}) copy-start(bf16[4,2,2,48,1152]{4,3,2,1,0:T(8,128)(2,1)S(1)} %get-tuple-element.516.refs_3_) | copy-start | bytes 5308420
  274.6 42.2 %collective-permute-start.30 = (bf16[8,48,1152]{2,1,0:T(8,128)(2,1)}, bf16[8,48,1152]{2,1,0:T(8,128)(2,1)}, u32[]{:S(2)}, u32[]{:S(2)}) collective-permute-start(bf16[8,48,1152]{2,1,0:T(8,128)(2,1)} %bitcast.35), channel_id=1, source_target_pairs={{0,4},{2,6},{4,0},{6,2},{8,12},{10,14},{12,8},{14,10},{16,20},{18,... | collective-permute-start | bytes 2654216 | tf_op jit(solution)/shard_map/ppermute | solution.py:220
  278.5 38.4 %collective-permute-start.28 = (bf16[8,48,1024]{2,1,0:T(8,128)(2,1)}, bf16[8,48,1024]{2,1,0:T(8,128)(2,1)}, u32[]{:S(2)}, u32[]{:S(2)}) collective-permute-start(bf16[8,48,1024]{2,1,0:T(8,128)(2,1)} %dynamic-slice_bitcast_fusion.1), channel_id=1, source_target_pairs={{0,2},{2,0},{4,6},{6,4},{8,10},{10,8},{12,14},{14,12},{16,18},{18,... | collective-permute-start | bytes 2359304 | tf_op jit(solution)/shard_map/ppermute | solution.py:220
  279.9 36.9 %collective-permute-start.29 = (bf16[8,48,896]{2,1,0:T(8,128)(2,1)}, bf16[8,48,896]{2,1,0:T(8,128)(2,1)}, u32[]{:S(2)}, u32[]{:S(2)}) collective-permute-start(bf16[8,48,896]{2,1,0:T(8,128)(2,1)} %bitcast.34), channel_id=1, source_target_pairs={{0,4},{2,6},{4,0},{6,2},{8,12},{10,14},{12,8},{14,10},{16,20},{18,... | collective-permute-start | bytes 2064392 | tf_op jit(solution)/shard_map/ppermute | solution.py:220
  281.3 27.0 %collective-permute-start.25 = (bf16[1,48,1152]{2,1,0:T(8,128)(2,1)S(1)}, bf16[1,48,1152]{2,1,0:T(8,128)(2,1)}, u32[]{:S(2)}, u32[]{:S(2)}) collective-permute-start(bf16[1,48,1152]{2,1,0:T(8,128)(2,1)S(1)} %get-tuple-element.517), channel_id=1, source_target_pairs={{0,16},{2,18},{4,20},{6,22},{8,24},{10,26},{12,28},{14,30},{16,0},... | collective-permute-start | bytes 331784 | tf_op jit(solution)/shard_map/ppermute | solution.py:220
  283.6 20.8 %collective-permute-start.32 = (f32[16,8,128]{2,1,0:T(8,128)S(1)}, f32[16,8,128]{2,1,0:T(8,128)S(1)}, u32[]{:S(2)}, u32[]{:S(2)}) collective-permute-start(f32[16,8,128]{2,1,0:T(8,128)S(1)} %copy-done.46), channel_id=1, source_target_pairs={{0,2},{2,0},{4,6},{6,4},{8,10},{10,8},{12,14},{14,12},{16,18},{18,... | collective-permute-start | bytes 196616 | tf_op jit(solution)/shard_map/ppermute | solution.py:1599
  304.5 3.8 %collective-permute-start.31 = (f32[6,8,128]{2,1,0:T(8,128)S(1)}, f32[6,8,128]{2,1,0:T(8,128)S(1)}, u32[]{:S(2)}, u32[]{:S(2)}) collective-permute-start(f32[6,8,128]{2,1,0:T(8,128)S(1)} %get-tuple-element.527), channel_id=1, source_target_pairs={{0,2},{2,0},{4,6},{6,4},{8,10},{10,8},{12,14},{14,12},{16,18},{18,... | collective-permute-start | bytes 73736 | tf_op jit(solution)/shard_map/ppermute | solution.py:1599
  320.7 18.2 %collective-permute-start.35 = (bf16[4,48,1152]{2,1,0:T(8,128)(2,1)S(1)}, bf16[4,48,1152]{2,1,0:T(8,128)(2,1)S(1)}, u32[]{:S(2)}, u32[]{:S(2)}) collective-permute-start(bf16[4,48,1152]{2,1,0:T(8,128)(2,1)S(1)} %get-tuple-element.544), channel_id=1, source_target_pairs={{0,8},{2,10},{4,12},{6,14},{8,0},{10,2},{12,4},{14,6},{16,24},{18,... | collective-permute-start | bytes 1327112 | tf_op jit(solution)/shard_map/ppermute | solution.py:220
  321.6 17.3 %collective-permute-start.33 = (bf16[4,48,1024]{2,1,0:T(8,128)(2,1)S(1)}, bf16[4,48,1024]{2,1,0:T(8,128)(2,1)S(1)}, u32[]{:S(2)}, u32[]{:S(2)}) collective-permute-start(bf16[4,48,1024]{2,1,0:T(8,128)(2,1)S(1)} %get-tuple-element.542), channel_id=1, source_target_pairs={{0,4},{2,6},{4,0},{6,2},{8,12},{10,14},{12,8},{14,10},{16,20},{18,... | collective-permute-start | bytes 1179656 | tf_op jit(solution)/shard_map/ppermute | solution.py:220
  323.1 15.8 %collective-permute-start.34 = (bf16[4,48,896]{2,1,0:T(8,128)(2,1)S(1)}, bf16[4,48,896]{2,1,0:T(8,128)(2,1)S(1)}, u32[]{:S(2)}, u32[]{:S(2)}) collective-permute-start(bf16[4,48,896]{2,1,0:T(8,128)(2,1)S(1)} %get-tuple-element.543), channel_id=1, source_target_pairs={{0,2},{2,0},{4,6},{6,4},{8,10},{10,8},{12,14},{14,12},{16,18},{18,... | collective-permute-start | bytes 1032200 | tf_op jit(solution)/shard_map/ppermute | solution.py:220
  324.6 8.8 %collective-permute-start.37 = (f32[16,8,128]{2,1,0:T(8,128)S(1)}, f32[16,8,128]{2,1,0:T(8,128)S(1)}, u32[]{:S(2)}, u32[]{:S(2)}) collective-permute-start(f32[16,8,128]{2,1,0:T(8,128)S(1)} %copy-done.44), channel_id=1, source_target_pairs={{0,4},{2,6},{4,0},{6,2},{8,12},{10,14},{12,8},{14,10},{16,20},{18,... | collective-permute-start | bytes 196616 | tf_op jit(solution)/shard_map/ppermute | solution.py:1599
  333.4 4.3 %collective-permute-start.38 = (f32[16,8,128]{2,1,0:T(8,128)S(1)}, f32[16,8,128]{2,1,0:T(8,128)S(1)}, u32[]{:S(2)}, u32[]{:S(2)}) collective-permute-start(f32[16,8,128]{2,1,0:T(8,128)S(1)} %add.145), channel_id=1, source_target_pairs={{0,8},{2,10},{4,12},{6,14},{8,0},{10,2},{12,4},{14,6},{16,24},{18,... | collective-permute-start | bytes 196616 | tf_op jit(solution)/shard_map/ppermute | solution.py:1599
  335.1 3.8 %collective-permute-start.36 = (f32[6,8,128]{2,1,0:T(8,128)S(1)}, f32[6,8,128]{2,1,0:T(8,128)S(1)}, u32[]{:S(2)}, u32[]{:S(2)}) collective-permute-start(f32[6,8,128]{2,1,0:T(8,128)S(1)} %add.144), channel_id=1, source_target_pairs={{0,4},{2,6},{4,0},{6,2},{8,12},{10,14},{12,8},{14,10},{16,20},{18,... | collective-permute-start | bytes 73736 | tf_op jit(solution)/shard_map/ppermute | solution.py:1599
  339.3 6.6 %collective-permute-start.43 = (f32[16,8,128]{2,1,0:T(8,128)S(1)}, f32[16,8,128]{2,1,0:T(8,128)S(1)}, u32[]{:S(2)}, u32[]{:S(2)}) collective-permute-start(f32[16,8,128]{2,1,0:T(8,128)S(1)} %add.146), channel_id=1, source_target_pairs={{0,16},{2,18},{4,20},{6,22},{8,24},{10,26},{12,28},{14,30},{16,0},... | collective-permute-start | bytes 196616 | tf_op jit(solution)/shard_map/ppermute | solution.py:1599
  341.6 13.8 %collective-permute-start.39 = (bf16[2,48,1024]{2,1,0:T(8,128)(2,1)S(1)}, bf16[2,48,1024]{2,1,0:T(8,128)(2,1)S(1)}, u32[]{:S(2)}, u32[]{:S(2)}) collective-permute-start(bf16[2,48,1024]{2,1,0:T(8,128)(2,1)S(1)} %get-tuple-element.558), channel_id=1, source_target_pairs={{0,8},{2,10},{4,12},{6,14},{8,0},{10,2},{12,4},{14,6},{16,24},{18,... | collective-permute-start | bytes 589832 | tf_op jit(solution)/shard_map/ppermute | solution.py:220
  342.0 13.3 %collective-permute-start.40 = (bf16[2,48,896]{2,1,0:T(8,128)(2,1)S(1)}, bf16[2,48,896]{2,1,0:T(8,128)(2,1)S(1)}, u32[]{:S(2)}, u32[]{:S(2)}) collective-permute-start(bf16[2,48,896]{2,1,0:T(8,128)(2,1)S(1)} %get-tuple-element.559), channel_id=1, source_target_pairs={{0,8},{2,10},{4,12},{6,14},{8,0},{10,2},{12,4},{14,6},{16,24},{18,... | collective-permute-start | bytes 516104 | tf_op jit(solution)/shard_map/ppermute | solution.py:220
  343.6 11.8 %collective-permute-start.41 = (bf16[2,48,1152]{2,1,0:T(8,128)(2,1)S(1)}, bf16[2,48,1152]{2,1,0:T(8,128)(2,1)S(1)}, u32[]{:S(2)}, u32[]{:S(2)}) collective-permute-start(bf16[2,48,1152]{2,1,0:T(8,128)(2,1)S(1)} %get-tuple-element.560), channel_id=1, source_target_pairs={{0,16},{2,18},{4,20},{6,22},{8,24},{10,26},{12,28},{14,30},{16,0},... | collective-permute-start | bytes 663560 | tf_op jit(solution)/shard_map/ppermute | solution.py:220
  344.3 11.0 %collective-permute-start.42 = (f32[6,8,128]{2,1,0:T(8,128)S(1)}, f32[6,8,128]{2,1,0:T(8,128)S(1)}, u32[]{:S(2)}, u32[]{:S(2)}) collective-permute-start(f32[6,8,128]{2,1,0:T(8,128)S(1)} %add.147), channel_id=1, source_target_pairs={{0,8},{2,10},{4,12},{6,14},{8,0},{10,2},{12,4},{14,6},{16,24},{18,... | collective-permute-start | bytes 73736 | tf_op jit(solution)/shard_map/ppermute | solution.py:1599
  355.5 12.9 %collective-permute-start.44 = (bf16[1,48,1024]{2,1,0:T(8,128)(2,1)S(1)}, bf16[1,48,1024]{2,1,0:T(8,128)(2,1)S(1)}, u32[]{:S(2)}, u32[]{:S(2)}) collective-permute-start(bf16[1,48,1024]{2,1,0:T(8,128)(2,1)S(1)} %get-tuple-element.571), channel_id=1, source_target_pairs={{0,16},{2,18},{4,20},{6,22},{8,24},{10,26},{12,28},{14,30},{16,0},... | collective-permute-start | bytes 294920 | tf_op jit(solution)/shard_map/ppermute | solution.py:220
  356.8 11.7 %collective-permute-start.45 = (bf16[1,48,896]{2,1,0:T(8,128)(2,1)S(1)}, bf16[1,48,896]{2,1,0:T(8,128)(2,1)S(1)}, u32[]{:S(2)}, u32[]{:S(2)}) collective-permute-start(bf16[1,48,896]{2,1,0:T(8,128)(2,1)S(1)} %get-tuple-element.572), channel_id=1, source_target_pairs={{0,16},{2,18},{4,20},{6,22},{8,24},{10,26},{12,28},{14,30},{16,0},... | collective-permute-start | bytes 258056 | tf_op jit(solution)/shard_map/ppermute | solution.py:220
  358.5 10.0 %collective-permute-start.46 = (bf16[1,48,1152]{2,1,0:T(8,128)(2,1)S(1)}, bf16[1,48,1152]{2,1,0:T(8,128)(2,1)S(1)}, u32[]{:S(2)}, u32[]{:S(2)}) collective-permute-start(bf16[1,48,1152]{2,1,0:T(8,128)(2,1)S(1)} %get-tuple-element.573), channel_id=1, source_target_pairs={{0,2},{2,0},{4,6},{6,4},{8,10},{10,8},{12,14},{14,12},{16,18},{18,... | collective-permute-start | bytes 331784 | tf_op jit(solution)/shard_map/ppermute | solution.py:220
  359.5 8.9 %collective-permute-start.47 = (f32[6,8,128]{2,1,0:T(8,128)S(1)}, f32[6,8,128]{2,1,0:T(8,128)S(1)}, u32[]{:S(2)}, u32[]{:S(2)}) collective-permute-start(f32[6,8,128]{2,1,0:T(8,128)S(1)} %add.149), channel_id=1, source_target_pairs={{0,16},{2,18},{4,20},{6,22},{8,24},{10,26},{12,28},{14,30},{16,0},... | collective-permute-start | bytes 73736 | tf_op jit(solution)/shard_map/ppermute | solution.py:1599
  368.6 1.5 collective-permute-start.48
  (63 other events, 246.9 us)
where the time goes:
time: 378 us; the launch traced here: 372 us
  Pallas kernels  184 us (49%)
  waiting for transfers between devices  90.2 us (24%)
  starting transfers between devices  59 us (16%)
  local copies, waits for them, and re-layouts  23.7 us (6%)
  other arithmetic  6.21 us (2%)
  between operations  5.39 us (1%)
  matrix products  4.08 us (1%)
    pallas_call x2, Pallas kernels, cross_backward(): pl.pallas_call(partial(cross_backward_kernel, chips=chips, span=span, fir...  47.6 us
    ppermute x8, waiting for transfers between devices, dp_hop(): lax.ppermute(value, 'dp', [(chip, chip ^ 1 << bit) for chip in range(chip...  42.3 us
    ppermute x4, waiting for transfers between devices, send(): lax.ppermute(sent, 'dp', [(chip, chip ^ 1 << order[0]) for chip in range(...  29.2 us
    pallas_call x2, Pallas kernels, cross_forward(): pl.pallas_call(partial(cross_forward_kernel, chips=chips, span=span), gri...  27.1 us
    ppermute x24, starting transfers between devices, leave(): lax.ppermute(leaving, 'dp', [(chip, chip ^ 1 << bit) for chip in range(ch...  26.8 us
    unnamed x140, local copies, waits for them, and re-layouts  17.7 us
    pallas_call x1, Pallas kernels, memory_weights(): pl.pallas_call(partial(memory_weights_kernel, pieces=pieces, chips=chips,...  12.5 us
    ppermute x13, waiting for transfers between devices, other_core(): return lax.ppermute(values, 'mp', [(0, 1), (1, 0)])  10.2 us
  transfers between devices with their start and end apart: 51, of which 15 were waited for; matrix products, arithmetic and copies ran while one was open for 4% of the time, Pallas kernels for 37%

commit v1 on v0

--- a/solution.py
+++ b/solution.py
@@ -302,14 +302,14 @@
             num_scalar_prefetch=1,
             grid=(),
             in_specs=[pl.BlockSpec(memory_space=pl.ANY)],
-            out_specs=pl.BlockSpec(memory_space=pltpu.HBM),
+            out_specs=pl.BlockSpec(memory_space=pl.ANY),
             scratch_shapes=[
                 pltpu.VMEM(memory_in.shape, low_type),
                 pltpu.SemaphoreType.DMA((docs,)),
                 pltpu.SemaphoreType.DMA((docs,)),
             ],
         ),
-        out_shape=jax.ShapeDtypeStruct(memory_in.shape, low_type),
+        out_shape=pltpu.HBM(memory_in.shape, low_type),
         compiler_params=pltpu.CompilerParams(vmem_limit_bytes=vmem_large),
         cost_estimate=heavy,
         name="gather_docs",
@@ -493,7 +493,7 @@
             in_specs=[slab(rows.shape, span), whole(stats.shape), whole(weight.shape)],
             out_specs=slab(rows.shape, span),
         ),
-        out_shape=jax.ShapeDtypeStruct(rows.shape, low_type),
+        out_shape=pltpu.HBM(rows.shape, low_type),
         compiler_params=pltpu.CompilerParams(vmem_limit_bytes=room(chips)),
         cost_estimate=heavy,
         name="memory_forward",
@@ -834,69 +834,26 @@
     )(second, own, came, gain, grad_out, weight, crossed_t)
 
 
-def feed_weights_kernel(
-    normed, grad_out, grad_cross, both_grad, both_active, crossed, left, middle, right, turned, *, steps
-):
-    step = pl.program_id(0)
-    third = (2 * steps + 1) // 3
-
-    @pl.when(step == 0)
-    def _():
-        turned[...] = normed[...].T
-
-    @pl.when(step == steps)
-    def _():
-        turned[...] = grad_out[...].T
-
-    @pl.when(step == 2 * steps)
-    def _():
-        turned[...] = grad_cross[...].T
-
-    for number, out in enumerate((left, middle, right)):
-        inside = (step >= number * third) & (step < number * third + third)
-
-        @pl.when(inside & (step < steps))
-        def _(out=out):
-            out[...] = dot_wide(turned[...], both_grad[...]).astype(low_type)
-
-        @pl.when(inside & (step >= steps) & (step < 2 * steps))
-        def _(out=out):
-            out[...] = dot_wide(turned[...], both_active[...]).astype(low_type)
-
-        @pl.when(inside & (step == 2 * steps))
-        def _(out=out):
-            out[...] = dot_wide(turned[...], crossed[...]).astype(low_type)
-
-
-def feed_weights(normed, grad_out, grad_cross, grad_lifted, active, crossed):
-    rows, width = normed.shape
-    hidden = active.shape[1]
-    block = crossed.shape[1]
-    steps = hidden // block
-    third = (2 * steps + 1) // 3
-
-    def piece(number):
-        return pl.BlockSpec((width, block), lambda j: (0, jnp.clip(j - number * third, 0, third - 1)))
-
-    still = pl.BlockSpec((rows, width), lambda j: (0, 0))
-    return pl.pallas_call(
-        partial(feed_weights_kernel, steps=steps),
-        grid=(2 * steps + 1,),
-        in_specs=[
-            still,
-            still,
-            still,
-            pl.BlockSpec((rows, block), lambda j: (0, jnp.minimum(j, steps - 1))),
-            pl.BlockSpec((rows, block), lambda j: (0, jnp.clip(j - steps, 0, steps - 1))),
-            pl.BlockSpec((rows, block), lambda j: (0, 0)),
-        ],
-        out_specs=[piece(number) for number in range(3)],
-        out_shape=[jax.ShapeDtypeStruct((width, third * block), low_type)] * 3,
-        scratch_shapes=[pltpu.VMEM((width, rows), low_type)],
+def feed_weights_kernel(normed, grad_out, grad_cross, grad_lifted, active, crossed, left, middle, right):
+    third = left.shape[1]
+    rest = grad_lifted.shape[1] - third
+    left[...] = dot_rows(normed[...], grad_lifted[:, :third]).astype(low_type)
+    middle[:, :rest] = dot_rows(normed[...], grad_lifted[:, third:]).astype(low_type)
+    middle[:, rest:] = dot_rows(grad_out[...], active[:, : third - rest]).astype(low_type)
+    right[:, : 2 * rest] = dot_rows(grad_out[...], active[:, third - rest :]).astype(low_type)
+    right[:, 2 * rest :] = dot_rows(grad_cross[...], crossed[...]).astype(low_type)
+
+
+def feed_weights(*args):
+    width = args[0].shape[1]
+    third = (2 * args[3].shape[1] + args[5].shape[1]) // 3
+    return pl.pallas_call(
+        feed_weights_kernel,
+        out_shape=[jax.ShapeDtypeStruct((width, third), low_type)] * 3,
         compiler_params=pltpu.CompilerParams(vmem_limit_bytes=vmem_budget),
         cost_estimate=heavy,
         name="feed_weights",
-    )(normed, grad_out, grad_cross, grad_lifted, active, crossed)
+    )(*args)
 
 
 def cross_backward_kernel(
@@ -1465,8 +1422,8 @@
         "middle": (0, 2, 3, 1),
         "right": (1, 0, 2, 3),
         "first": (0, 1, 2, 3),
-        "second": (1, 0, 2, 3),
-        "memory": (1, 2, 3, 0),
+        "second": (2, 0, 1, 3),
+        "memory": (1, 2, 0, 3),
     }
     orders = {
         name: order + rest if bits >= 4 else tuple(range(bits)) for name, order in order_sets.items()
@@ -1524,13 +1481,15 @@
     pair_weight, query_heads = next_step(stat_sums, (pair_weight, query_heads))
     grad_low, query_heads, pair_weight = tie((out_grad.reshape(DEC, width), query_heads, pair_weight))
     grad_active = dot_columns(grad_low, ffn_out).astype(low_type)
-    grad_active, query_heads = tie((grad_active, query_heads))
+    document = doc_owner[chip_index]
+    length = mem_lengths[document]
+    facts_own = jnp.stack((length, core_index, core_index, 1)).astype(jnp.int32)
+    facts_other = jnp.stack((length, 1 - core_index, core_index, 0)).astype(jnp.int32)
+    grad_active, query_heads, facts_own, facts_other = tie((grad_active, query_heads, facts_own, facts_other))
     while stat_sums.orders[0]:
         query_heads = next_step(stat_sums, query_heads)
     sums_all = stat_sums.current[0]
 
-    document = doc_owner[chip_index]
-    length = mem_lengths[document]
     entries = (length * per_group).astype(wide_type)
     center = sums_all[:GROUPS] / entries
     spread = lax.rsqrt(sums_all[GROUPS:] / entries - center * center + group_eps)
@@ -1539,8 +1498,6 @@
         (channel_stats, group_gain[None], group_bias[None], jnp.zeros((4, width), wide_type))
     )
 
-    facts_own = jnp.stack((length, core_index, core_index, 1)).astype(jnp.int32)
-    facts_other = jnp.stack((length, 1 - core_index, core_index, 0)).astype(jnp.int32)
     features, stats, query_heads, query_heads_t = tie((features, stats, query_heads, query_heads_t))
     memory_own = memory_forward(facts_own, features, stats, conv_weight)
     memory_other = other_core(memory_own)

time: 378 us -> 361 us (0.955)
  waiting for transfers between devices: 90.2 us -> 72.4 us
  starting transfers between devices: 59 us -> 66.1 us
  Pallas kernels: 184 us -> 179 us
    ppermute x8, waiting for transfers between devices: 42.3 us -> 31.9 us  [dp_hop(): lax.ppermute(value, 'dp', [(chip, chip ^ 1 << bit) for chip in range(chip...]
    ppermute x24, waiting for transfers between devices: 8.59 us -> 1.09 us  [leave(): lax.ppermute(leaving, 'dp', [(chip, chip ^ 1 << bit) for chip in range(ch...]
    ppermute x24, starting transfers between devices: 26.8 us -> 33.2 us  [leave(): lax.ppermute(leaving, 'dp', [(chip, chip ^ 1 << bit) for chip in range(ch...]
    pallas_call x1, Pallas kernels: 7.81 us -> 3.27 us  [feed_weights(): pl.pallas_call(feed_weights_kernel, out_shape=[jax.ShapeDtypeStruct((widt...]
    unnamed x140 -> x138, local copies, waits for them, and re-layouts: 17.7 us -> 16.8 us
  transfers between devices with their start and end apart: 51 -> 51, of which waited for: 15 -> 12; matrix products, arithmetic and copies ran while one was open for 4% -> 4% of each run, Pallas kernels for 37% -> 38%
where the time goes in v1:
time: 361 us; the launch traced here: 355 us
  Pallas kernels  179 us (50%)
  waiting for transfers between devices  72.4 us (20%)
  starting transfers between devices  66.1 us (18%)
  local copies, waits for them, and re-layouts  22.8 us (6%)
  other arithmetic  5.49 us (2%)
  between operations  5.43 us (2%)
  matrix products  4.08 us (1%)
    pallas_call x2, Pallas kernels, cross_backward(): pl.pallas_call(partial(cross_backward_kernel, chips=chips, span=span, fir...  47.9 us
    ppermute x24, starting transfers between devices, leave(): lax.ppermute(leaving, 'dp', [(chip, chip ^ 1 << bit) for chip in range(ch...  33.2 us
    ppermute x8, waiting for transfers between devices, dp_hop(): lax.ppermute(value, 'dp', [(chip, chip ^ 1 << bit) for chip in range(chip...  31.9 us
    ppermute x4, waiting for transfers between devices, send(): lax.ppermute(sent, 'dp', [(chip, chip ^ 1 << order[0]) for chip in range(...  29.2 us
    pallas_call x2, Pallas kernels, cross_forward(): pl.pallas_call(partial(cross_forward_kernel, chips=chips, span=span), gri...  25.9 us
    unnamed x138, local copies, waits for them, and re-layouts  16.8 us
    pallas_call x1, Pallas kernels, memory_weights(): pl.pallas_call(partial(memory_weights_kernel, pieces=pieces, chips=chips,...  12.5 us
    ppermute x13, waiting for transfers between devices, other_core(): return lax.ppermute(values, 'mp', [(0, 1), (1, 0)])  10.2 us
  transfers between devices with their start and end apart: 51, of which 12 were waited for; matrix products, arithmetic and copies ran while one was open for 4% of the time, Pallas kernels for 38%

profile of v1, /device:TPU:0, one launch (start us, length us, event | category | flops | bytes accessed | tf_op | source)
XLA Modules:
  0.0 355.4 jit_solution(14979627075696497543)
XLA Ops:
  0.7 1.9 copy-done
  3.2 6.5 %gather_docs.1 = bf16[16,128,768]{2,1,0:T(8,128)(2,1)} custom-call(s32[16]{0:T(128)S(1)} %copy-done.2, bf16[16,128,768]{2,1,0:T(8,128)(2,1)S(1)} %bitcast.61), custom_call_target="tpu_custom_call" | custom-call | flops 10000000000 | bytes 10000000 | tf_op jit(solution)/shard_map/gather_docs/pallas_call | solution.py:299
  9.8 8.3 %all-to-all-start = ((bf16[16,128,768]{2,1,0:T(8,128)(2,1)}), bf16[16,128,768]{2,1,0:T(8,128)(2,1)S(1)}, u32[]{:S(2)}, u32[]{:S(2)}) async-start(bf16[16,128,768]{2,1,0:T(8,128)(2,1)} %gather_docs.1), calls=%async_computation | async-start | bytes 6291456 | tf_op jit(solution)/shard_map/all_to_all | solution.py:1433
  18.7 9.0 %self_forward.1 = (bf16[512,768]{1,0:T(8,128)(2,1)}, bf16[512,1152]{1,0:T(8,128)(2,1)}, bf16[512,384]{1,0:T(8,128)(2,1)}, f32[8,512]{1,0:T(8,128)}, f32[512,768]{1,0:T(8,128)}) custom-call(s32[1]{0:T(128)} %dynamic_slice.62.facts, bf16[512,768]{1,0:T(8,128)(2,1)} %bitcast.90, f32[1,768]{1,0:T(1,128)S(1)} %broadcast_in_dim.82.gain, ...), custom_call_target="tpu_custom_call" | custom-call | flops 10000000000 | bytes 10000000 | tf_op jit(solution)/shard_map/self_forward/pallas_call | solution.py:1155
  27.8 3.3 select_reduce_fusion
  37.7 2.0 collective-permute-start.7
  39.7 4.0 %query_forward.1 = (f32[512,768]{1,0:T(8,128)}, bf16[512,768]{1,0:T(8,128)(2,1)}, bf16[6,512,128]{2,1,0:T(8,128)(2,1)S(1)}, bf16[6,128,512]{2,1,0:T(8,128)(2,1)S(1)}) custom-call(bf16[512,768]{1,0:T(8,128)(2,1)} %bitcast.91, f32[512,768]{1,0:T(8,128)} %get-tuple-element.382.own, f32[512,768]{1,0:T(8,128)} %collective-permute-done.6.came, ...), custom_call_target="tpu_custom_call" | custom-call | flops 10000000000 | bytes 10000000 | tf_op jit(solution)/shard_map/query_forward/pallas_call | solution.py:1199
  43.8 1.5 collective-permute-start.8
  45.3 5.3 %prepare_weights.1.key_weight.value_weight = bf16[768,1536]{1,0:T(8,128)(2,1)S(1)} custom-call(bf16[768,2,768]{2,1,0:T(2,128)(2,1)S(1)} %copy-done.5), custom_call_target="tpu_custom_call" | custom-call | flops 10000000000 | bytes 10000000 | tf_op jit(solution)/shard_map/prepare_weights/pallas_call | solution.py:327
  50.6 1.4 copy-done.20
  52.0 1.5 collective-permute-start.9
  53.6 2.6 convolution_convert_fusion.grad_active
  56.1 14.0 %collective-permute-done.9 = f32[2,64]{1,0:T(2,128)S(1)} collective-permute-done((f32[2,64]{1,0:T(2,128)S(1)}, f32[2,64]{1,0:T(2,128)S(1)}, u32[]{:S(2)}, u32[]{:S(2)}) %collective-permute-start.9) | collective-permute-done | bytes 544 | tf_op jit(solution)/shard_map/ppermute | solution.py:103
  70.2 3.3 collective-permute-start.10
  73.6 15.1 %collective-permute-done.10 = f32[64]{0:T(128)S(1)} collective-permute-done((f32[64]{0:T(128)S(1)}, f32[64]{0:T(128)S(1)}, u32[]{:S(2)}, u32[]{:S(2)}) %collective-permute-start.10) | collective-permute-done | bytes 288 | tf_op jit(solution)/shard_map/ppermute | solution.py:103
  89.9 1.3 copy-done.9
  91.2 6.2 %memory_forward.1.rows = bf16[16,128,768]{2,1,0:T(8,128)(2,1)} custom-call(s32[4]{0:T(128)S(1)} %get-tuple-element.470.facts, bf16[16,128,768]{2,1,0:T(8,128)(2,1)S(1)} %all-to-all-done.rows, f32[8,768]{1,0:T(8,128)S(1)} %maximum_maximum_fusion.stats, bf16[768,768]{1,0:T(8,128)(2,1)S(1)} %copy-done.9), custom_call_target="tpu_custom_call" | custom-call | flops 10000000000 | bytes 10000000 | tf_op jit(solution)/shard_map/memory_forward/pallas_call | solution.py:488
  97.5 14.0 %cross_forward.2 = (bf16[16,128,768]{2,1,0:T(8,128)(2,1)S(1)}, f32[8,512]{1,0:T(8,128)S(1)}, f32[8,512]{1,0:T(8,128)S(1)}, f32[384,512]{1,0:T(8,128)S(1)}) custom-call(s32[4]{0:T(128)S(1)} %get-tuple-element.470.facts, bf16[6,128,512]{2,1,0:T(8,128)(2,1)S(1)} %copy-done.25, bf16[16,128,768]{2,1,0:T(8,128)(2,1)} %memory_forward.1.rows, ...), custom_call_target="tpu_custom_call" | custom-call | flops 10000000000 | bytes 10000000 | tf_op jit(solution)/shard_map/cross_forward/pallas_call | solution.py:663
  111.5 12.0 %cross_forward.3 = (bf16[16,128,768]{2,1,0:T(8,128)(2,1)S(1)}, f32[8,512]{1,0:T(8,128)S(1)}, f32[8,512]{1,0:T(8,128)S(1)}, f32[384,512]{1,0:T(8,128)S(1)}) custom-call(s32[4]{0:T(128)S(1)} %get-tuple-element.411.facts, bf16[6,128,512]{2,1,0:T(8,128)(2,1)S(1)} %copy-done.25, bf16[16,128,768]{2,1,0:T(8,128)(2,1)S(1)} %collective-permute-done.11.rows, ...), custom_call_target="tpu_custom_call" | custom-call | flops 10000000000 | bytes 10000000 | tf_op jit(solution)/shard_map/cross_forward/pallas_call | solution.py:663
  124.8 3.0 collective-permute-done.12.came
  127.9 5.7 %feed_forward.1 = (f32[512,768]{1,0:T(8,128)S(1)}, bf16[512,768]{1,0:T(8,128)(2,1)S(1)}, bf16[512,1536]{1,0:T(8,128)(2,1)S(1)}, bf16[512,1536]{1,0:T(8,128)(2,1)S(1)}, f32[512,768]{1,0:T(8,128)S(1)}) custom-call(f32[512,768]{1,0:T(8,128)S(1)} %copy-done.63, f32[512,768]{1,0:T(8,128)S(1)} %get-tuple-element.420.own, ...), custom_call_target="tpu_custom_call" | custom-call | flops 10000000000 | bytes 10000000 | tf_op jit(solution)/shard_map/feed_forward/pallas_call | solution.py:756
  134.1 3.1 product.1
  137.2 2.4 feed_close.1
  139.6 3.3 feed_weights.1
  143.2 1.8 collective-permute-start.15
  145.0 2.1 collective-permute-start.16
  147.0 24.0 %cross_backward.2 = (bf16[16,128,768]{2,1,0:T(8,128)(2,1)}, bf16[16,128,768]{2,1,0:T(8,128)(2,1)S(1)}, f32[384,512]{1,0:T(8,128)}) custom-call(s32[4]{0:T(128)S(1)} %get-tuple-element.411.facts, bf16[6,512,128]{2,1,0:T(8,128)(2,1)S(1)} %copy-done.23, bf16[6,128,512]{2,1,0:T(8,128)(2,1)S(1)} %copy-done.25, bf16[6,512,128]{2,1,0:T(8,128)(2,1)S(1)} %get-tuple-element.439.grad, ...), custom_call_target="tpu_custom_call" | custom-call | flops 10000000000 | bytes 10000000 | tf_op jit(solution)/shard_map/cross_backward/pallas_call | solution.py:926
  172.5 23.9 %cross_backward.3 = (bf16[16,128,768]{2,1,0:T(8,128)(2,1)}, f32[16,128,768]{2,1,0:T(8,128)S(1)}, f32[384,512]{1,0:T(8,128)}) custom-call(s32[4]{0:T(128)S(1)} %get-tuple-element.470.facts, bf16[6,512,128]{2,1,0:T(8,128)(2,1)S(1)} %copy-done.23, bf16[6,128,512]{2,1,0:T(8,128)(2,1)S(1)} %copy-done.25, bf16[6,512,128]{2,1,0:T(8,128)(2,1)S(1)} %get-tuple-element.439.grad, ...), custom_call_target="tpu_custom_call" | custom-call | flops 10000000000 | bytes 10000000 | tf_op jit(solution)/shard_map/cross_backward/pallas_call | solution.py:926
  196.8 1.8 collective-permute-start.21
  198.6 1.2 collective-permute-start.22
  200.7 9.8 %memory_backward.1 = (bf16[16,128,768]{2,1,0:T(8,128)(2,1)}, bf16[16,128,768]{2,1,0:T(8,128)(2,1)}, bf16[16,128,768]{2,1,0:T(8,128)(2,1)}, f32[8,768]{1,0:T(8,128)}, f32[8,128]{1,0:T(8,128)S(1)}) custom-call(s32[4]{0:T(128)S(1)} %get-tuple-element.470.facts, bf16[16,128,768]{2,1,0:T(8,128)(2,1)S(1)} %all-to-all-done.rows, ...), custom_call_target="tpu_custom_call" | custom-call | flops 10000000000 | bytes 10000000 | tf_op jit(solution)/shard_map/memory_backward/pallas_call | solution.py:549
  213.0 3.9 %all-to-all-start.1 = ((bf16[16,128,768]{2,1,0:T(8,128)(2,1)}), bf16[16,128,768]{2,1,0:T(8,128)(2,1)S(1)}, u32[]{:S(2)}, u32[]{:S(2)}) async-start(bf16[16,128,768]{2,1,0:T(8,128)(2,1)} %get-tuple-element.530), calls=%async_computation.1 | async-start | bytes 6291456 | tf_op jit(solution)/shard_map/all_to_all | solution.py:1561
  223.2 1.8 collective-permute-start.26
  226.6 21.1 %conditional.2 = (f32[512,768]{1,0:T(8,128)}, f32[8,768]{1,0:T(8,128)S(1)}, f32[512,768]{1,0:T(8,128)}, f32[512,768]{1,0:T(8,128)}, f32[16,8,128]{2,1,0:T(8,128)...) conditional(s32[]{:T(128)} %bitcast.6, () %tuple.90, (f32[384,512]{1,0:T(8,128)S(1)}, ...), branch_computations={%region_2.3_spmd, %region_3.4_spmd} | conditional | flops 30000017408 | bytes 42687572 | solution.py:1564
  227.9 3.0 collective-permute-done.came
  230.9 9.7 %self_backward.1 = (f32[512,768]{1,0:T(8,128)}, bf16[512,768]{1,0:T(8,128)(2,1)S(1)}, f32[8,768]{1,0:T(8,128)S(1)}, bf16[512,1152]{1,0:T(8,128)(2,1)S(1)}, f32[512,768]{1,0:T(8,128)}) custom-call(s32[1]{0:T(128)} %get-tuple-element.73.facts, f32[512,768]{1,0:T(8,128)S(1)} %get-tuple-element.74.values, f32[512,768]{1,0:T(8,128)S(1)} %get-tuple-element.78.own, ...), custom_call_target="tpu_custom_call" | custom-call | flops 10000000000 | bytes 10000000 | tf_op jit(solution)/shard_map/cond/branch_1_fun/self_backward/pallas_call | solution.py:1266
  241.2 2.9 collective-permute-done.2
  244.1 3.3 side_weights.1
  248.3 18.8 %conditional.3 = (f32[6,8,128]{2,1,0:T(8,128)S(1)}, f32[1,512,768]{2,1,0:T(8,128)}, bf16[1,512,768]{2,1,0:T(8,128)(2,1)}, bf16[4,2,2,48,1152]{4,3,2,1,0:T(8,128)(2,1)S(1)}) conditional(s32[]{:T(128)} %bitcast.6, () %tuple.70, (s32[18]{0:T(128)S(1)}, bf16[16,128,768]{2,1,0:T(8,128)(2,1)}, bf16[16,128,768]{2,1,0:T(8,128)(2,1)}, ...), branch_computations={%region_4.5_spmd, %region_5.6_spmd} | conditional | flops 20004429824 | bytes 50652696 | solution.py:1564
  248.4 12.5 %memory_weights.1 = (bf16[768,768]{1,0:T(8,128)(2,1)S(1)}, f32[768,384]{1,0:T(8,128)S(1)}, bf16[768,384]{1,0:T(8,128)(2,1)S(1)}) custom-call(s32[18]{0:T(128)S(1)} %get-tuple-element.103.facts, bf16[16,128,768]{2,1,0:T(8,128)(2,1)} %get-tuple-element.104.refs_0_, bf16[16,128,768]{2,1,0:T(8,128)(2,1)} %get-tuple-element.105.refs_1_, ...), custom_call_target="tpu_custom_call" | custom-call | flops 10000000000 | bytes 10000000 | tf_op jit(solution)/shard_map/cond/branch_1_fun/memory_weights/pallas_call | solution.py:1029
  261.1 4.8 %input_back.1 = (f32[512,768]{1,0:T(8,128)}, bf16[512,768]{1,0:T(8,128)(2,1)}, f32[6,8,128]{2,1,0:T(8,128)S(1)}) custom-call(bf16[512,768]{1,0:T(8,128)(2,1)S(1)} %copy-done.57, f32[512,768]{1,0:T(8,128)} %get-tuple-element.101.own, f32[512,768]{1,0:T(8,128)} %get-tuple-element.111.came, f32[1,768]{1,0:T(1,128)S(1)} %broadcast_in_dim.48.gain, ...), custom_call_target="tpu_custom_call" | custom-call | flops 10000000000 | bytes 10000000 | tf_op jit(solution)/shard_map/cond/branch_1_fun/input_back/pallas_call | solution.py:1307
  268.1 1.7 collective-permute-start.30
  271.8 1.5 collective-permute-start.28
  273.3 1.5 collective-permute-start.29
  274.8 2.4 collective-permute-start.25
  277.8 19.9 %collective-permute-done.32 = f32[16,8,128]{2,1,0:T(8,128)S(1)} collective-permute-done((f32[16,8,128]{2,1,0:T(8,128)S(1)}, f32[16,8,128]{2,1,0:T(8,128)S(1)}, u32[]{:S(2)}, u32[]{:S(2)}) %collective-permute-start.32) | collective-permute-done | bytes 65568 | tf_op jit(solution)/shard_map/ppermute | solution.py:1556
  298.9 2.6 collective-permute-done.31
  302.5 3.0 merge_sums.11
  305.5 5.4 %collective-permute-start.35 = (bf16[4,48,1152]{2,1,0:T(8,128)(2,1)S(1)}, bf16[4,48,1152]{2,1,0:T(8,128)(2,1)S(1)}, u32[]{:S(2)}, u32[]{:S(2)}) collective-permute-start(bf16[4,48,1152]{2,1,0:T(8,128)(2,1)S(1)} %get-tuple-element.548), channel_id=1, source_target_pairs={{0,8},{2,10},{4,12},{6,14},{8,0},{10,2},{12,4},{14,6},{16,24},{18,... | collective-permute-start | bytes 1327112 | tf_op jit(solution)/shard_map/ppermute | solution.py:220
  310.8 1.5 collective-permute-start.33
  312.3 1.5 collective-permute-start.34
  314.3 7.0 %collective-permute-done.37 = f32[16,8,128]{2,1,0:T(8,128)S(1)} collective-permute-done((f32[16,8,128]{2,1,0:T(8,128)S(1)}, f32[16,8,128]{2,1,0:T(8,128)S(1)}, u32[]{:S(2)}, u32[]{:S(2)}) %collective-permute-start.37) | collective-permute-done | bytes 65568 | tf_op jit(solution)/shard_map/ppermute | solution.py:1556
  321.7 1.5 collective-permute-start.36
  323.3 2.4 collective-permute-done.38
  326.0 3.1 collective-permute-start.43
  330.5 1.5 collective-permute-start.41
  332.9 2.9 moved_rows.1.refs_1_
  335.8 1.7 copy-done.19
  337.6 1.6 collective-permute-start.44
  339.3 1.4 collective-permute-start.45
  340.6 1.6 collective-permute-start.46
  342.2 1.4 collective-permute-start.47
  343.6 7.7 %spread_docs.1 = f32[16,128,768]{2,1,0:T(8,128)} custom-call(s32[16]{0:T(128)S(1)} %copy-done.4, bf16[16,128,768]{2,1,0:T(8,128)(2,1)S(1)} %all-to-all-done.1.refs_0_, bf16[16,128,768]{2,1,0:T(8,128)(2,1)} %copy-done.19), custom_call_target="tpu_custom_call" | custom-call | flops 10000000000 | bytes 10000000 | tf_op jit(solution)/shard_map/spread_docs/pallas_call | solution.py:417
  353.0 1.9 assemble.1
  (285 shorter events, 35.9 us)
Async XLA Ops:
  9.8 80.1 %all-to-all-start = ((bf16[16,128,768]{2,1,0:T(8,128)(2,1)}), bf16[16,128,768]{2,1,0:T(8,128)(2,1)S(1)}, u32[]{:S(2)}, u32[]{:S(2)}) async-start(bf16[16,128,768]{2,1,0:T(8,128)(2,1)} %gather_docs.1), calls=%async_computation | async-start | bytes 6291456 | tf_op jit(solution)/shard_map/all_to_all | solution.py:1433
  27.7 10.0 %collective-permute-start.6 = (f32[512,768]{1,0:T(8,128)}, f32[512,768]{1,0:T(8,128)}, u32[]{:S(2)}, u32[]{:S(2)}) collective-permute-start(f32[512,768]{1,0:T(8,128)} %get-tuple-element.382.own), channel_id=1, source_target_pairs={{0,1},{1,0},{2,3},{3,2},{4,5},{5,4},{6,7},{7,6},{8,9},{9,8},{10,11... | collective-permute-start | bytes 4718600 | tf_op jit(solution)/shard_map/ppermute | solution.py:59
  32.6 5.1 %collective-permute-start.5 = (f32[16,64]{1,0:T(8,128)S(1)}, f32[16,64]{1,0:T(8,128)S(1)}, u32[]{:S(2)}, u32[]{:S(2)}) collective-permute-start(f32[16,64]{1,0:T(8,128)S(1)} %gather_fusion), channel_id=1, source_target_pairs={{0,1},{1,0},{2,3},{3,2},{4,5},{5,4},{6,7},{7,6},{8,9},{9,8},{10,11... | collective-permute-start | bytes 12296 | tf_op jit(solution)/shard_map/ppermute | solution.py:59
  37.7 6.0 %collective-permute-start.7 = (f32[2,2,2,64]{3,2,1,0:T(2,128)S(1)}, f32[2,2,2,64]{3,2,1,0:T(2,128)S(1)}, u32[]{:S(2)}, u32[]{:S(2)}) collective-permute-start(f32[2,2,2,64]{3,2,1,0:T(2,128)S(1)} %bitcast.83), channel_id=1, source_target_pairs={{0,2},{2,0},{4,6},{6,4},{8,10},{10,8},{12,14},{14,12},{16,18},{18,... | collective-permute-start | bytes 6152 | tf_op jit(solution)/shard_map/ppermute | solution.py:103
  43.8 8.3 %collective-permute-start.8 = (f32[2,2,64]{2,1,0:T(2,128)S(1)}, f32[2,2,64]{2,1,0:T(2,128)S(1)}, u32[]{:S(2)}, u32[]{:S(2)}) collective-permute-start(f32[2,2,64]{2,1,0:T(2,128)S(1)} %bitcast.85), channel_id=1, source_target_pairs={{0,4},{2,6},{4,0},{6,2},{8,12},{10,14},{12,8},{14,10},{16,20},{18,... | collective-permute-start | bytes 3080 | tf_op jit(solution)/shard_map/ppermute | solution.py:103
  52.0 18.1 %collective-permute-start.9 = (f32[2,64]{1,0:T(2,128)S(1)}, f32[2,64]{1,0:T(2,128)S(1)}, u32[]{:S(2)}, u32[]{:S(2)}) collective-permute-start(f32[2,64]{1,0:T(2,128)S(1)} %bitcast.86), channel_id=1, source_target_pairs={{0,8},{2,10},{4,12},{6,14},{8,0},{10,2},{12,4},{14,6},{16,24},{18,... | collective-permute-start | bytes 1544 | tf_op jit(solution)/shard_map/ppermute | solution.py:103
  70.2 18.6 %collective-permute-start.10 = (f32[64]{0:T(128)S(1)}, f32[64]{0:T(128)S(1)}, u32[]{:S(2)}, u32[]{:S(2)}) collective-permute-start(f32[64]{0:T(128)S(1)} %fusion.17), channel_id=1, source_target_pairs={{0,16},{2,18},{4,20},{6,22},{8,24},{10,26},{12,28},{14,30},{16,0},... | collective-permute-start | bytes 776 | tf_op jit(solution)/shard_map/ppermute | solution.py:103
  97.4 14.1 %collective-permute-start.11 = (bf16[16,128,768]{2,1,0:T(8,128)(2,1)}, bf16[16,128,768]{2,1,0:T(8,128)(2,1)S(1)}, u32[]{:S(2)}, u32[]{:S(2)}) collective-permute-start(bf16[16,128,768]{2,1,0:T(8,128)(2,1)} %memory_forward.1.rows), channel_id=1, source_target_pairs={{0,1},{1,0},{2,3},{3,2},{4,5},{5,4},{6,7},{7,6},{8,9},{9,8},{10,11... | collective-permute-start | bytes 9437192 | tf_op jit(solution)/shard_map/ppermute | solution.py:59
  111.5 12.0 %copy-start.54 = (bf16[16,128,768]{2,1,0:T(8,128)(2,1)}, bf16[16,128,768]{2,1,0:T(8,128)(2,1)S(1)}, u32[]{:S(2)}) copy-start(bf16[16,128,768]{2,1,0:T(8,128)(2,1)S(1)} %collective-permute-done.11.rows) | copy-start | bytes 9437188
  111.5 12.0 %copy-start.13 = (bf16[384,768]{1,0:T(8,128)(2,1)S(1)}, bf16[384,768]{1,0:T(8,128)(2,1)}, u32[]{:S(2)}) copy-start(bf16[384,768]{1,0:T(8,128)(2,1)} %weight.10) | copy-start | bytes 1769476
  124.3 3.6 %collective-permute-start.12 = (f32[512,768]{1,0:T(8,128)S(1)}, f32[512,768]{1,0:T(8,128)S(1)}, u32[]{:S(2)}, u32[]{:S(2)}) collective-permute-start(f32[512,768]{1,0:T(8,128)S(1)} %get-tuple-element.420.own), channel_id=1, source_target_pairs={{0,1},{1,0},{2,3},{3,2},{4,5},{5,4},{6,7},{7,6},{8,9},{9,8},{10,11... | collective-permute-start | bytes 4718600 | tf_op jit(solution)/shard_map/ppermute | solution.py:59
  133.6 3.6 %collective-permute-start.13 = (f32[512,768]{1,0:T(8,128)S(1)}, f32[512,768]{1,0:T(8,128)S(1)}, u32[]{:S(2)}, u32[]{:S(2)}) collective-permute-start(f32[512,768]{1,0:T(8,128)S(1)} %get-tuple-element.424.own), channel_id=1, source_target_pairs={{0,1},{1,0},{2,3},{3,2},{4,5},{5,4},{6,7},{7,6},{8,9},{9,8},{10,11... | collective-permute-start | bytes 4718600 | tf_op jit(solution)/shard_map/ppermute | solution.py:59
  143.1 27.9 %collective-permute-start.14 = (bf16[8,48,1152]{2,1,0:T(8,128)(2,1)S(1)}, bf16[8,48,1152]{2,1,0:T(8,128)(2,1)S(1)}, u32[]{:S(2)}, u32[]{:S(2)}) collective-permute-start(bf16[8,48,1152]{2,1,0:T(8,128)(2,1)S(1)} %bitcast.78), channel_id=1, source_target_pairs={{0,8},{2,10},{4,12},{6,14},{8,0},{10,2},{12,4},{14,6},{16,24},{18,... | collective-permute-start | bytes 2654216 | tf_op jit(solution)/shard_map/ppermute | solution.py:220
  143.2 27.9 %collective-permute-start.15 = (bf16[8,48,1152]{2,1,0:T(8,128)(2,1)S(1)}, bf16[8,48,1152]{2,1,0:T(8,128)(2,1)S(1)}, u32[]{:S(2)}, u32[]{:S(2)}) collective-permute-start(bf16[8,48,1152]{2,1,0:T(8,128)(2,1)S(1)} %dynamic-slice_bitcast_fusion), channel_id=1, source_target_pairs={{0,2},{2,0},{4,6},{6,4},{8,10},{10,8},{12,14},{14,12},{16,18},{18,... | collective-permute-start | bytes 2654216 | tf_op jit(solution)/shard_map/ppermute | solution.py:220
  145.0 26.1 %collective-permute-start.16 = (bf16[8,48,1152]{2,1,0:T(8,128)(2,1)S(1)}, bf16[8,48,1152]{2,1,0:T(8,128)(2,1)S(1)}, u32[]{:S(2)}, u32[]{:S(2)}) collective-permute-start(bf16[8,48,1152]{2,1,0:T(8,128)(2,1)S(1)} %bitcast.77), channel_id=1, source_target_pairs={{0,4},{2,6},{4,0},{6,2},{8,12},{10,14},{12,8},{14,10},{16,20},{18,... | collective-permute-start | bytes 2654216 | tf_op jit(solution)/shard_map/ppermute | solution.py:220
  171.0 29.7 %collective-permute-start.20 = (bf16[16,128,768]{2,1,0:T(8,128)(2,1)S(1)}, bf16[16,128,768]{2,1,0:T(8,128)(2,1)S(1)}, u32[]{:S(2)}, u32[]{:S(2)}) collective-permute-start(bf16[16,128,768]{2,1,0:T(8,128)(2,1)S(1)} %get-tuple-element.472), channel_id=1, source_target_pairs={{0,1},{1,0},{2,3},{3,2},{4,5},{5,4},{6,7},{7,6},{8,9},{9,8},{10,11... | collective-permute-start | bytes 9437192 | tf_op jit(solution)/shard_map/ppermute | solution.py:59
  172.1 24.3 %collective-permute-start.17 = (bf16[4,48,1152]{2,1,0:T(8,128)(2,1)S(1)}, bf16[4,48,1152]{2,1,0:T(8,128)(2,1)S(1)}, u32[]{:S(2)}, u32[]{:S(2)}) collective-permute-start(bf16[4,48,1152]{2,1,0:T(8,128)(2,1)S(1)} %get-tuple-element.456), channel_id=1, source_target_pairs={{0,16},{2,18},{4,20},{6,22},{8,24},{10,26},{12,28},{14,30},{16,0},... | collective-permute-start | bytes 1327112 | tf_op jit(solution)/shard_map/ppermute | solution.py:220
  172.1 24.3 %collective-permute-start.18 = (bf16[4,48,1152]{2,1,0:T(8,128)(2,1)S(1)}, bf16[4,48,1152]{2,1,0:T(8,128)(2,1)S(1)}, u32[]{:S(2)}, u32[]{:S(2)}) collective-permute-start(bf16[4,48,1152]{2,1,0:T(8,128)(2,1)S(1)} %get-tuple-element.457), channel_id=1, source_target_pairs={{0,8},{2,10},{4,12},{6,14},{8,0},{10,2},{12,4},{14,6},{16,24},{18,... | collective-permute-start | bytes 1327112 | tf_op jit(solution)/shard_map/ppermute | solution.py:220
  172.2 24.2 %collective-permute-start.19 = (bf16[4,48,1152]{2,1,0:T(8,128)(2,1)S(1)}, bf16[4,48,1152]{2,1,0:T(8,128)(2,1)S(1)}, u32[]{:S(2)}, u32[]{:S(2)}) collective-permute-start(bf16[4,48,1152]{2,1,0:T(8,128)(2,1)S(1)} %get-tuple-element.458), channel_id=1, source_target_pairs={{0,2},{2,0},{4,6},{6,4},{8,10},{10,8},{12,14},{14,12},{16,18},{18,... | collective-permute-start | bytes 1327112 | tf_op jit(solution)/shard_map/ppermute | solution.py:220
  196.8 13.8 %copy-start.26 = (bf16[2,48,1152]{2,1,0:T(8,128)(2,1)}, bf16[2,48,1152]{2,1,0:T(8,128)(2,1)S(1)}, u32[]{:S(2)}) copy-start(bf16[2,48,1152]{2,1,0:T(8,128)(2,1)S(1)} %get-tuple-element.477.refs_0_) | copy-start | bytes 663556
  196.8 13.8 %copy-start.28 = (bf16[2,48,1152]{2,1,0:T(8,128)(2,1)}, bf16[2,48,1152]{2,1,0:T(8,128)(2,1)S(1)}, u32[]{:S(2)}) copy-start(bf16[2,48,1152]{2,1,0:T(8,128)(2,1)S(1)} %get-tuple-element.478.refs_1_) | copy-start | bytes 663556
  196.8 13.8 %copy-start.30 = (bf16[2,48,1152]{2,1,0:T(8,128)(2,1)}, bf16[2,48,1152]{2,1,0:T(8,128)(2,1)S(1)}, u32[]{:S(2)}) copy-start(bf16[2,48,1152]{2,1,0:T(8,128)(2,1)S(1)} %get-tuple-element.479.refs_2_) | copy-start | bytes 663556
  196.8 13.8 %collective-permute-start.21 = (bf16[2,48,1152]{2,1,0:T(8,128)(2,1)S(1)}, bf16[2,48,1152]{2,1,0:T(8,128)(2,1)S(1)}, u32[]{:S(2)}, u32[]{:S(2)}) collective-permute-start(bf16[2,48,1152]{2,1,0:T(8,128)(2,1)S(1)} %get-tuple-element.480), channel_id=1, source_target_pairs={{0,2},{2,0},{4,6},{6,4},{8,10},{10,8},{12,14},{14,12},{16,18},{18,... | collective-permute-start | bytes 663560 | tf_op jit(solution)/shard_map/ppermute | solution.py:220
  198.6 13.0 %collective-permute-start.22 = (bf16[2,48,1152]{2,1,0:T(8,128)(2,1)S(1)}, bf16[2,48,1152]{2,1,0:T(8,128)(2,1)S(1)}, u32[]{:S(2)}, u32[]{:S(2)}) collective-permute-start(bf16[2,48,1152]{2,1,0:T(8,128)(2,1)S(1)} %get-tuple-element.481), channel_id=1, source_target_pairs={{0,16},{2,18},{4,20},{6,22},{8,24},{10,26},{12,28},{14,30},{16,0},... | collective-permute-start | bytes 663560 | tf_op jit(solution)/shard_map/ppermute | solution.py:220
  199.8 12.5 %collective-permute-start.23 = (bf16[2,48,1152]{2,1,0:T(8,128)(2,1)S(1)}, bf16[2,48,1152]{2,1,0:T(8,128)(2,1)S(1)}, u32[]{:S(2)}, u32[]{:S(2)}) collective-permute-start(bf16[2,48,1152]{2,1,0:T(8,128)(2,1)S(1)} %get-tuple-element.482), channel_id=1, source_target_pairs={{0,8},{2,10},{4,12},{6,14},{8,0},{10,2},{12,4},{14,6},{16,24},{18,... | collective-permute-start | bytes 663560 | tf_op jit(solution)/shard_map/ppermute | solution.py:220
  213.0 88.6 %all-to-all-start.1 = ((bf16[16,128,768]{2,1,0:T(8,128)(2,1)}), bf16[16,128,768]{2,1,0:T(8,128)(2,1)S(1)}, u32[]{:S(2)}, u32[]{:S(2)}) async-start(bf16[16,128,768]{2,1,0:T(8,128)(2,1)} %get-tuple-element.530), calls=%async_computation.1 | async-start | bytes 6291456 | tf_op jit(solution)/shard_map/all_to_all | solution.py:1561
  216.8 30.9 %collective-permute-start.24 = (f32[512,768]{1,0:T(8,128)}, f32[512,768]{1,0:T(8,128)}, u32[]{:S(2)}, u32[]{:S(2)}) collective-permute-start(f32[512,768]{1,0:T(8,128)} %product.1), channel_id=1, source_target_pairs={{0,1},{1,0},{2,3},{3,2},{4,5},{5,4},{6,7},{7,6},{8,9},{9,8},{10,11... | collective-permute-start | bytes 4718600 | tf_op jit(solution)/shard_map/ppermute | solution.py:59
  223.2 48.6 %collective-permute-start.26 = (bf16[1,48,1152]{2,1,0:T(8,128)(2,1)}, bf16[1,48,1152]{2,1,0:T(8,128)(2,1)S(1)}, u32[]{:S(2)}, u32[]{:S(2)}) collective-permute-start(bf16[1,48,1152]{2,1,0:T(8,128)(2,1)} %get-tuple-element.522), channel_id=1, source_target_pairs={{0,4},{2,6},{4,0},{6,2},{8,12},{10,14},{12,8},{14,10},{16,20},{18,... | collective-permute-start | bytes 331784 | tf_op jit(solution)/shard_map/ppermute | solution.py:220
  225.0 46.9 %collective-permute-start.27 = (bf16[1,48,1152]{2,1,0:T(8,128)(2,1)}, bf16[1,48,1152]{2,1,0:T(8,128)(2,1)S(1)}, u32[]{:S(2)}, u32[]{:S(2)}) collective-permute-start(bf16[1,48,1152]{2,1,0:T(8,128)(2,1)} %get-tuple-element.523), channel_id=1, source_target_pairs={{0,4},{2,6},{4,0},{6,2},{8,12},{10,14},{12,8},{14,10},{16,20},{18,... | collective-permute-start | bytes 331784 | tf_op jit(solution)/shard_map/ppermute | solution.py:220
  226.6 21.1 %copy-start.48 = (f32[768]{0:T(1024)S(1)}, f32[768]{0:T(1024)}, u32[]{:S(2)}) copy-start(f32[768]{0:T(1024)} %param.33) | copy-start | bytes 9220
  227.3 3.6 %collective-permute-start = (f32[512,768]{1,0:T(8,128)S(1)}, f32[512,768]{1,0:T(8,128)S(1)}, u32[]{:S(2)}, u32[]{:S(2)}) collective-permute-start(f32[512,768]{1,0:T(8,128)S(1)} %get-tuple-element.78.own), channel_id=1, source_target_pairs={{0,1},{1,0},{2,3},{3,2},{4,5},{5,4},{6,7},{7,6},{8,9},{9,8},{10,11... | collective-permute-start | bytes 4718600 | tf_op jit(solution)/shard_map/cond/branch_1_fun/ppermute | solution.py:59
  240.6 6.8 %collective-permute-start.1 = (f32[512,768]{1,0:T(8,128)}, f32[512,768]{1,0:T(8,128)}, u32[]{:S(2)}, u32[]{:S(2)}) collective-permute-start(f32[512,768]{1,0:T(8,128)} %get-tuple-element.635), channel_id=1, source_target_pairs={{0,1},{1,0},{2,3},{3,2},{4,5},{5,4},{6,7},{7,6},{8,9},{9,8},{10,11... | collective-permute-start | bytes 4718600 | tf_op jit(solution)/shard_map/cond/branch_1_fun/ppermute | solution.py:59
  241.0 3.0 collective-permute-start.2
  248.3 12.7 %copy-start.41 = (f32[512,768]{1,0:T(8,128)S(1)}, f32[512,768]{1,0:T(8,128)}, u32[]{:S(2)}) copy-start(f32[512,768]{1,0:T(8,128)} %get-tuple-element.113.grad_first) | copy-start | bytes 4718596 | tf_op jit(solution)/shard_map/cond
  248.3 12.7 %copy-start.56 = (f32[512,768]{1,0:T(8,128)S(1)}, f32[512,768]{1,0:T(8,128)}, u32[]{:S(2)}) copy-start(f32[512,768]{1,0:T(8,128)} %get-tuple-element.115.result_own) | copy-start | bytes 4718596 | tf_op jit(solution)/shard_map/cond
  248.3 12.7 %copy-start.57 = (bf16[512,768]{1,0:T(8,128)(2,1)S(1)}, bf16[512,768]{1,0:T(8,128)(2,1)}, u32[]{:S(2)}) copy-start(bf16[512,768]{1,0:T(8,128)(2,1)} %get-tuple-element.100.values) | copy-start | bytes 2359300 | tf_op jit(solution)/shard_map/cond
  248.3 12.7 %copy-start.62 = (f32[512,768]{1,0:T(8,128)S(1)}, f32[512,768]{1,0:T(8,128)}, u32[]{:S(2)}) copy-start(f32[512,768]{1,0:T(8,128)} %get-tuple-element.114.second) | copy-start | bytes 4718596 | tf_op jit(solution)/shard_map/cond
  248.3 12.7 %copy-start.72 = (f32[8,768]{1,0:T(8,128)S(1)}, f32[8,768]{1,0:T(8,128)}, u32[]{:S(2)}) copy-start(f32[8,768]{1,0:T(8,128)} %get-tuple-element.117.act_sums) | copy-start | bytes 73732 | tf_op jit(solution)/shard_map/cond
  248.4 12.7 %copy-start.73 = (f32[8,768]{1,0:T(8,128)S(1)}, f32[8,768]{1,0:T(8,128)}, u32[]{:S(2)}) copy-start(f32[8,768]{1,0:T(8,128)} %get-tuple-element.119.ffn_gain_grad) | copy-start | bytes 73732 | tf_op jit(solution)/shard_map/cond
  260.8 5.0 %collective-permute-start.3 = (bf16[768,384]{1,0:T(8,128)(2,1)S(1)}, bf16[768,384]{1,0:T(8,128)(2,1)S(1)}, u32[]{:S(2)}, u32[]{:S(2)}) collective-permute-start(bf16[768,384]{1,0:T(8,128)(2,1)S(1)} %get-tuple-element.121), channel_id=1, source_target_pairs={{0,1},{1,0},{2,3},{3,2},{4,5},{5,4},{6,7},{7,6},{8,9},{9,8},{10,11... | collective-permute-start | bytes 1769480 | tf_op jit(solution)/shard_map/cond/branch_1_fun/ppermute | solution.py:59
  265.9 1.2 collective-permute-start.4
  267.1 31.8 %copy-start.38 = (bf16[4,2,2,48,1152]{4,3,2,1,0:T(8,128)(2,1)}, bf16[4,2,2,48,1152]{4,3,2,1,0:T(8,128)(2,1)S(1)}, u32[]{:S(2)}) copy-start(bf16[4,2,2,48,1152]{4,3,2,1,0:T(8,128)(2,1)S(1)} %get-tuple-element.520.refs_3_) | copy-start | bytes 5308420
  268.1 33.4 %collective-permute-start.30 = (bf16[8,48,1152]{2,1,0:T(8,128)(2,1)}, bf16[8,48,1152]{2,1,0:T(8,128)(2,1)}, u32[]{:S(2)}, u32[]{:S(2)}) collective-permute-start(bf16[8,48,1152]{2,1,0:T(8,128)(2,1)} %bitcast.35), channel_id=1, source_target_pairs={{0,4},{2,6},{4,0},{6,2},{8,12},{10,14},{12,8},{14,10},{16,20},{18,... | collective-permute-start | bytes 2654216 | tf_op jit(solution)/shard_map/ppermute | solution.py:220
  271.8 29.7 %collective-permute-start.28 = (bf16[8,48,1024]{2,1,0:T(8,128)(2,1)}, bf16[8,48,1024]{2,1,0:T(8,128)(2,1)}, u32[]{:S(2)}, u32[]{:S(2)}) collective-permute-start(bf16[8,48,1024]{2,1,0:T(8,128)(2,1)} %dynamic-slice_bitcast_fusion.1), channel_id=1, source_target_pairs={{0,2},{2,0},{4,6},{6,4},{8,10},{10,8},{12,14},{14,12},{16,18},{18,... | collective-permute-start | bytes 2359304 | tf_op jit(solution)/shard_map/ppermute | solution.py:220
  273.3 28.2 %collective-permute-start.29 = (bf16[8,48,896]{2,1,0:T(8,128)(2,1)}, bf16[8,48,896]{2,1,0:T(8,128)(2,1)}, u32[]{:S(2)}, u32[]{:S(2)}) collective-permute-start(bf16[8,48,896]{2,1,0:T(8,128)(2,1)} %bitcast.34), channel_id=1, source_target_pairs={{0,8},{2,10},{4,12},{6,14},{8,0},{10,2},{12,4},{14,6},{16,24},{18,... | collective-permute-start | bytes 2064392 | tf_op jit(solution)/shard_map/ppermute | solution.py:220
  274.8 26.7 %collective-permute-start.25 = (bf16[1,48,1152]{2,1,0:T(8,128)(2,1)S(1)}, bf16[1,48,1152]{2,1,0:T(8,128)(2,1)}, u32[]{:S(2)}, u32[]{:S(2)}) collective-permute-start(bf16[1,48,1152]{2,1,0:T(8,128)(2,1)S(1)} %get-tuple-element.521), channel_id=1, source_target_pairs={{0,16},{2,18},{4,20},{6,22},{8,24},{10,26},{12,28},{14,30},{16,0},... | collective-permute-start | bytes 331784 | tf_op jit(solution)/shard_map/ppermute | solution.py:220
  277.2 20.5 %collective-permute-start.32 = (f32[16,8,128]{2,1,0:T(8,128)S(1)}, f32[16,8,128]{2,1,0:T(8,128)S(1)}, u32[]{:S(2)}, u32[]{:S(2)}) collective-permute-start(f32[16,8,128]{2,1,0:T(8,128)S(1)} %copy-done.44), channel_id=1, source_target_pairs={{0,2},{2,0},{4,6},{6,4},{8,10},{10,8},{12,14},{14,12},{16,18},{18,... | collective-permute-start | bytes 196616 | tf_op jit(solution)/shard_map/ppermute | solution.py:1556
  297.7 3.8 %collective-permute-start.31 = (f32[6,8,128]{2,1,0:T(8,128)S(1)}, f32[6,8,128]{2,1,0:T(8,128)S(1)}, u32[]{:S(2)}, u32[]{:S(2)}) collective-permute-start(f32[6,8,128]{2,1,0:T(8,128)S(1)} %get-tuple-element.531), channel_id=1, source_target_pairs={{0,2},{2,0},{4,6},{6,4},{8,10},{10,8},{12,14},{14,12},{16,18},{18,... | collective-permute-start | bytes 73736 | tf_op jit(solution)/shard_map/ppermute | solution.py:1556
  305.5 20.3 %collective-permute-start.35 = (bf16[4,48,1152]{2,1,0:T(8,128)(2,1)S(1)}, bf16[4,48,1152]{2,1,0:T(8,128)(2,1)S(1)}, u32[]{:S(2)}, u32[]{:S(2)}) collective-permute-start(bf16[4,48,1152]{2,1,0:T(8,128)(2,1)S(1)} %get-tuple-element.548), channel_id=1, source_target_pairs={{0,8},{2,10},{4,12},{6,14},{8,0},{10,2},{12,4},{14,6},{16,24},{18,... | collective-permute-start | bytes 1327112 | tf_op jit(solution)/shard_map/ppermute | solution.py:220
  310.8 14.9 %collective-permute-start.33 = (bf16[4,48,1024]{2,1,0:T(8,128)(2,1)S(1)}, bf16[4,48,1024]{2,1,0:T(8,128)(2,1)S(1)}, u32[]{:S(2)}, u32[]{:S(2)}) collective-permute-start(bf16[4,48,1024]{2,1,0:T(8,128)(2,1)S(1)} %get-tuple-element.546), channel_id=1, source_target_pairs={{0,4},{2,6},{4,0},{6,2},{8,12},{10,14},{12,8},{14,10},{16,20},{18,... | collective-permute-start | bytes 1179656 | tf_op jit(solution)/shard_map/ppermute | solution.py:220
  312.3 13.4 %collective-permute-start.34 = (bf16[4,48,896]{2,1,0:T(8,128)(2,1)S(1)}, bf16[4,48,896]{2,1,0:T(8,128)(2,1)S(1)}, u32[]{:S(2)}, u32[]{:S(2)}) collective-permute-start(bf16[4,48,896]{2,1,0:T(8,128)(2,1)S(1)} %get-tuple-element.547), channel_id=1, source_target_pairs={{0,2},{2,0},{4,6},{6,4},{8,10},{10,8},{12,14},{14,12},{16,18},{18,... | collective-permute-start | bytes 1032200 | tf_op jit(solution)/shard_map/ppermute | solution.py:220
  313.8 7.5 %collective-permute-start.37 = (f32[16,8,128]{2,1,0:T(8,128)S(1)}, f32[16,8,128]{2,1,0:T(8,128)S(1)}, u32[]{:S(2)}, u32[]{:S(2)}) collective-permute-start(f32[16,8,128]{2,1,0:T(8,128)S(1)} %copy-done.42), channel_id=1, source_target_pairs={{0,4},{2,6},{4,0},{6,2},{8,12},{10,14},{12,8},{14,10},{16,20},{18,... | collective-permute-start | bytes 196616 | tf_op jit(solution)/shard_map/ppermute | solution.py:1556
  321.3 4.3 %collective-permute-start.38 = (f32[16,8,128]{2,1,0:T(8,128)S(1)}, f32[16,8,128]{2,1,0:T(8,128)S(1)}, u32[]{:S(2)}, u32[]{:S(2)}) collective-permute-start(f32[16,8,128]{2,1,0:T(8,128)S(1)} %add.145), channel_id=1, source_target_pairs={{0,8},{2,10},{4,12},{6,14},{8,0},{10,2},{12,4},{14,6},{16,24},{18,... | collective-permute-start | bytes 196616 | tf_op jit(solution)/shard_map/ppermute | solution.py:1556
  321.7 3.9 %collective-permute-start.36 = (f32[6,8,128]{2,1,0:T(8,128)S(1)}, f32[6,8,128]{2,1,0:T(8,128)S(1)}, u32[]{:S(2)}, u32[]{:S(2)}) collective-permute-start(f32[6,8,128]{2,1,0:T(8,128)S(1)} %add.144), channel_id=1, source_target_pairs={{0,4},{2,6},{4,0},{6,2},{8,12},{10,14},{12,8},{14,10},{16,20},{18,... | collective-permute-start | bytes 73736 | tf_op jit(solution)/shard_map/ppermute | solution.py:1556
  326.0 6.8 %collective-permute-start.43 = (f32[16,8,128]{2,1,0:T(8,128)S(1)}, f32[16,8,128]{2,1,0:T(8,128)S(1)}, u32[]{:S(2)}, u32[]{:S(2)}) collective-permute-start(f32[16,8,128]{2,1,0:T(8,128)S(1)} %add.146), channel_id=1, source_target_pairs={{0,16},{2,18},{4,20},{6,22},{8,24},{10,26},{12,28},{14,30},{16,0},... | collective-permute-start | bytes 196616 | tf_op jit(solution)/shard_map/ppermute | solution.py:1556
  329.1 8.3 %collective-permute-start.39 = (bf16[2,48,1024]{2,1,0:T(8,128)(2,1)S(1)}, bf16[2,48,1024]{2,1,0:T(8,128)(2,1)S(1)}, u32[]{:S(2)}, u32[]{:S(2)}) collective-permute-start(bf16[2,48,1024]{2,1,0:T(8,128)(2,1)S(1)} %get-tuple-element.562), channel_id=1, source_target_pairs={{0,8},{2,10},{4,12},{6,14},{8,0},{10,2},{12,4},{14,6},{16,24},{18,... | collective-permute-start | bytes 589832 | tf_op jit(solution)/shard_map/ppermute | solution.py:220
  330.2 7.3 %collective-permute-start.40 = (bf16[2,48,896]{2,1,0:T(8,128)(2,1)S(1)}, bf16[2,48,896]{2,1,0:T(8,128)(2,1)S(1)}, u32[]{:S(2)}, u32[]{:S(2)}) collective-permute-start(bf16[2,48,896]{2,1,0:T(8,128)(2,1)S(1)} %get-tuple-element.563), channel_id=1, source_target_pairs={{0,4},{2,6},{4,0},{6,2},{8,12},{10,14},{12,8},{14,10},{16,20},{18,... | collective-permute-start | bytes 516104 | tf_op jit(solution)/shard_map/ppermute | solution.py:220
  330.5 7.0 %collective-permute-start.41 = (bf16[2,48,1152]{2,1,0:T(8,128)(2,1)S(1)}, bf16[2,48,1152]{2,1,0:T(8,128)(2,1)S(1)}, u32[]{:S(2)}, u32[]{:S(2)}) collective-permute-start(bf16[2,48,1152]{2,1,0:T(8,128)(2,1)S(1)} %get-tuple-element.564), channel_id=1, source_target_pairs={{0,2},{2,0},{4,6},{6,4},{8,10},{10,8},{12,14},{14,12},{16,18},{18,... | collective-permute-start | bytes 663560 | tf_op jit(solution)/shard_map/ppermute | solution.py:220
  332.0 5.5 %collective-permute-start.42 = (f32[6,8,128]{2,1,0:T(8,128)S(1)}, f32[6,8,128]{2,1,0:T(8,128)S(1)}, u32[]{:S(2)}, u32[]{:S(2)}) collective-permute-start(f32[6,8,128]{2,1,0:T(8,128)S(1)} %add.147), channel_id=1, source_target_pairs={{0,8},{2,10},{4,12},{6,14},{8,0},{10,2},{12,4},{14,6},{16,24},{18,... | collective-permute-start | bytes 73736 | tf_op jit(solution)/shard_map/ppermute | solution.py:1556
  337.6 13.7 %collective-permute-start.44 = (bf16[1,48,1024]{2,1,0:T(8,128)(2,1)S(1)}, bf16[1,48,1024]{2,1,0:T(8,128)(2,1)S(1)}, u32[]{:S(2)}, u32[]{:S(2)}) collective-permute-start(bf16[1,48,1024]{2,1,0:T(8,128)(2,1)S(1)} %get-tuple-element.575), channel_id=1, source_target_pairs={{0,16},{2,18},{4,20},{6,22},{8,24},{10,26},{12,28},{14,30},{16,0},... | collective-permute-start | bytes 294920 | tf_op jit(solution)/shard_map/ppermute | solution.py:220
  339.3 12.0 %collective-permute-start.45 = (bf16[1,48,896]{2,1,0:T(8,128)(2,1)S(1)}, bf16[1,48,896]{2,1,0:T(8,128)(2,1)S(1)}, u32[]{:S(2)}, u32[]{:S(2)}) collective-permute-start(bf16[1,48,896]{2,1,0:T(8,128)(2,1)S(1)} %get-tuple-element.576), channel_id=1, source_target_pairs={{0,16},{2,18},{4,20},{6,22},{8,24},{10,26},{12,28},{14,30},{16,0},... | collective-permute-start | bytes 258056 | tf_op jit(solution)/shard_map/ppermute | solution.py:220
  340.6 10.7 %collective-permute-start.46 = (bf16[1,48,1152]{2,1,0:T(8,128)(2,1)S(1)}, bf16[1,48,1152]{2,1,0:T(8,128)(2,1)S(1)}, u32[]{:S(2)}, u32[]{:S(2)}) collective-permute-start(bf16[1,48,1152]{2,1,0:T(8,128)(2,1)S(1)} %get-tuple-element.577), channel_id=1, source_target_pairs={{0,16},{2,18},{4,20},{6,22},{8,24},{10,26},{12,28},{14,30},{16,0},... | collective-permute-start | bytes 331784 | tf_op jit(solution)/shard_map/ppermute | solution.py:220
  342.2 9.1 %collective-permute-start.47 = (f32[6,8,128]{2,1,0:T(8,128)S(1)}, f32[6,8,128]{2,1,0:T(8,128)S(1)}, u32[]{:S(2)}, u32[]{:S(2)}) collective-permute-start(f32[6,8,128]{2,1,0:T(8,128)S(1)} %add.149), channel_id=1, source_target_pairs={{0,16},{2,18},{4,20},{6,22},{8,24},{10,26},{12,28},{14,30},{16,0},... | collective-permute-start | bytes 73736 | tf_op jit(solution)/shard_map/ppermute | solution.py:1556
  351.4 1.5 collective-permute-start.48
  (62 other events, 263.6 us)

commit v2 on v1

--- a/solution.py
+++ b/solution.py
@@ -282,16 +282,12 @@
     return nothing
 
 
-def gather_kernel(owner, rows, out, held, came, gone, *, docs):
-    loads = [pltpu.make_async_copy(rows.at[owner[slot]], held.at[slot], came.at[slot]) for slot in range(docs)]
-    stores = [pltpu.make_async_copy(held.at[slot], out.at[slot], gone.at[slot]) for slot in range(docs)]
-    for load in loads:
-        load.start()
-    for load, store in zip(loads, stores):
-        load.wait()
-        store.start()
-    for store in stores:
-        store.wait()
+def gather_kernel(owner, rows, out, done, *, docs):
+    copies = [pltpu.make_async_copy(rows.at[owner[slot]], out.at[slot], done.at[slot]) for slot in range(docs)]
+    for copy in copies:
+        copy.start()
+    for copy in copies:
+        copy.wait()
 
 
 def gather_docs(memory_in, doc_owner):
@@ -301,16 +297,12 @@
         grid_spec=pltpu.PrefetchScalarGridSpec(
             num_scalar_prefetch=1,
             grid=(),
-            in_specs=[pl.BlockSpec(memory_space=pl.ANY)],
+            in_specs=[pl.BlockSpec(memory_space=pltpu.VMEM)],
             out_specs=pl.BlockSpec(memory_space=pl.ANY),
-            scratch_shapes=[
-                pltpu.VMEM(memory_in.shape, low_type),
-                pltpu.SemaphoreType.DMA((docs,)),
-                pltpu.SemaphoreType.DMA((docs,)),
-            ],
+            scratch_shapes=[pltpu.SemaphoreType.DMA((docs,))],
         ),
         out_shape=pltpu.HBM(memory_in.shape, low_type),
-        compiler_params=pltpu.CompilerParams(vmem_limit_bytes=vmem_large),
+        compiler_params=pltpu.CompilerParams(vmem_limit_bytes=vmem_budget),
         cost_estimate=heavy,
         name="gather_docs",
     )(doc_owner, memory_in)

time: 361 us -> 358 us (level)
  Pallas kernels: 179 us -> 175 us
    pallas_call x1, Pallas kernels: 6.53 us -> 2.33 us  [gather_docs(): pl.pallas_call(partial(gather_kernel, docs=docs), grid_spec=pltpu.Prefetc...]
  transfers between devices with their start and end apart: 51 -> 51, of which waited for: 12 -> 11; matrix products, arithmetic and copies ran while one was open for 4% -> 4% of each run, Pallas kernels for 38% -> 39%
where the time goes in v2:
time: 358 us; the launch traced here: 353 us
  Pallas kernels  175 us (49%)
  waiting for transfers between devices  71.7 us (20%)
  starting transfers between devices  68.5 us (19%)
  local copies, waits for them, and re-layouts  22.8 us (6%)
  other arithmetic  5.49 us (2%)
  between operations  5.45 us (2%)
  matrix products  4.08 us (1%)
    pallas_call x2, Pallas kernels, cross_backward(): pl.pallas_call(partial(cross_backward_kernel, chips=chips, span=span, fir...  47.9 us
    ppermute x24, starting transfers between devices, leave(): lax.ppermute(leaving, 'dp', [(chip, chip ^ 1 << bit) for chip in range(ch...  35.6 us
    ppermute x8, waiting for transfers between devices, dp_hop(): lax.ppermute(value, 'dp', [(chip, chip ^ 1 << bit) for chip in range(chip...  32.3 us
    ppermute x4, waiting for transfers between devices, send(): lax.ppermute(sent, 'dp', [(chip, chip ^ 1 << order[0]) for chip in range(...  29.2 us
    pallas_call x2, Pallas kernels, cross_forward(): pl.pallas_call(partial(cross_forward_kernel, chips=chips, span=span), gri...  25.9 us
    unnamed x138, local copies, waits for them, and re-layouts  16.8 us
    pallas_call x1, Pallas kernels, memory_weights(): pl.pallas_call(partial(memory_weights_kernel, pieces=pieces, chips=chips,...  12.5 us
    ppermute x13, waiting for transfers between devices, other_core(): return lax.ppermute(values, 'mp', [(0, 1), (1, 0)])  10.2 us
  transfers between devices with their start and end apart: 51, of which 11 were waited for; matrix products, arithmetic and copies ran while one was open for 4% of the time, Pallas kernels for 39%

profile of v2, /device:TPU:0, one launch (start us, length us, event | category | flops | bytes accessed | tf_op | source)
XLA Modules:
  0.0 352.9 jit_solution(5648158260515420356)
XLA Ops:
  0.7 1.9 copy-done
  3.2 2.3 gather_docs.1
  5.6 8.3 %all-to-all-start = ((bf16[16,128,768]{2,1,0:T(8,128)(2,1)}), bf16[16,128,768]{2,1,0:T(8,128)(2,1)S(1)}, u32[]{:S(2)}, u32[]{:S(2)}) async-start(bf16[16,128,768]{2,1,0:T(8,128)(2,1)} %gather_docs.1), calls=%async_computation | async-start | bytes 6291456 | tf_op jit(solution)/shard_map/all_to_all | solution.py:1425
  14.5 9.0 %self_forward.1 = (bf16[512,768]{1,0:T(8,128)(2,1)}, bf16[512,1152]{1,0:T(8,128)(2,1)}, bf16[512,384]{1,0:T(8,128)(2,1)}, f32[8,512]{1,0:T(8,128)}, f32[512,768]{1,0:T(8,128)}) custom-call(s32[1]{0:T(128)} %dynamic_slice.62.facts, bf16[512,768]{1,0:T(8,128)(2,1)} %bitcast.90, f32[1,768]{1,0:T(1,128)S(1)} %broadcast_in_dim.82.gain, ...), custom_call_target="tpu_custom_call" | custom-call | flops 10000000000 | bytes 10000000 | tf_op jit(solution)/shard_map/self_forward/pallas_call | solution.py:1147
  23.6 3.3 select_reduce_fusion
  33.5 2.0 collective-permute-start.7
  35.5 4.0 %query_forward.1 = (f32[512,768]{1,0:T(8,128)}, bf16[512,768]{1,0:T(8,128)(2,1)}, bf16[6,512,128]{2,1,0:T(8,128)(2,1)S(1)}, bf16[6,128,512]{2,1,0:T(8,128)(2,1)S(1)}) custom-call(bf16[512,768]{1,0:T(8,128)(2,1)} %bitcast.91, f32[512,768]{1,0:T(8,128)} %get-tuple-element.382.own, f32[512,768]{1,0:T(8,128)} %collective-permute-done.6.came, ...), custom_call_target="tpu_custom_call" | custom-call | flops 10000000000 | bytes 10000000 | tf_op jit(solution)/shard_map/query_forward/pallas_call | solution.py:1191
  39.6 1.5 collective-permute-start.8
  41.1 5.3 %prepare_weights.1.key_weight.value_weight = bf16[768,1536]{1,0:T(8,128)(2,1)S(1)} custom-call(bf16[768,2,768]{2,1,0:T(2,128)(2,1)S(1)} %copy-done.5), custom_call_target="tpu_custom_call" | custom-call | flops 10000000000 | bytes 10000000 | tf_op jit(solution)/shard_map/prepare_weights/pallas_call | solution.py:319
  46.4 1.4 copy-done.20
  47.8 1.5 collective-permute-start.9
  49.4 2.6 convolution_convert_fusion.grad_active
  51.9 14.0 %collective-permute-done.9 = f32[2,64]{1,0:T(2,128)S(1)} collective-permute-done((f32[2,64]{1,0:T(2,128)S(1)}, f32[2,64]{1,0:T(2,128)S(1)}, u32[]{:S(2)}, u32[]{:S(2)}) %collective-permute-start.9) | collective-permute-done | bytes 544 | tf_op jit(solution)/shard_map/ppermute | solution.py:103
  66.0 3.3 collective-permute-start.10
  69.4 15.1 %collective-permute-done.10 = f32[64]{0:T(128)S(1)} collective-permute-done((f32[64]{0:T(128)S(1)}, f32[64]{0:T(128)S(1)}, u32[]{:S(2)}, u32[]{:S(2)}) %collective-permute-start.10) | collective-permute-done | bytes 288 | tf_op jit(solution)/shard_map/ppermute | solution.py:103
  85.7 1.3 copy-done.9
  87.0 6.2 %memory_forward.1.rows = bf16[16,128,768]{2,1,0:T(8,128)(2,1)} custom-call(s32[4]{0:T(128)S(1)} %get-tuple-element.470.facts, bf16[16,128,768]{2,1,0:T(8,128)(2,1)S(1)} %all-to-all-done.rows, f32[8,768]{1,0:T(8,128)S(1)} %maximum_maximum_fusion.stats, bf16[768,768]{1,0:T(8,128)(2,1)S(1)} %copy-done.9), custom_call_target="tpu_custom_call" | custom-call | flops 10000000000 | bytes 10000000 | tf_op jit(solution)/shard_map/memory_forward/pallas_call | solution.py:480
  93.3 14.0 %cross_forward.2 = (bf16[16,128,768]{2,1,0:T(8,128)(2,1)S(1)}, f32[8,512]{1,0:T(8,128)S(1)}, f32[8,512]{1,0:T(8,128)S(1)}, f32[384,512]{1,0:T(8,128)S(1)}) custom-call(s32[4]{0:T(128)S(1)} %get-tuple-element.470.facts, bf16[6,128,512]{2,1,0:T(8,128)(2,1)S(1)} %copy-done.25, bf16[16,128,768]{2,1,0:T(8,128)(2,1)} %memory_forward.1.rows, ...), custom_call_target="tpu_custom_call" | custom-call | flops 10000000000 | bytes 10000000 | tf_op jit(solution)/shard_map/cross_forward/pallas_call | solution.py:655
  107.3 12.0 %cross_forward.3 = (bf16[16,128,768]{2,1,0:T(8,128)(2,1)S(1)}, f32[8,512]{1,0:T(8,128)S(1)}, f32[8,512]{1,0:T(8,128)S(1)}, f32[384,512]{1,0:T(8,128)S(1)}) custom-call(s32[4]{0:T(128)S(1)} %get-tuple-element.411.facts, bf16[6,128,512]{2,1,0:T(8,128)(2,1)S(1)} %copy-done.25, bf16[16,128,768]{2,1,0:T(8,128)(2,1)S(1)} %collective-permute-done.11.rows, ...), custom_call_target="tpu_custom_call" | custom-call | flops 10000000000 | bytes 10000000 | tf_op jit(solution)/shard_map/cross_forward/pallas_call | solution.py:655
  120.6 3.0 collective-permute-done.12.came
  123.7 5.7 %feed_forward.1 = (f32[512,768]{1,0:T(8,128)S(1)}, bf16[512,768]{1,0:T(8,128)(2,1)S(1)}, bf16[512,1536]{1,0:T(8,128)(2,1)S(1)}, bf16[512,1536]{1,0:T(8,128)(2,1)S(1)}, f32[512,768]{1,0:T(8,128)S(1)}) custom-call(f32[512,768]{1,0:T(8,128)S(1)} %copy-done.63, f32[512,768]{1,0:T(8,128)S(1)} %get-tuple-element.420.own, ...), custom_call_target="tpu_custom_call" | custom-call | flops 10000000000 | bytes 10000000 | tf_op jit(solution)/shard_map/feed_forward/pallas_call | solution.py:748
  129.9 3.1 product.1
  133.0 2.4 feed_close.1
  135.4 3.3 feed_weights.1
  139.5 3.0 collective-permute-start.16
  142.6 24.0 %cross_backward.2 = (bf16[16,128,768]{2,1,0:T(8,128)(2,1)}, bf16[16,128,768]{2,1,0:T(8,128)(2,1)S(1)}, f32[384,512]{1,0:T(8,128)}) custom-call(s32[4]{0:T(128)S(1)} %get-tuple-element.411.facts, bf16[6,512,128]{2,1,0:T(8,128)(2,1)S(1)} %copy-done.23, bf16[6,128,512]{2,1,0:T(8,128)(2,1)S(1)} %copy-done.25, bf16[6,512,128]{2,1,0:T(8,128)(2,1)S(1)} %get-tuple-element.439.grad, ...), custom_call_target="tpu_custom_call" | custom-call | flops 10000000000 | bytes 10000000 | tf_op jit(solution)/shard_map/cross_backward/pallas_call | solution.py:918
  167.7 1.2 collective-permute-start.18
  168.9 2.8 collective-permute-start.19
  171.6 23.9 %cross_backward.3 = (bf16[16,128,768]{2,1,0:T(8,128)(2,1)}, f32[16,128,768]{2,1,0:T(8,128)S(1)}, f32[384,512]{1,0:T(8,128)}) custom-call(s32[4]{0:T(128)S(1)} %get-tuple-element.470.facts, bf16[6,512,128]{2,1,0:T(8,128)(2,1)S(1)} %copy-done.23, bf16[6,128,512]{2,1,0:T(8,128)(2,1)S(1)} %copy-done.25, bf16[6,512,128]{2,1,0:T(8,128)(2,1)S(1)} %get-tuple-element.439.grad, ...), custom_call_target="tpu_custom_call" | custom-call | flops 10000000000 | bytes 10000000 | tf_op jit(solution)/shard_map/cross_backward/pallas_call | solution.py:918
  196.0 3.0 collective-permute-start.23
  199.0 9.8 %memory_backward.1 = (bf16[16,128,768]{2,1,0:T(8,128)(2,1)}, bf16[16,128,768]{2,1,0:T(8,128)(2,1)}, bf16[16,128,768]{2,1,0:T(8,128)(2,1)}, f32[8,768]{1,0:T(8,128)}, f32[8,128]{1,0:T(8,128)S(1)}) custom-call(s32[4]{0:T(128)S(1)} %get-tuple-element.470.facts, bf16[16,128,768]{2,1,0:T(8,128)(2,1)S(1)} %all-to-all-done.rows, ...), custom_call_target="tpu_custom_call" | custom-call | flops 10000000000 | bytes 10000000 | tf_op jit(solution)/shard_map/memory_backward/pallas_call | solution.py:541
  210.2 4.3 %all-to-all-start.1 = ((bf16[16,128,768]{2,1,0:T(8,128)(2,1)}), bf16[16,128,768]{2,1,0:T(8,128)(2,1)S(1)}, u32[]{:S(2)}, u32[]{:S(2)}) async-start(bf16[16,128,768]{2,1,0:T(8,128)(2,1)} %get-tuple-element.530), calls=%async_computation.1 | async-start | bytes 6291456 | tf_op jit(solution)/shard_map/all_to_all | solution.py:1553
  220.9 1.9 collective-permute-start.26
  224.3 21.1 %conditional.2 = (f32[512,768]{1,0:T(8,128)}, f32[8,768]{1,0:T(8,128)S(1)}, f32[512,768]{1,0:T(8,128)}, f32[512,768]{1,0:T(8,128)}, f32[16,8,128]{2,1,0:T(8,128)...) conditional(s32[]{:T(128)} %bitcast.6, () %tuple.90, (f32[384,512]{1,0:T(8,128)S(1)}, ...), branch_computations={%region_2.3_spmd, %region_3.4_spmd} | conditional | flops 30000017408 | bytes 42687572 | solution.py:1556
  225.6 3.0 collective-permute-done.came
  228.6 9.7 %self_backward.1 = (f32[512,768]{1,0:T(8,128)}, bf16[512,768]{1,0:T(8,128)(2,1)S(1)}, f32[8,768]{1,0:T(8,128)S(1)}, bf16[512,1152]{1,0:T(8,128)(2,1)S(1)}, f32[512,768]{1,0:T(8,128)}) custom-call(s32[1]{0:T(128)} %get-tuple-element.73.facts, f32[512,768]{1,0:T(8,128)S(1)} %get-tuple-element.74.values, f32[512,768]{1,0:T(8,128)S(1)} %get-tuple-element.78.own, ...), custom_call_target="tpu_custom_call" | custom-call | flops 10000000000 | bytes 10000000 | tf_op jit(solution)/shard_map/cond/branch_1_fun/self_backward/pallas_call | solution.py:1258
  238.9 2.9 collective-permute-done.2
  241.9 3.3 side_weights.1
  246.0 18.8 %conditional.3 = (f32[6,8,128]{2,1,0:T(8,128)S(1)}, f32[1,512,768]{2,1,0:T(8,128)}, bf16[1,512,768]{2,1,0:T(8,128)(2,1)}, bf16[4,2,2,48,1152]{4,3,2,1,0:T(8,128)(2,1)S(1)}) conditional(s32[]{:T(128)} %bitcast.6, () %tuple.70, (s32[18]{0:T(128)S(1)}, bf16[16,128,768]{2,1,0:T(8,128)(2,1)}, bf16[16,128,768]{2,1,0:T(8,128)(2,1)}, ...), branch_computations={%region_4.5_spmd, %region_5.6_spmd} | conditional | flops 20004429824 | bytes 50652696 | solution.py:1556
  246.1 12.5 %memory_weights.1 = (bf16[768,768]{1,0:T(8,128)(2,1)S(1)}, f32[768,384]{1,0:T(8,128)S(1)}, bf16[768,384]{1,0:T(8,128)(2,1)S(1)}) custom-call(s32[18]{0:T(128)S(1)} %get-tuple-element.103.facts, bf16[16,128,768]{2,1,0:T(8,128)(2,1)} %get-tuple-element.104.refs_0_, bf16[16,128,768]{2,1,0:T(8,128)(2,1)} %get-tuple-element.105.refs_1_, ...), custom_call_target="tpu_custom_call" | custom-call | flops 10000000000 | bytes 10000000 | tf_op jit(solution)/shard_map/cond/branch_1_fun/memory_weights/pallas_call | solution.py:1021
  258.8 4.8 %input_back.1 = (f32[512,768]{1,0:T(8,128)}, bf16[512,768]{1,0:T(8,128)(2,1)}, f32[6,8,128]{2,1,0:T(8,128)S(1)}) custom-call(bf16[512,768]{1,0:T(8,128)(2,1)S(1)} %copy-done.57, f32[512,768]{1,0:T(8,128)} %get-tuple-element.101.own, f32[512,768]{1,0:T(8,128)} %get-tuple-element.111.came, f32[1,768]{1,0:T(1,128)S(1)} %broadcast_in_dim.48.gain, ...), custom_call_target="tpu_custom_call" | custom-call | flops 10000000000 | bytes 10000000 | tf_op jit(solution)/shard_map/cond/branch_1_fun/input_back/pallas_call | solution.py:1299
  265.8 1.9 collective-permute-start.30
  269.7 1.5 collective-permute-start.28
  271.1 1.5 collective-permute-start.29
  272.6 2.4 collective-permute-start.25
  275.5 20.2 %collective-permute-done.32 = f32[16,8,128]{2,1,0:T(8,128)S(1)} collective-permute-done((f32[16,8,128]{2,1,0:T(8,128)S(1)}, f32[16,8,128]{2,1,0:T(8,128)S(1)}, u32[]{:S(2)}, u32[]{:S(2)}) %collective-permute-start.32) | collective-permute-done | bytes 65568 | tf_op jit(solution)/shard_map/ppermute | solution.py:1548
  297.0 2.6 collective-permute-done.31
  300.5 3.0 merge_sums.11
  303.5 5.1 %collective-permute-start.35 = (bf16[4,48,1152]{2,1,0:T(8,128)(2,1)S(1)}, bf16[4,48,1152]{2,1,0:T(8,128)(2,1)S(1)}, u32[]{:S(2)}, u32[]{:S(2)}) collective-permute-start(bf16[4,48,1152]{2,1,0:T(8,128)(2,1)S(1)} %get-tuple-element.548), channel_id=1, source_target_pairs={{0,8},{2,10},{4,12},{6,14},{8,0},{10,2},{12,4},{14,6},{16,24},{18,... | collective-permute-start | bytes 1327112 | tf_op jit(solution)/shard_map/ppermute | solution.py:220
  308.6 1.5 collective-permute-start.33
  310.1 1.5 collective-permute-start.34
  312.1 7.0 %collective-permute-done.37 = f32[16,8,128]{2,1,0:T(8,128)S(1)} collective-permute-done((f32[16,8,128]{2,1,0:T(8,128)S(1)}, f32[16,8,128]{2,1,0:T(8,128)S(1)}, u32[]{:S(2)}, u32[]{:S(2)}) %collective-permute-start.37) | collective-permute-done | bytes 65568 | tf_op jit(solution)/shard_map/ppermute | solution.py:1548
  319.6 1.5 collective-permute-start.36
  321.1 2.4 collective-permute-done.38
  323.9 3.0 collective-permute-start.43
  326.9 1.2 collective-permute-start.39
  330.4 2.9 moved_rows.1.refs_1_
  333.4 1.7 copy-done.19
  335.2 1.8 collective-permute-start.44
  337.0 1.2 collective-permute-start.45
  338.2 1.8 collective-permute-start.46
  340.0 1.2 collective-permute-start.47
  341.1 7.7 %spread_docs.1 = f32[16,128,768]{2,1,0:T(8,128)} custom-call(s32[16]{0:T(128)S(1)} %copy-done.4, bf16[16,128,768]{2,1,0:T(8,128)(2,1)S(1)} %all-to-all-done.1.refs_0_, bf16[16,128,768]{2,1,0:T(8,128)(2,1)} %copy-done.19), custom_call_target="tpu_custom_call" | custom-call | flops 10000000000 | bytes 10000000 | tf_op jit(solution)/shard_map/spread_docs/pallas_call | solution.py:409
  350.6 1.9 assemble.1
  (285 shorter events, 34.4 us)
Async XLA Ops:
  5.6 80.1 %all-to-all-start = ((bf16[16,128,768]{2,1,0:T(8,128)(2,1)}), bf16[16,128,768]{2,1,0:T(8,128)(2,1)S(1)}, u32[]{:S(2)}, u32[]{:S(2)}) async-start(bf16[16,128,768]{2,1,0:T(8,128)(2,1)} %gather_docs.1), calls=%async_computation | async-start | bytes 6291456 | tf_op jit(solution)/shard_map/all_to_all | solution.py:1425
  23.5 10.0 %collective-permute-start.6 = (f32[512,768]{1,0:T(8,128)}, f32[512,768]{1,0:T(8,128)}, u32[]{:S(2)}, u32[]{:S(2)}) collective-permute-start(f32[512,768]{1,0:T(8,128)} %get-tuple-element.382.own), channel_id=1, source_target_pairs={{0,1},{1,0},{2,3},{3,2},{4,5},{5,4},{6,7},{7,6},{8,9},{9,8},{10,11... | collective-permute-start | bytes 4718600 | tf_op jit(solution)/shard_map/ppermute | solution.py:59
  28.4 5.1 %collective-permute-start.5 = (f32[16,64]{1,0:T(8,128)S(1)}, f32[16,64]{1,0:T(8,128)S(1)}, u32[]{:S(2)}, u32[]{:S(2)}) collective-permute-start(f32[16,64]{1,0:T(8,128)S(1)} %gather_fusion), channel_id=1, source_target_pairs={{0,1},{1,0},{2,3},{3,2},{4,5},{5,4},{6,7},{7,6},{8,9},{9,8},{10,11... | collective-permute-start | bytes 12296 | tf_op jit(solution)/shard_map/ppermute | solution.py:59
  33.5 6.0 %collective-permute-start.7 = (f32[2,2,2,64]{3,2,1,0:T(2,128)S(1)}, f32[2,2,2,64]{3,2,1,0:T(2,128)S(1)}, u32[]{:S(2)}, u32[]{:S(2)}) collective-permute-start(f32[2,2,2,64]{3,2,1,0:T(2,128)S(1)} %bitcast.83), channel_id=1, source_target_pairs={{0,2},{2,0},{4,6},{6,4},{8,10},{10,8},{12,14},{14,12},{16,18},{18,... | collective-permute-start | bytes 6152 | tf_op jit(solution)/shard_map/ppermute | solution.py:103
  39.6 8.3 %collective-permute-start.8 = (f32[2,2,64]{2,1,0:T(2,128)S(1)}, f32[2,2,64]{2,1,0:T(2,128)S(1)}, u32[]{:S(2)}, u32[]{:S(2)}) collective-permute-start(f32[2,2,64]{2,1,0:T(2,128)S(1)} %bitcast.85), channel_id=1, source_target_pairs={{0,4},{2,6},{4,0},{6,2},{8,12},{10,14},{12,8},{14,10},{16,20},{18,... | collective-permute-start | bytes 3080 | tf_op jit(solution)/shard_map/ppermute | solution.py:103
  47.8 18.1 %collective-permute-start.9 = (f32[2,64]{1,0:T(2,128)S(1)}, f32[2,64]{1,0:T(2,128)S(1)}, u32[]{:S(2)}, u32[]{:S(2)}) collective-permute-start(f32[2,64]{1,0:T(2,128)S(1)} %bitcast.86), channel_id=1, source_target_pairs={{0,8},{2,10},{4,12},{6,14},{8,0},{10,2},{12,4},{14,6},{16,24},{18,... | collective-permute-start | bytes 1544 | tf_op jit(solution)/shard_map/ppermute | solution.py:103
  66.0 18.6 %collective-permute-start.10 = (f32[64]{0:T(128)S(1)}, f32[64]{0:T(128)S(1)}, u32[]{:S(2)}, u32[]{:S(2)}) collective-permute-start(f32[64]{0:T(128)S(1)} %fusion.17), channel_id=1, source_target_pairs={{0,16},{2,18},{4,20},{6,22},{8,24},{10,26},{12,28},{14,30},{16,0},... | collective-permute-start | bytes 776 | tf_op jit(solution)/shard_map/ppermute | solution.py:103
  93.2 14.1 %collective-permute-start.11 = (bf16[16,128,768]{2,1,0:T(8,128)(2,1)}, bf16[16,128,768]{2,1,0:T(8,128)(2,1)S(1)}, u32[]{:S(2)}, u32[]{:S(2)}) collective-permute-start(bf16[16,128,768]{2,1,0:T(8,128)(2,1)} %memory_forward.1.rows), channel_id=1, source_target_pairs={{0,1},{1,0},{2,3},{3,2},{4,5},{5,4},{6,7},{7,6},{8,9},{9,8},{10,11... | collective-permute-start | bytes 9437192 | tf_op jit(solution)/shard_map/ppermute | solution.py:59
  107.3 12.0 %copy-start.54 = (bf16[16,128,768]{2,1,0:T(8,128)(2,1)}, bf16[16,128,768]{2,1,0:T(8,128)(2,1)S(1)}, u32[]{:S(2)}) copy-start(bf16[16,128,768]{2,1,0:T(8,128)(2,1)S(1)} %collective-permute-done.11.rows) | copy-start | bytes 9437188
  107.3 12.0 %copy-start.13 = (bf16[384,768]{1,0:T(8,128)(2,1)S(1)}, bf16[384,768]{1,0:T(8,128)(2,1)}, u32[]{:S(2)}) copy-start(bf16[384,768]{1,0:T(8,128)(2,1)} %weight.10) | copy-start | bytes 1769476
  120.1 3.6 %collective-permute-start.12 = (f32[512,768]{1,0:T(8,128)S(1)}, f32[512,768]{1,0:T(8,128)S(1)}, u32[]{:S(2)}, u32[]{:S(2)}) collective-permute-start(f32[512,768]{1,0:T(8,128)S(1)} %get-tuple-element.420.own), channel_id=1, source_target_pairs={{0,1},{1,0},{2,3},{3,2},{4,5},{5,4},{6,7},{7,6},{8,9},{9,8},{10,11... | collective-permute-start | bytes 4718600 | tf_op jit(solution)/shard_map/ppermute | solution.py:59
  129.4 3.6 %collective-permute-start.13 = (f32[512,768]{1,0:T(8,128)S(1)}, f32[512,768]{1,0:T(8,128)S(1)}, u32[]{:S(2)}, u32[]{:S(2)}) collective-permute-start(f32[512,768]{1,0:T(8,128)S(1)} %get-tuple-element.424.own), channel_id=1, source_target_pairs={{0,1},{1,0},{2,3},{3,2},{4,5},{5,4},{6,7},{7,6},{8,9},{9,8},{10,11... | collective-permute-start | bytes 4718600 | tf_op jit(solution)/shard_map/ppermute | solution.py:59
  138.9 27.7 %collective-permute-start.14 = (bf16[8,48,1152]{2,1,0:T(8,128)(2,1)S(1)}, bf16[8,48,1152]{2,1,0:T(8,128)(2,1)S(1)}, u32[]{:S(2)}, u32[]{:S(2)}) collective-permute-start(bf16[8,48,1152]{2,1,0:T(8,128)(2,1)S(1)} %bitcast.78), channel_id=1, source_target_pairs={{0,8},{2,10},{4,12},{6,14},{8,0},{10,2},{12,4},{14,6},{16,24},{18,... | collective-permute-start | bytes 2654216 | tf_op jit(solution)/shard_map/ppermute | solution.py:220
  139.0 27.6 %collective-permute-start.15 = (bf16[8,48,1152]{2,1,0:T(8,128)(2,1)S(1)}, bf16[8,48,1152]{2,1,0:T(8,128)(2,1)S(1)}, u32[]{:S(2)}, u32[]{:S(2)}) collective-permute-start(bf16[8,48,1152]{2,1,0:T(8,128)(2,1)S(1)} %dynamic-slice_bitcast_fusion), channel_id=1, source_target_pairs={{0,2},{2,0},{4,6},{6,4},{8,10},{10,8},{12,14},{14,12},{16,18},{18,... | collective-permute-start | bytes 2654216 | tf_op jit(solution)/shard_map/ppermute | solution.py:220
  139.5 27.0 %collective-permute-start.16 = (bf16[8,48,1152]{2,1,0:T(8,128)(2,1)S(1)}, bf16[8,48,1152]{2,1,0:T(8,128)(2,1)S(1)}, u32[]{:S(2)}, u32[]{:S(2)}) collective-permute-start(bf16[8,48,1152]{2,1,0:T(8,128)(2,1)S(1)} %bitcast.77), channel_id=1, source_target_pairs={{0,4},{2,6},{4,0},{6,2},{8,12},{10,14},{12,8},{14,10},{16,20},{18,... | collective-permute-start | bytes 2654216 | tf_op jit(solution)/shard_map/ppermute | solution.py:220
  166.6 32.5 %collective-permute-start.20 = (bf16[16,128,768]{2,1,0:T(8,128)(2,1)S(1)}, bf16[16,128,768]{2,1,0:T(8,128)(2,1)S(1)}, u32[]{:S(2)}, u32[]{:S(2)}) collective-permute-start(bf16[16,128,768]{2,1,0:T(8,128)(2,1)S(1)} %get-tuple-element.472), channel_id=1, source_target_pairs={{0,1},{1,0},{2,3},{3,2},{4,5},{5,4},{6,7},{7,6},{8,9},{9,8},{10,11... | collective-permute-start | bytes 9437192 | tf_op jit(solution)/shard_map/ppermute | solution.py:59
  167.6 27.9 %collective-permute-start.17 = (bf16[4,48,1152]{2,1,0:T(8,128)(2,1)S(1)}, bf16[4,48,1152]{2,1,0:T(8,128)(2,1)S(1)}, u32[]{:S(2)}, u32[]{:S(2)}) collective-permute-start(bf16[4,48,1152]{2,1,0:T(8,128)(2,1)S(1)} %get-tuple-element.456), channel_id=1, source_target_pairs={{0,16},{2,18},{4,20},{6,22},{8,24},{10,26},{12,28},{14,30},{16,0},... | collective-permute-start | bytes 1327112 | tf_op jit(solution)/shard_map/ppermute | solution.py:220
  167.7 27.8 %collective-permute-start.18 = (bf16[4,48,1152]{2,1,0:T(8,128)(2,1)S(1)}, bf16[4,48,1152]{2,1,0:T(8,128)(2,1)S(1)}, u32[]{:S(2)}, u32[]{:S(2)}) collective-permute-start(bf16[4,48,1152]{2,1,0:T(8,128)(2,1)S(1)} %get-tuple-element.457), channel_id=1, source_target_pairs={{0,8},{2,10},{4,12},{6,14},{8,0},{10,2},{12,4},{14,6},{16,24},{18,... | collective-permute-start | bytes 1327112 | tf_op jit(solution)/shard_map/ppermute | solution.py:220
  168.9 26.6 %collective-permute-start.19 = (bf16[4,48,1152]{2,1,0:T(8,128)(2,1)S(1)}, bf16[4,48,1152]{2,1,0:T(8,128)(2,1)S(1)}, u32[]{:S(2)}, u32[]{:S(2)}) collective-permute-start(bf16[4,48,1152]{2,1,0:T(8,128)(2,1)S(1)} %get-tuple-element.458), channel_id=1, source_target_pairs={{0,2},{2,0},{4,6},{6,4},{8,10},{10,8},{12,14},{14,12},{16,18},{18,... | collective-permute-start | bytes 1327112 | tf_op jit(solution)/shard_map/ppermute | solution.py:220
  195.8 13.0 %copy-start.26 = (bf16[2,48,1152]{2,1,0:T(8,128)(2,1)}, bf16[2,48,1152]{2,1,0:T(8,128)(2,1)S(1)}, u32[]{:S(2)}) copy-start(bf16[2,48,1152]{2,1,0:T(8,128)(2,1)S(1)} %get-tuple-element.477.refs_0_) | copy-start | bytes 663556
  195.9 13.0 %copy-start.28 = (bf16[2,48,1152]{2,1,0:T(8,128)(2,1)}, bf16[2,48,1152]{2,1,0:T(8,128)(2,1)S(1)}, u32[]{:S(2)}) copy-start(bf16[2,48,1152]{2,1,0:T(8,128)(2,1)S(1)} %get-tuple-element.478.refs_1_) | copy-start | bytes 663556
  195.9 13.0 %copy-start.30 = (bf16[2,48,1152]{2,1,0:T(8,128)(2,1)}, bf16[2,48,1152]{2,1,0:T(8,128)(2,1)S(1)}, u32[]{:S(2)}) copy-start(bf16[2,48,1152]{2,1,0:T(8,128)(2,1)S(1)} %get-tuple-element.479.refs_2_) | copy-start | bytes 663556
  195.9 12.9 %collective-permute-start.21 = (bf16[2,48,1152]{2,1,0:T(8,128)(2,1)S(1)}, bf16[2,48,1152]{2,1,0:T(8,128)(2,1)S(1)}, u32[]{:S(2)}, u32[]{:S(2)}) collective-permute-start(bf16[2,48,1152]{2,1,0:T(8,128)(2,1)S(1)} %get-tuple-element.480), channel_id=1, source_target_pairs={{0,2},{2,0},{4,6},{6,4},{8,10},{10,8},{12,14},{14,12},{16,18},{18,... | collective-permute-start | bytes 663560 | tf_op jit(solution)/shard_map/ppermute | solution.py:220
  196.0 12.9 %collective-permute-start.22 = (bf16[2,48,1152]{2,1,0:T(8,128)(2,1)S(1)}, bf16[2,48,1152]{2,1,0:T(8,128)(2,1)S(1)}, u32[]{:S(2)}, u32[]{:S(2)}) collective-permute-start(bf16[2,48,1152]{2,1,0:T(8,128)(2,1)S(1)} %get-tuple-element.481), channel_id=1, source_target_pairs={{0,16},{2,18},{4,20},{6,22},{8,24},{10,26},{12,28},{14,30},{16,0},... | collective-permute-start | bytes 663560 | tf_op jit(solution)/shard_map/ppermute | solution.py:220
  196.0 13.5 %collective-permute-start.23 = (bf16[2,48,1152]{2,1,0:T(8,128)(2,1)S(1)}, bf16[2,48,1152]{2,1,0:T(8,128)(2,1)S(1)}, u32[]{:S(2)}, u32[]{:S(2)}) collective-permute-start(bf16[2,48,1152]{2,1,0:T(8,128)(2,1)S(1)} %get-tuple-element.482), channel_id=1, source_target_pairs={{0,8},{2,10},{4,12},{6,14},{8,0},{10,2},{12,4},{14,6},{16,24},{18,... | collective-permute-start | bytes 663560 | tf_op jit(solution)/shard_map/ppermute | solution.py:220
  210.2 89.4 %all-to-all-start.1 = ((bf16[16,128,768]{2,1,0:T(8,128)(2,1)}), bf16[16,128,768]{2,1,0:T(8,128)(2,1)S(1)}, u32[]{:S(2)}, u32[]{:S(2)}) async-start(bf16[16,128,768]{2,1,0:T(8,128)(2,1)} %get-tuple-element.530), calls=%async_computation.1 | async-start | bytes 6291456 | tf_op jit(solution)/shard_map/all_to_all | solution.py:1553
  214.6 30.9 %collective-permute-start.24 = (f32[512,768]{1,0:T(8,128)}, f32[512,768]{1,0:T(8,128)}, u32[]{:S(2)}, u32[]{:S(2)}) collective-permute-start(f32[512,768]{1,0:T(8,128)} %product.1), channel_id=1, source_target_pairs={{0,1},{1,0},{2,3},{3,2},{4,5},{5,4},{6,7},{7,6},{8,9},{9,8},{10,11... | collective-permute-start | bytes 4718600 | tf_op jit(solution)/shard_map/ppermute | solution.py:59
  220.9 48.8 %collective-permute-start.26 = (bf16[1,48,1152]{2,1,0:T(8,128)(2,1)}, bf16[1,48,1152]{2,1,0:T(8,128)(2,1)S(1)}, u32[]{:S(2)}, u32[]{:S(2)}) collective-permute-start(bf16[1,48,1152]{2,1,0:T(8,128)(2,1)} %get-tuple-element.522), channel_id=1, source_target_pairs={{0,4},{2,6},{4,0},{6,2},{8,12},{10,14},{12,8},{14,10},{16,20},{18,... | collective-permute-start | bytes 331784 | tf_op jit(solution)/shard_map/ppermute | solution.py:220
  222.8 46.9 %collective-permute-start.27 = (bf16[1,48,1152]{2,1,0:T(8,128)(2,1)}, bf16[1,48,1152]{2,1,0:T(8,128)(2,1)S(1)}, u32[]{:S(2)}, u32[]{:S(2)}) collective-permute-start(bf16[1,48,1152]{2,1,0:T(8,128)(2,1)} %get-tuple-element.523), channel_id=1, source_target_pairs={{0,4},{2,6},{4,0},{6,2},{8,12},{10,14},{12,8},{14,10},{16,20},{18,... | collective-permute-start | bytes 331784 | tf_op jit(solution)/shard_map/ppermute | solution.py:220
  224.3 21.1 %copy-start.48 = (f32[768]{0:T(1024)S(1)}, f32[768]{0:T(1024)}, u32[]{:S(2)}) copy-start(f32[768]{0:T(1024)} %param.33) | copy-start | bytes 9220
  225.0 3.6 %collective-permute-start = (f32[512,768]{1,0:T(8,128)S(1)}, f32[512,768]{1,0:T(8,128)S(1)}, u32[]{:S(2)}, u32[]{:S(2)}) collective-permute-start(f32[512,768]{1,0:T(8,128)S(1)} %get-tuple-element.78.own), channel_id=1, source_target_pairs={{0,1},{1,0},{2,3},{3,2},{4,5},{5,4},{6,7},{7,6},{8,9},{9,8},{10,11... | collective-permute-start | bytes 4718600 | tf_op jit(solution)/shard_map/cond/branch_1_fun/ppermute | solution.py:59
  238.3 6.8 %collective-permute-start.1 = (f32[512,768]{1,0:T(8,128)}, f32[512,768]{1,0:T(8,128)}, u32[]{:S(2)}, u32[]{:S(2)}) collective-permute-start(f32[512,768]{1,0:T(8,128)} %get-tuple-element.635), channel_id=1, source_target_pairs={{0,1},{1,0},{2,3},{3,2},{4,5},{5,4},{6,7},{7,6},{8,9},{9,8},{10,11... | collective-permute-start | bytes 4718600 | tf_op jit(solution)/shard_map/cond/branch_1_fun/ppermute | solution.py:59
  238.7 3.0 collective-permute-start.2
  246.0 12.7 %copy-start.41 = (f32[512,768]{1,0:T(8,128)S(1)}, f32[512,768]{1,0:T(8,128)}, u32[]{:S(2)}) copy-start(f32[512,768]{1,0:T(8,128)} %get-tuple-element.113.grad_first) | copy-start | bytes 4718596 | tf_op jit(solution)/shard_map/cond
  246.1 12.7 %copy-start.56 = (f32[512,768]{1,0:T(8,128)S(1)}, f32[512,768]{1,0:T(8,128)}, u32[]{:S(2)}) copy-start(f32[512,768]{1,0:T(8,128)} %get-tuple-element.115.result_own) | copy-start | bytes 4718596 | tf_op jit(solution)/shard_map/cond
  246.1 12.7 %copy-start.57 = (bf16[512,768]{1,0:T(8,128)(2,1)S(1)}, bf16[512,768]{1,0:T(8,128)(2,1)}, u32[]{:S(2)}) copy-start(bf16[512,768]{1,0:T(8,128)(2,1)} %get-tuple-element.100.values) | copy-start | bytes 2359300 | tf_op jit(solution)/shard_map/cond
  246.1 12.7 %copy-start.62 = (f32[512,768]{1,0:T(8,128)S(1)}, f32[512,768]{1,0:T(8,128)}, u32[]{:S(2)}) copy-start(f32[512,768]{1,0:T(8,128)} %get-tuple-element.114.second) | copy-start | bytes 4718596 | tf_op jit(solution)/shard_map/cond
  246.1 12.7 %copy-start.72 = (f32[8,768]{1,0:T(8,128)S(1)}, f32[8,768]{1,0:T(8,128)}, u32[]{:S(2)}) copy-start(f32[8,768]{1,0:T(8,128)} %get-tuple-element.117.act_sums) | copy-start | bytes 73732 | tf_op jit(solution)/shard_map/cond
  246.1 12.7 %copy-start.73 = (f32[8,768]{1,0:T(8,128)S(1)}, f32[8,768]{1,0:T(8,128)}, u32[]{:S(2)}) copy-start(f32[8,768]{1,0:T(8,128)} %get-tuple-element.119.ffn_gain_grad) | copy-start | bytes 73732 | tf_op jit(solution)/shard_map/cond
  258.6 5.0 %collective-permute-start.3 = (bf16[768,384]{1,0:T(8,128)(2,1)S(1)}, bf16[768,384]{1,0:T(8,128)(2,1)S(1)}, u32[]{:S(2)}, u32[]{:S(2)}) collective-permute-start(bf16[768,384]{1,0:T(8,128)(2,1)S(1)} %get-tuple-element.121), channel_id=1, source_target_pairs={{0,1},{1,0},{2,3},{3,2},{4,5},{5,4},{6,7},{7,6},{8,9},{9,8},{10,11... | collective-permute-start | bytes 1769480 | tf_op jit(solution)/shard_map/cond/branch_1_fun/ppermute | solution.py:59
  263.6 1.2 collective-permute-start.4
  264.8 32.1 %copy-start.38 = (bf16[4,2,2,48,1152]{4,3,2,1,0:T(8,128)(2,1)}, bf16[4,2,2,48,1152]{4,3,2,1,0:T(8,128)(2,1)S(1)}, u32[]{:S(2)}) copy-start(bf16[4,2,2,48,1152]{4,3,2,1,0:T(8,128)(2,1)S(1)} %get-tuple-element.520.refs_3_) | copy-start | bytes 5308420
  265.8 33.8 %collective-permute-start.30 = (bf16[8,48,1152]{2,1,0:T(8,128)(2,1)}, bf16[8,48,1152]{2,1,0:T(8,128)(2,1)}, u32[]{:S(2)}, u32[]{:S(2)}) collective-permute-start(bf16[8,48,1152]{2,1,0:T(8,128)(2,1)} %bitcast.35), channel_id=1, source_target_pairs={{0,4},{2,6},{4,0},{6,2},{8,12},{10,14},{12,8},{14,10},{16,20},{18,... | collective-permute-start | bytes 2654216 | tf_op jit(solution)/shard_map/ppermute | solution.py:220
  269.7 29.9 %collective-permute-start.28 = (bf16[8,48,1024]{2,1,0:T(8,128)(2,1)}, bf16[8,48,1024]{2,1,0:T(8,128)(2,1)}, u32[]{:S(2)}, u32[]{:S(2)}) collective-permute-start(bf16[8,48,1024]{2,1,0:T(8,128)(2,1)} %dynamic-slice_bitcast_fusion.1), channel_id=1, source_target_pairs={{0,2},{2,0},{4,6},{6,4},{8,10},{10,8},{12,14},{14,12},{16,18},{18,... | collective-permute-start | bytes 2359304 | tf_op jit(solution)/shard_map/ppermute | solution.py:220
  271.1 28.5 %collective-permute-start.29 = (bf16[8,48,896]{2,1,0:T(8,128)(2,1)}, bf16[8,48,896]{2,1,0:T(8,128)(2,1)}, u32[]{:S(2)}, u32[]{:S(2)}) collective-permute-start(bf16[8,48,896]{2,1,0:T(8,128)(2,1)} %bitcast.34), channel_id=1, source_target_pairs={{0,8},{2,10},{4,12},{6,14},{8,0},{10,2},{12,4},{14,6},{16,24},{18,... | collective-permute-start | bytes 2064392 | tf_op jit(solution)/shard_map/ppermute | solution.py:220
  272.6 27.0 %collective-permute-start.25 = (bf16[1,48,1152]{2,1,0:T(8,128)(2,1)S(1)}, bf16[1,48,1152]{2,1,0:T(8,128)(2,1)}, u32[]{:S(2)}, u32[]{:S(2)}) collective-permute-start(bf16[1,48,1152]{2,1,0:T(8,128)(2,1)S(1)} %get-tuple-element.521), channel_id=1, source_target_pairs={{0,16},{2,18},{4,20},{6,22},{8,24},{10,26},{12,28},{14,30},{16,0},... | collective-permute-start | bytes 331784 | tf_op jit(solution)/shard_map/ppermute | solution.py:220
  275.0 20.8 %collective-permute-start.32 = (f32[16,8,128]{2,1,0:T(8,128)S(1)}, f32[16,8,128]{2,1,0:T(8,128)S(1)}, u32[]{:S(2)}, u32[]{:S(2)}) collective-permute-start(f32[16,8,128]{2,1,0:T(8,128)S(1)} %copy-done.44), channel_id=1, source_target_pairs={{0,2},{2,0},{4,6},{6,4},{8,10},{10,8},{12,14},{14,12},{16,18},{18,... | collective-permute-start | bytes 196616 | tf_op jit(solution)/shard_map/ppermute | solution.py:1548
  295.8 3.8 %collective-permute-start.31 = (f32[6,8,128]{2,1,0:T(8,128)S(1)}, f32[6,8,128]{2,1,0:T(8,128)S(1)}, u32[]{:S(2)}, u32[]{:S(2)}) collective-permute-start(f32[6,8,128]{2,1,0:T(8,128)S(1)} %get-tuple-element.531), channel_id=1, source_target_pairs={{0,2},{2,0},{4,6},{6,4},{8,10},{10,8},{12,14},{14,12},{16,18},{18,... | collective-permute-start | bytes 73736 | tf_op jit(solution)/shard_map/ppermute | solution.py:1548
  303.5 20.0 %collective-permute-start.35 = (bf16[4,48,1152]{2,1,0:T(8,128)(2,1)S(1)}, bf16[4,48,1152]{2,1,0:T(8,128)(2,1)S(1)}, u32[]{:S(2)}, u32[]{:S(2)}) collective-permute-start(bf16[4,48,1152]{2,1,0:T(8,128)(2,1)S(1)} %get-tuple-element.548), channel_id=1, source_target_pairs={{0,8},{2,10},{4,12},{6,14},{8,0},{10,2},{12,4},{14,6},{16,24},{18,... | collective-permute-start | bytes 1327112 | tf_op jit(solution)/shard_map/ppermute | solution.py:220
  308.6 14.9 %collective-permute-start.33 = (bf16[4,48,1024]{2,1,0:T(8,128)(2,1)S(1)}, bf16[4,48,1024]{2,1,0:T(8,128)(2,1)S(1)}, u32[]{:S(2)}, u32[]{:S(2)}) collective-permute-start(bf16[4,48,1024]{2,1,0:T(8,128)(2,1)S(1)} %get-tuple-element.546), channel_id=1, source_target_pairs={{0,4},{2,6},{4,0},{6,2},{8,12},{10,14},{12,8},{14,10},{16,20},{18,... | collective-permute-start | bytes 1179656 | tf_op jit(solution)/shard_map/ppermute | solution.py:220
  310.1 13.4 %collective-permute-start.34 = (bf16[4,48,896]{2,1,0:T(8,128)(2,1)S(1)}, bf16[4,48,896]{2,1,0:T(8,128)(2,1)S(1)}, u32[]{:S(2)}, u32[]{:S(2)}) collective-permute-start(bf16[4,48,896]{2,1,0:T(8,128)(2,1)S(1)} %get-tuple-element.547), channel_id=1, source_target_pairs={{0,2},{2,0},{4,6},{6,4},{8,10},{10,8},{12,14},{14,12},{16,18},{18,... | collective-permute-start | bytes 1032200 | tf_op jit(solution)/shard_map/ppermute | solution.py:220
  311.6 7.6 %collective-permute-start.37 = (f32[16,8,128]{2,1,0:T(8,128)S(1)}, f32[16,8,128]{2,1,0:T(8,128)S(1)}, u32[]{:S(2)}, u32[]{:S(2)}) collective-permute-start(f32[16,8,128]{2,1,0:T(8,128)S(1)} %copy-done.42), channel_id=1, source_target_pairs={{0,4},{2,6},{4,0},{6,2},{8,12},{10,14},{12,8},{14,10},{16,20},{18,... | collective-permute-start | bytes 196616 | tf_op jit(solution)/shard_map/ppermute | solution.py:1548
  319.1 4.3 %collective-permute-start.38 = (f32[16,8,128]{2,1,0:T(8,128)S(1)}, f32[16,8,128]{2,1,0:T(8,128)S(1)}, u32[]{:S(2)}, u32[]{:S(2)}) collective-permute-start(f32[16,8,128]{2,1,0:T(8,128)S(1)} %add.145), channel_id=1, source_target_pairs={{0,8},{2,10},{4,12},{6,14},{8,0},{10,2},{12,4},{14,6},{16,24},{18,... | collective-permute-start | bytes 196616 | tf_op jit(solution)/shard_map/ppermute | solution.py:1548
  319.6 3.9 %collective-permute-start.36 = (f32[6,8,128]{2,1,0:T(8,128)S(1)}, f32[6,8,128]{2,1,0:T(8,128)S(1)}, u32[]{:S(2)}, u32[]{:S(2)}) collective-permute-start(f32[6,8,128]{2,1,0:T(8,128)S(1)} %add.144), channel_id=1, source_target_pairs={{0,4},{2,6},{4,0},{6,2},{8,12},{10,14},{12,8},{14,10},{16,20},{18,... | collective-permute-start | bytes 73736 | tf_op jit(solution)/shard_map/ppermute | solution.py:1548
  323.9 6.5 %collective-permute-start.43 = (f32[16,8,128]{2,1,0:T(8,128)S(1)}, f32[16,8,128]{2,1,0:T(8,128)S(1)}, u32[]{:S(2)}, u32[]{:S(2)}) collective-permute-start(f32[16,8,128]{2,1,0:T(8,128)S(1)} %add.146), channel_id=1, source_target_pairs={{0,16},{2,18},{4,20},{6,22},{8,24},{10,26},{12,28},{14,30},{16,0},... | collective-permute-start | bytes 196616 | tf_op jit(solution)/shard_map/ppermute | solution.py:1548
  326.9 8.2 %collective-permute-start.39 = (bf16[2,48,1024]{2,1,0:T(8,128)(2,1)S(1)}, bf16[2,48,1024]{2,1,0:T(8,128)(2,1)S(1)}, u32[]{:S(2)}, u32[]{:S(2)}) collective-permute-start(bf16[2,48,1024]{2,1,0:T(8,128)(2,1)S(1)} %get-tuple-element.562), channel_id=1, source_target_pairs={{0,8},{2,10},{4,12},{6,14},{8,0},{10,2},{12,4},{14,6},{16,24},{18,... | collective-permute-start | bytes 589832 | tf_op jit(solution)/shard_map/ppermute | solution.py:220
  328.1 7.0 %collective-permute-start.40 = (bf16[2,48,896]{2,1,0:T(8,128)(2,1)S(1)}, bf16[2,48,896]{2,1,0:T(8,128)(2,1)S(1)}, u32[]{:S(2)}, u32[]{:S(2)}) collective-permute-start(bf16[2,48,896]{2,1,0:T(8,128)(2,1)S(1)} %get-tuple-element.563), channel_id=1, source_target_pairs={{0,4},{2,6},{4,0},{6,2},{8,12},{10,14},{12,8},{14,10},{16,20},{18,... | collective-permute-start | bytes 516104 | tf_op jit(solution)/shard_map/ppermute | solution.py:220
  328.8 6.3 %collective-permute-start.41 = (bf16[2,48,1152]{2,1,0:T(8,128)(2,1)S(1)}, bf16[2,48,1152]{2,1,0:T(8,128)(2,1)S(1)}, u32[]{:S(2)}, u32[]{:S(2)}) collective-permute-start(bf16[2,48,1152]{2,1,0:T(8,128)(2,1)S(1)} %get-tuple-element.564), channel_id=1, source_target_pairs={{0,2},{2,0},{4,6},{6,4},{8,10},{10,8},{12,14},{14,12},{16,18},{18,... | collective-permute-start | bytes 663560 | tf_op jit(solution)/shard_map/ppermute | solution.py:220
  329.7 5.4 %collective-permute-start.42 = (f32[6,8,128]{2,1,0:T(8,128)S(1)}, f32[6,8,128]{2,1,0:T(8,128)S(1)}, u32[]{:S(2)}, u32[]{:S(2)}) collective-permute-start(f32[6,8,128]{2,1,0:T(8,128)S(1)} %add.147), channel_id=1, source_target_pairs={{0,8},{2,10},{4,12},{6,14},{8,0},{10,2},{12,4},{14,6},{16,24},{18,... | collective-permute-start | bytes 73736 | tf_op jit(solution)/shard_map/ppermute | solution.py:1548
  335.2 13.7 %collective-permute-start.44 = (bf16[1,48,1024]{2,1,0:T(8,128)(2,1)S(1)}, bf16[1,48,1024]{2,1,0:T(8,128)(2,1)S(1)}, u32[]{:S(2)}, u32[]{:S(2)}) collective-permute-start(bf16[1,48,1024]{2,1,0:T(8,128)(2,1)S(1)} %get-tuple-element.575), channel_id=1, source_target_pairs={{0,16},{2,18},{4,20},{6,22},{8,24},{10,26},{12,28},{14,30},{16,0},... | collective-permute-start | bytes 294920 | tf_op jit(solution)/shard_map/ppermute | solution.py:220
  337.0 11.8 %collective-permute-start.45 = (bf16[1,48,896]{2,1,0:T(8,128)(2,1)S(1)}, bf16[1,48,896]{2,1,0:T(8,128)(2,1)S(1)}, u32[]{:S(2)}, u32[]{:S(2)}) collective-permute-start(bf16[1,48,896]{2,1,0:T(8,128)(2,1)S(1)} %get-tuple-element.576), channel_id=1, source_target_pairs={{0,16},{2,18},{4,20},{6,22},{8,24},{10,26},{12,28},{14,30},{16,0},... | collective-permute-start | bytes 258056 | tf_op jit(solution)/shard_map/ppermute | solution.py:220
  338.2 10.7 %collective-permute-start.46 = (bf16[1,48,1152]{2,1,0:T(8,128)(2,1)S(1)}, bf16[1,48,1152]{2,1,0:T(8,128)(2,1)S(1)}, u32[]{:S(2)}, u32[]{:S(2)}) collective-permute-start(bf16[1,48,1152]{2,1,0:T(8,128)(2,1)S(1)} %get-tuple-element.577), channel_id=1, source_target_pairs={{0,16},{2,18},{4,20},{6,22},{8,24},{10,26},{12,28},{14,30},{16,0},... | collective-permute-start | bytes 331784 | tf_op jit(solution)/shard_map/ppermute | solution.py:220
  340.0 8.9 %collective-permute-start.47 = (f32[6,8,128]{2,1,0:T(8,128)S(1)}, f32[6,8,128]{2,1,0:T(8,128)S(1)}, u32[]{:S(2)}, u32[]{:S(2)}) collective-permute-start(f32[6,8,128]{2,1,0:T(8,128)S(1)} %add.149), channel_id=1, source_target_pairs={{0,16},{2,18},{4,20},{6,22},{8,24},{10,26},{12,28},{14,30},{16,0},... | collective-permute-start | bytes 73736 | tf_op jit(solution)/shard_map/ppermute | solution.py:1548
  349.0 1.5 collective-permute-start.48
  (62 other events, 262.5 us)

commit v3 on v2

--- a/solution.py
+++ b/solution.py
@@ -1535,7 +1535,7 @@
     row_came = other_core(row_other)
     pair_own, row_own, query_own = cross_backward(
         facts_two, query_heads, query_heads_t, grad_heads, grad_heads_t, log_total, inner, pairs_own, pair_weight,
-        wide_type, 0, steps,
+        low_type, 0, steps,
     )
 
     facts_three, query_own = feed_sums.round((facts_own, query_own))

time: 358 us -> 358 us (level)
  transfers between devices with their start and end apart: 51 -> 51, of which waited for: 11 -> 12; matrix products, arithmetic and copies ran while one was open for 4% -> 4% of each run, Pallas kernels for 39% -> 39%
where the time goes in v3:
time: 358 us; the launch traced here: 352 us
  Pallas kernels  174 us (49%)
  waiting for transfers between devices  72 us (20%)
  starting transfers between devices  67.3 us (19%)
  local copies, waits for them, and re-layouts  23.5 us (7%)
  other arithmetic  5.49 us (2%)
  between operations  5.43 us (2%)
  matrix products  4.08 us (1%)
    pallas_call x2, Pallas kernels, cross_backward(): pl.pallas_call(partial(cross_backward_kernel, chips=chips, span=span, fir...  47.7 us
    ppermute x24, starting transfers between devices, leave(): lax.ppermute(leaving, 'dp', [(chip, chip ^ 1 << bit) for chip in range(ch...  33.4 us
    ppermute x8, waiting for transfers between devices, dp_hop(): lax.ppermute(value, 'dp', [(chip, chip ^ 1 << bit) for chip in range(chip...  31.7 us
    ppermute x4, waiting for transfers between devices, send(): lax.ppermute(sent, 'dp', [(chip, chip ^ 1 << order[0]) for chip in range(...  29.2 us
    pallas_call x2, Pallas kernels, cross_forward(): pl.pallas_call(partial(cross_forward_kernel, chips=chips, span=span), gri...  25.9 us
    unnamed x138, local copies, waits for them, and re-layouts  17.5 us
    pallas_call x1, Pallas kernels, memory_weights(): pl.pallas_call(partial(memory_weights_kernel, pieces=pieces, chips=chips,...  12.5 us
    ppermute x13, waiting for transfers between devices, other_core(): return lax.ppermute(values, 'mp', [(0, 1), (1, 0)])  10.2 us
  transfers between devices with their start and end apart: 51, of which 12 were waited for; matrix products, arithmetic and copies ran while one was open for 4% of the time, Pallas kernels for 39%

profile of v3, /device:TPU:0, one launch (start us, length us, event | category | flops | bytes accessed | tf_op | source)
XLA Modules:
  0.0 352.5 jit_solution(13260604991537047325)
XLA Ops:
  0.7 1.9 copy-done
  3.2 2.3 gather_docs.1
  5.6 8.3 %all-to-all-start = ((bf16[16,128,768]{2,1,0:T(8,128)(2,1)}), bf16[16,128,768]{2,1,0:T(8,128)(2,1)S(1)}, u32[]{:S(2)}, u32[]{:S(2)}) async-start(bf16[16,128,768]{2,1,0:T(8,128)(2,1)} %gather_docs.1), calls=%async_computation | async-start | bytes 6291456 | tf_op jit(solution)/shard_map/all_to_all | solution.py:1425
  14.5 9.0 %self_forward.1 = (bf16[512,768]{1,0:T(8,128)(2,1)}, bf16[512,1152]{1,0:T(8,128)(2,1)}, bf16[512,384]{1,0:T(8,128)(2,1)}, f32[8,512]{1,0:T(8,128)}, f32[512,768]{1,0:T(8,128)}) custom-call(s32[1]{0:T(128)} %dynamic_slice.62.facts, bf16[512,768]{1,0:T(8,128)(2,1)} %bitcast.90, f32[1,768]{1,0:T(1,128)S(1)} %broadcast_in_dim.82.gain, ...), custom_call_target="tpu_custom_call" | custom-call | flops 10000000000 | bytes 10000000 | tf_op jit(solution)/shard_map/self_forward/pallas_call | solution.py:1147
  23.6 3.3 select_reduce_fusion
  33.5 2.0 collective-permute-start.7
  35.5 4.0 %query_forward.1 = (f32[512,768]{1,0:T(8,128)}, bf16[512,768]{1,0:T(8,128)(2,1)}, bf16[6,512,128]{2,1,0:T(8,128)(2,1)S(1)}, bf16[6,128,512]{2,1,0:T(8,128)(2,1)S(1)}) custom-call(bf16[512,768]{1,0:T(8,128)(2,1)} %bitcast.91, f32[512,768]{1,0:T(8,128)} %get-tuple-element.382.own, f32[512,768]{1,0:T(8,128)} %collective-permute-done.6.came, ...), custom_call_target="tpu_custom_call" | custom-call | flops 10000000000 | bytes 10000000 | tf_op jit(solution)/shard_map/query_forward/pallas_call | solution.py:1191
  39.6 1.5 collective-permute-start.8
  41.1 5.3 %prepare_weights.1.key_weight.value_weight = bf16[768,1536]{1,0:T(8,128)(2,1)S(1)} custom-call(bf16[768,2,768]{2,1,0:T(2,128)(2,1)S(1)} %copy-done.5), custom_call_target="tpu_custom_call" | custom-call | flops 10000000000 | bytes 10000000 | tf_op jit(solution)/shard_map/prepare_weights/pallas_call | solution.py:319
  46.4 1.4 copy-done.20
  47.8 1.5 collective-permute-start.9
  49.4 2.6 convolution_convert_fusion.grad_active
  51.9 14.0 %collective-permute-done.9 = f32[2,64]{1,0:T(2,128)S(1)} collective-permute-done((f32[2,64]{1,0:T(2,128)S(1)}, f32[2,64]{1,0:T(2,128)S(1)}, u32[]{:S(2)}, u32[]{:S(2)}) %collective-permute-start.9) | collective-permute-done | bytes 544 | tf_op jit(solution)/shard_map/ppermute | solution.py:103
  66.0 3.3 collective-permute-start.10
  69.4 15.1 %collective-permute-done.10 = f32[64]{0:T(128)S(1)} collective-permute-done((f32[64]{0:T(128)S(1)}, f32[64]{0:T(128)S(1)}, u32[]{:S(2)}, u32[]{:S(2)}) %collective-permute-start.10) | collective-permute-done | bytes 288 | tf_op jit(solution)/shard_map/ppermute | solution.py:103
  85.7 1.3 copy-done.9
  87.0 6.2 %memory_forward.1.rows = bf16[16,128,768]{2,1,0:T(8,128)(2,1)} custom-call(s32[4]{0:T(128)S(1)} %get-tuple-element.470.facts, bf16[16,128,768]{2,1,0:T(8,128)(2,1)S(1)} %all-to-all-done.rows, f32[8,768]{1,0:T(8,128)S(1)} %maximum_maximum_fusion.stats, bf16[768,768]{1,0:T(8,128)(2,1)S(1)} %copy-done.9), custom_call_target="tpu_custom_call" | custom-call | flops 10000000000 | bytes 10000000 | tf_op jit(solution)/shard_map/memory_forward/pallas_call | solution.py:480
  93.3 14.0 %cross_forward.2 = (bf16[16,128,768]{2,1,0:T(8,128)(2,1)S(1)}, f32[8,512]{1,0:T(8,128)S(1)}, f32[8,512]{1,0:T(8,128)S(1)}, f32[384,512]{1,0:T(8,128)S(1)}) custom-call(s32[4]{0:T(128)S(1)} %get-tuple-element.470.facts, bf16[6,128,512]{2,1,0:T(8,128)(2,1)S(1)} %copy-done.25, bf16[16,128,768]{2,1,0:T(8,128)(2,1)} %memory_forward.1.rows, ...), custom_call_target="tpu_custom_call" | custom-call | flops 10000000000 | bytes 10000000 | tf_op jit(solution)/shard_map/cross_forward/pallas_call | solution.py:655
  107.3 12.0 %cross_forward.3 = (bf16[16,128,768]{2,1,0:T(8,128)(2,1)S(1)}, f32[8,512]{1,0:T(8,128)S(1)}, f32[8,512]{1,0:T(8,128)S(1)}, f32[384,512]{1,0:T(8,128)S(1)}) custom-call(s32[4]{0:T(128)S(1)} %get-tuple-element.411.facts, bf16[6,128,512]{2,1,0:T(8,128)(2,1)S(1)} %copy-done.25, bf16[16,128,768]{2,1,0:T(8,128)(2,1)S(1)} %collective-permute-done.11.rows, ...), custom_call_target="tpu_custom_call" | custom-call | flops 10000000000 | bytes 10000000 | tf_op jit(solution)/shard_map/cross_forward/pallas_call | solution.py:655
  120.6 3.0 collective-permute-done.12.came
  123.7 5.7 %feed_forward.1 = (f32[512,768]{1,0:T(8,128)S(1)}, bf16[512,768]{1,0:T(8,128)(2,1)S(1)}, bf16[512,1536]{1,0:T(8,128)(2,1)S(1)}, bf16[512,1536]{1,0:T(8,128)(2,1)S(1)}, f32[512,768]{1,0:T(8,128)S(1)}) custom-call(f32[512,768]{1,0:T(8,128)S(1)} %copy-done.63, f32[512,768]{1,0:T(8,128)S(1)} %get-tuple-element.420.own, ...), custom_call_target="tpu_custom_call" | custom-call | flops 10000000000 | bytes 10000000 | tf_op jit(solution)/shard_map/feed_forward/pallas_call | solution.py:748
  129.9 3.1 product.1
  133.0 2.4 feed_close.1
  135.4 3.3 feed_weights.1
  139.1 3.0 collective-permute-start.16
  142.1 24.0 %cross_backward.2 = (bf16[16,128,768]{2,1,0:T(8,128)(2,1)}, bf16[16,128,768]{2,1,0:T(8,128)(2,1)S(1)}, f32[384,512]{1,0:T(8,128)}) custom-call(s32[4]{0:T(128)S(1)} %get-tuple-element.411.facts, bf16[6,512,128]{2,1,0:T(8,128)(2,1)S(1)} %copy-done.23, bf16[6,128,512]{2,1,0:T(8,128)(2,1)S(1)} %copy-done.25, bf16[6,512,128]{2,1,0:T(8,128)(2,1)S(1)} %get-tuple-element.439.grad, ...), custom_call_target="tpu_custom_call" | custom-call | flops 10000000000 | bytes 10000000 | tf_op jit(solution)/shard_map/cross_backward/pallas_call | solution.py:918
  167.3 3.0 collective-permute-start.19
  170.2 23.7 %cross_backward.3 = (bf16[16,128,768]{2,1,0:T(8,128)(2,1)}, bf16[16,128,768]{2,1,0:T(8,128)(2,1)S(1)}, f32[384,512]{1,0:T(8,128)}) custom-call(s32[4]{0:T(128)S(1)} %get-tuple-element.470.facts, bf16[6,512,128]{2,1,0:T(8,128)(2,1)S(1)} %copy-done.23, bf16[6,128,512]{2,1,0:T(8,128)(2,1)S(1)} %copy-done.25, bf16[6,512,128]{2,1,0:T(8,128)(2,1)S(1)} %get-tuple-element.439.grad, ...), custom_call_target="tpu_custom_call" | custom-call | flops 10000000000 | bytes 10000000 | tf_op jit(solution)/shard_map/cross_backward/pallas_call | solution.py:918
  195.0 1.9 collective-permute-start.22
  196.9 9.8 %memory_backward.1 = (bf16[16,128,768]{2,1,0:T(8,128)(2,1)}, bf16[16,128,768]{2,1,0:T(8,128)(2,1)}, bf16[16,128,768]{2,1,0:T(8,128)(2,1)}, f32[8,768]{1,0:T(8,128)}, f32[8,128]{1,0:T(8,128)S(1)}) custom-call(s32[4]{0:T(128)S(1)} %get-tuple-element.470.facts, bf16[16,128,768]{2,1,0:T(8,128)(2,1)S(1)} %all-to-all-done.rows, ...), custom_call_target="tpu_custom_call" | custom-call | flops 10000000000 | bytes 10000000 | tf_op jit(solution)/shard_map/memory_backward/pallas_call | solution.py:541
  209.0 5.2 %all-to-all-start.1 = ((bf16[16,128,768]{2,1,0:T(8,128)(2,1)}), bf16[16,128,768]{2,1,0:T(8,128)(2,1)S(1)}, u32[]{:S(2)}, u32[]{:S(2)}) async-start(bf16[16,128,768]{2,1,0:T(8,128)(2,1)} %get-tuple-element.530), calls=%async_computation.1 | async-start | bytes 6291456 | tf_op jit(solution)/shard_map/all_to_all | solution.py:1553
  220.5 1.9 collective-permute-start.26
  224.0 21.1 %conditional.2 = (f32[512,768]{1,0:T(8,128)}, f32[8,768]{1,0:T(8,128)S(1)}, f32[512,768]{1,0:T(8,128)}, f32[512,768]{1,0:T(8,128)}, f32[16,8,128]{2,1,0:T(8,128)...) conditional(s32[]{:T(128)} %bitcast.6, () %tuple.90, (f32[384,512]{1,0:T(8,128)S(1)}, ...), branch_computations={%region_2.3_spmd, %region_3.4_spmd} | conditional | flops 30000017408 | bytes 42687572 | solution.py:1556
  225.2 3.0 collective-permute-done.came
  228.2 9.7 %self_backward.1 = (f32[512,768]{1,0:T(8,128)}, bf16[512,768]{1,0:T(8,128)(2,1)S(1)}, f32[8,768]{1,0:T(8,128)S(1)}, bf16[512,1152]{1,0:T(8,128)(2,1)S(1)}, f32[512,768]{1,0:T(8,128)}) custom-call(s32[1]{0:T(128)} %get-tuple-element.73.facts, f32[512,768]{1,0:T(8,128)S(1)} %get-tuple-element.74.values, f32[512,768]{1,0:T(8,128)S(1)} %get-tuple-element.78.own, ...), custom_call_target="tpu_custom_call" | custom-call | flops 10000000000 | bytes 10000000 | tf_op jit(solution)/shard_map/cond/branch_1_fun/self_backward/pallas_call | solution.py:1258
  238.5 2.9 collective-permute-done.2
  241.5 3.3 side_weights.1
  245.7 18.8 %conditional.3 = (f32[6,8,128]{2,1,0:T(8,128)S(1)}, f32[1,512,768]{2,1,0:T(8,128)}, bf16[1,512,768]{2,1,0:T(8,128)(2,1)}, bf16[4,2,2,48,1152]{4,3,2,1,0:T(8,128)(2,1)S(1)}) conditional(s32[]{:T(128)} %bitcast.6, () %tuple.70, (s32[18]{0:T(128)S(1)}, bf16[16,128,768]{2,1,0:T(8,128)(2,1)}, bf16[16,128,768]{2,1,0:T(8,128)(2,1)}, ...), branch_computations={%region_4.5_spmd, %region_5.6_spmd} | conditional | flops 20004429824 | bytes 50652696 | solution.py:1556
  245.7 12.5 %memory_weights.1 = (bf16[768,768]{1,0:T(8,128)(2,1)S(1)}, f32[768,384]{1,0:T(8,128)S(1)}, bf16[768,384]{1,0:T(8,128)(2,1)S(1)}) custom-call(s32[18]{0:T(128)S(1)} %get-tuple-element.103.facts, bf16[16,128,768]{2,1,0:T(8,128)(2,1)} %get-tuple-element.104.refs_0_, bf16[16,128,768]{2,1,0:T(8,128)(2,1)} %get-tuple-element.105.refs_1_, ...), custom_call_target="tpu_custom_call" | custom-call | flops 10000000000 | bytes 10000000 | tf_op jit(solution)/shard_map/cond/branch_1_fun/memory_weights/pallas_call | solution.py:1021
  258.4 4.8 %input_back.1 = (f32[512,768]{1,0:T(8,128)}, bf16[512,768]{1,0:T(8,128)(2,1)}, f32[6,8,128]{2,1,0:T(8,128)S(1)}) custom-call(bf16[512,768]{1,0:T(8,128)(2,1)S(1)} %copy-done.57, f32[512,768]{1,0:T(8,128)} %get-tuple-element.101.own, f32[512,768]{1,0:T(8,128)} %get-tuple-element.111.came, f32[1,768]{1,0:T(1,128)S(1)} %broadcast_in_dim.48.gain, ...), custom_call_target="tpu_custom_call" | custom-call | flops 10000000000 | bytes 10000000 | tf_op jit(solution)/shard_map/cond/branch_1_fun/input_back/pallas_call | solution.py:1299
  264.4 1.0 constant_dynamic-slice_fusion
  265.5 1.9 collective-permute-start.30
  267.3 1.0 dynamic-slice_bitcast_fusion.1
  269.3 1.5 collective-permute-start.28
  270.8 1.5 collective-permute-start.29
  272.2 2.4 collective-permute-start.25
  275.2 19.7 %collective-permute-done.32 = f32[16,8,128]{2,1,0:T(8,128)S(1)} collective-permute-done((f32[16,8,128]{2,1,0:T(8,128)S(1)}, f32[16,8,128]{2,1,0:T(8,128)S(1)}, u32[]{:S(2)}, u32[]{:S(2)}) %collective-permute-start.32) | collective-permute-done | bytes 65568 | tf_op jit(solution)/shard_map/ppermute | solution.py:1548
  296.1 2.6 collective-permute-done.31
  299.6 3.0 merge_sums.11
  302.6 5.7 %collective-permute-start.35 = (bf16[4,48,1152]{2,1,0:T(8,128)(2,1)S(1)}, bf16[4,48,1152]{2,1,0:T(8,128)(2,1)S(1)}, u32[]{:S(2)}, u32[]{:S(2)}) collective-permute-start(bf16[4,48,1152]{2,1,0:T(8,128)(2,1)S(1)} %get-tuple-element.548), channel_id=1, source_target_pairs={{0,8},{2,10},{4,12},{6,14},{8,0},{10,2},{12,4},{14,6},{16,24},{18,... | collective-permute-start | bytes 1327112 | tf_op jit(solution)/shard_map/ppermute | solution.py:220
  308.3 1.5 collective-permute-start.33
  309.7 1.5 collective-permute-start.34
  311.7 7.0 %collective-permute-done.37 = f32[16,8,128]{2,1,0:T(8,128)S(1)} collective-permute-done((f32[16,8,128]{2,1,0:T(8,128)S(1)}, f32[16,8,128]{2,1,0:T(8,128)S(1)}, u32[]{:S(2)}, u32[]{:S(2)}) %collective-permute-start.37) | collective-permute-done | bytes 65568 | tf_op jit(solution)/shard_map/ppermute | solution.py:1548
  319.2 1.5 collective-permute-start.36
  320.7 2.4 collective-permute-done.38
  323.5 3.2 collective-permute-start.43
  326.7 1.2 collective-permute-start.39
  327.9 1.2 collective-permute-start.41
  330.0 2.9 moved_rows.1.refs_1_
  332.9 1.7 copy-done.19
  334.8 2.1 collective-permute-start.44
  337.8 2.0 collective-permute-start.46
  340.7 7.7 %spread_docs.1 = f32[16,128,768]{2,1,0:T(8,128)} custom-call(s32[16]{0:T(128)S(1)} %copy-done.4, bf16[16,128,768]{2,1,0:T(8,128)(2,1)S(1)} %all-to-all-done.1.refs_0_, bf16[16,128,768]{2,1,0:T(8,128)(2,1)} %copy-done.19), custom_call_target="tpu_custom_call" | custom-call | flops 10000000000 | bytes 10000000 | tf_op jit(solution)/shard_map/spread_docs/pallas_call | solution.py:409
  350.1 1.9 assemble.1
  (285 shorter events, 33.6 us)
Async XLA Ops:
  5.6 80.1 %all-to-all-start = ((bf16[16,128,768]{2,1,0:T(8,128)(2,1)}), bf16[16,128,768]{2,1,0:T(8,128)(2,1)S(1)}, u32[]{:S(2)}, u32[]{:S(2)}) async-start(bf16[16,128,768]{2,1,0:T(8,128)(2,1)} %gather_docs.1), calls=%async_computation | async-start | bytes 6291456 | tf_op jit(solution)/shard_map/all_to_all | solution.py:1425
  23.5 10.0 %collective-permute-start.6 = (f32[512,768]{1,0:T(8,128)}, f32[512,768]{1,0:T(8,128)}, u32[]{:S(2)}, u32[]{:S(2)}) collective-permute-start(f32[512,768]{1,0:T(8,128)} %get-tuple-element.382.own), channel_id=1, source_target_pairs={{0,1},{1,0},{2,3},{3,2},{4,5},{5,4},{6,7},{7,6},{8,9},{9,8},{10,11... | collective-permute-start | bytes 4718600 | tf_op jit(solution)/shard_map/ppermute | solution.py:59
  28.4 5.1 %collective-permute-start.5 = (f32[16,64]{1,0:T(8,128)S(1)}, f32[16,64]{1,0:T(8,128)S(1)}, u32[]{:S(2)}, u32[]{:S(2)}) collective-permute-start(f32[16,64]{1,0:T(8,128)S(1)} %gather_fusion), channel_id=1, source_target_pairs={{0,1},{1,0},{2,3},{3,2},{4,5},{5,4},{6,7},{7,6},{8,9},{9,8},{10,11... | collective-permute-start | bytes 12296 | tf_op jit(solution)/shard_map/ppermute | solution.py:59
  33.5 6.0 %collective-permute-start.7 = (f32[2,2,2,64]{3,2,1,0:T(2,128)S(1)}, f32[2,2,2,64]{3,2,1,0:T(2,128)S(1)}, u32[]{:S(2)}, u32[]{:S(2)}) collective-permute-start(f32[2,2,2,64]{3,2,1,0:T(2,128)S(1)} %bitcast.83), channel_id=1, source_target_pairs={{0,2},{2,0},{4,6},{6,4},{8,10},{10,8},{12,14},{14,12},{16,18},{18,... | collective-permute-start | bytes 6152 | tf_op jit(solution)/shard_map/ppermute | solution.py:103
  39.6 8.3 %collective-permute-start.8 = (f32[2,2,64]{2,1,0:T(2,128)S(1)}, f32[2,2,64]{2,1,0:T(2,128)S(1)}, u32[]{:S(2)}, u32[]{:S(2)}) collective-permute-start(f32[2,2,64]{2,1,0:T(2,128)S(1)} %bitcast.85), channel_id=1, source_target_pairs={{0,4},{2,6},{4,0},{6,2},{8,12},{10,14},{12,8},{14,10},{16,20},{18,... | collective-permute-start | bytes 3080 | tf_op jit(solution)/shard_map/ppermute | solution.py:103
  47.8 18.1 %collective-permute-start.9 = (f32[2,64]{1,0:T(2,128)S(1)}, f32[2,64]{1,0:T(2,128)S(1)}, u32[]{:S(2)}, u32[]{:S(2)}) collective-permute-start(f32[2,64]{1,0:T(2,128)S(1)} %bitcast.86), channel_id=1, source_target_pairs={{0,8},{2,10},{4,12},{6,14},{8,0},{10,2},{12,4},{14,6},{16,24},{18,... | collective-permute-start | bytes 1544 | tf_op jit(solution)/shard_map/ppermute | solution.py:103
  66.0 18.6 %collective-permute-start.10 = (f32[64]{0:T(128)S(1)}, f32[64]{0:T(128)S(1)}, u32[]{:S(2)}, u32[]{:S(2)}) collective-permute-start(f32[64]{0:T(128)S(1)} %fusion.17), channel_id=1, source_target_pairs={{0,16},{2,18},{4,20},{6,22},{8,24},{10,26},{12,28},{14,30},{16,0},... | collective-permute-start | bytes 776 | tf_op jit(solution)/shard_map/ppermute | solution.py:103
  93.2 14.1 %collective-permute-start.11 = (bf16[16,128,768]{2,1,0:T(8,128)(2,1)}, bf16[16,128,768]{2,1,0:T(8,128)(2,1)S(1)}, u32[]{:S(2)}, u32[]{:S(2)}) collective-permute-start(bf16[16,128,768]{2,1,0:T(8,128)(2,1)} %memory_forward.1.rows), channel_id=1, source_target_pairs={{0,1},{1,0},{2,3},{3,2},{4,5},{5,4},{6,7},{7,6},{8,9},{9,8},{10,11... | collective-permute-start | bytes 9437192 | tf_op jit(solution)/shard_map/ppermute | solution.py:59
  107.3 12.0 %copy-start.54 = (bf16[16,128,768]{2,1,0:T(8,128)(2,1)}, bf16[16,128,768]{2,1,0:T(8,128)(2,1)S(1)}, u32[]{:S(2)}) copy-start(bf16[16,128,768]{2,1,0:T(8,128)(2,1)S(1)} %collective-permute-done.11.rows) | copy-start | bytes 9437188
  107.3 12.0 %copy-start.13 = (bf16[384,768]{1,0:T(8,128)(2,1)S(1)}, bf16[384,768]{1,0:T(8,128)(2,1)}, u32[]{:S(2)}) copy-start(bf16[384,768]{1,0:T(8,128)(2,1)} %weight.10) | copy-start | bytes 1769476
  120.1 3.6 %collective-permute-start.12 = (f32[512,768]{1,0:T(8,128)S(1)}, f32[512,768]{1,0:T(8,128)S(1)}, u32[]{:S(2)}, u32[]{:S(2)}) collective-permute-start(f32[512,768]{1,0:T(8,128)S(1)} %get-tuple-element.420.own), channel_id=1, source_target_pairs={{0,1},{1,0},{2,3},{3,2},{4,5},{5,4},{6,7},{7,6},{8,9},{9,8},{10,11... | collective-permute-start | bytes 4718600 | tf_op jit(solution)/shard_map/ppermute | solution.py:59
  129.4 3.6 %collective-permute-start.13 = (f32[512,768]{1,0:T(8,128)S(1)}, f32[512,768]{1,0:T(8,128)S(1)}, u32[]{:S(2)}, u32[]{:S(2)}) collective-permute-start(f32[512,768]{1,0:T(8,128)S(1)} %get-tuple-element.424.own), channel_id=1, source_target_pairs={{0,1},{1,0},{2,3},{3,2},{4,5},{5,4},{6,7},{7,6},{8,9},{9,8},{10,11... | collective-permute-start | bytes 4718600 | tf_op jit(solution)/shard_map/ppermute | solution.py:59
  138.9 27.2 %collective-permute-start.14 = (bf16[8,48,1152]{2,1,0:T(8,128)(2,1)S(1)}, bf16[8,48,1152]{2,1,0:T(8,128)(2,1)S(1)}, u32[]{:S(2)}, u32[]{:S(2)}) collective-permute-start(bf16[8,48,1152]{2,1,0:T(8,128)(2,1)S(1)} %bitcast.78), channel_id=1, source_target_pairs={{0,8},{2,10},{4,12},{6,14},{8,0},{10,2},{12,4},{14,6},{16,24},{18,... | collective-permute-start | bytes 2654216 | tf_op jit(solution)/shard_map/ppermute | solution.py:220
  139.0 27.1 %collective-permute-start.15 = (bf16[8,48,1152]{2,1,0:T(8,128)(2,1)S(1)}, bf16[8,48,1152]{2,1,0:T(8,128)(2,1)S(1)}, u32[]{:S(2)}, u32[]{:S(2)}) collective-permute-start(bf16[8,48,1152]{2,1,0:T(8,128)(2,1)S(1)} %dynamic-slice_bitcast_fusion), channel_id=1, source_target_pairs={{0,2},{2,0},{4,6},{6,4},{8,10},{10,8},{12,14},{14,12},{16,18},{18,... | collective-permute-start | bytes 2654216 | tf_op jit(solution)/shard_map/ppermute | solution.py:220
  139.1 27.0 %collective-permute-start.16 = (bf16[8,48,1152]{2,1,0:T(8,128)(2,1)S(1)}, bf16[8,48,1152]{2,1,0:T(8,128)(2,1)S(1)}, u32[]{:S(2)}, u32[]{:S(2)}) collective-permute-start(bf16[8,48,1152]{2,1,0:T(8,128)(2,1)S(1)} %bitcast.77), channel_id=1, source_target_pairs={{0,4},{2,6},{4,0},{6,2},{8,12},{10,14},{12,8},{14,10},{16,20},{18,... | collective-permute-start | bytes 2654216 | tf_op jit(solution)/shard_map/ppermute | solution.py:220
  166.1 30.8 %collective-permute-start.20 = (bf16[16,128,768]{2,1,0:T(8,128)(2,1)S(1)}, bf16[16,128,768]{2,1,0:T(8,128)(2,1)S(1)}, u32[]{:S(2)}, u32[]{:S(2)}) collective-permute-start(bf16[16,128,768]{2,1,0:T(8,128)(2,1)S(1)} %get-tuple-element.472), channel_id=1, source_target_pairs={{0,1},{1,0},{2,3},{3,2},{4,5},{5,4},{6,7},{7,6},{8,9},{9,8},{10,11... | collective-permute-start | bytes 9437192 | tf_op jit(solution)/shard_map/ppermute | solution.py:59
  167.1 26.9 %collective-permute-start.17 = (bf16[4,48,1152]{2,1,0:T(8,128)(2,1)S(1)}, bf16[4,48,1152]{2,1,0:T(8,128)(2,1)S(1)}, u32[]{:S(2)}, u32[]{:S(2)}) collective-permute-start(bf16[4,48,1152]{2,1,0:T(8,128)(2,1)S(1)} %get-tuple-element.456), channel_id=1, source_target_pairs={{0,16},{2,18},{4,20},{6,22},{8,24},{10,26},{12,28},{14,30},{16,0},... | collective-permute-start | bytes 1327112 | tf_op jit(solution)/shard_map/ppermute | solution.py:220
  167.2 26.8 %collective-permute-start.18 = (bf16[4,48,1152]{2,1,0:T(8,128)(2,1)S(1)}, bf16[4,48,1152]{2,1,0:T(8,128)(2,1)S(1)}, u32[]{:S(2)}, u32[]{:S(2)}) collective-permute-start(bf16[4,48,1152]{2,1,0:T(8,128)(2,1)S(1)} %get-tuple-element.457), channel_id=1, source_target_pairs={{0,8},{2,10},{4,12},{6,14},{8,0},{10,2},{12,4},{14,6},{16,24},{18,... | collective-permute-start | bytes 1327112 | tf_op jit(solution)/shard_map/ppermute | solution.py:220
  167.3 26.7 %collective-permute-start.19 = (bf16[4,48,1152]{2,1,0:T(8,128)(2,1)S(1)}, bf16[4,48,1152]{2,1,0:T(8,128)(2,1)S(1)}, u32[]{:S(2)}, u32[]{:S(2)}) collective-permute-start(bf16[4,48,1152]{2,1,0:T(8,128)(2,1)S(1)} %get-tuple-element.458), channel_id=1, source_target_pairs={{0,2},{2,0},{4,6},{6,4},{8,10},{10,8},{12,14},{14,12},{16,18},{18,... | collective-permute-start | bytes 1327112 | tf_op jit(solution)/shard_map/ppermute | solution.py:220
  195.0 11.7 %copy-start.28 = (bf16[2,48,1152]{2,1,0:T(8,128)(2,1)}, bf16[2,48,1152]{2,1,0:T(8,128)(2,1)S(1)}, u32[]{:S(2)}) copy-start(bf16[2,48,1152]{2,1,0:T(8,128)(2,1)S(1)} %get-tuple-element.478.refs_1_) | copy-start | bytes 663556
  195.0 11.7 %copy-start.30 = (bf16[2,48,1152]{2,1,0:T(8,128)(2,1)}, bf16[2,48,1152]{2,1,0:T(8,128)(2,1)S(1)}, u32[]{:S(2)}) copy-start(bf16[2,48,1152]{2,1,0:T(8,128)(2,1)S(1)} %get-tuple-element.479.refs_2_) | copy-start | bytes 663556
  195.0 11.7 %collective-permute-start.21 = (bf16[2,48,1152]{2,1,0:T(8,128)(2,1)S(1)}, bf16[2,48,1152]{2,1,0:T(8,128)(2,1)S(1)}, u32[]{:S(2)}, u32[]{:S(2)}) collective-permute-start(bf16[2,48,1152]{2,1,0:T(8,128)(2,1)S(1)} %get-tuple-element.480), channel_id=1, source_target_pairs={{0,2},{2,0},{4,6},{6,4},{8,10},{10,8},{12,14},{14,12},{16,18},{18,... | collective-permute-start | bytes 663560 | tf_op jit(solution)/shard_map/ppermute | solution.py:220
  195.0 11.7 %collective-permute-start.22 = (bf16[2,48,1152]{2,1,0:T(8,128)(2,1)S(1)}, bf16[2,48,1152]{2,1,0:T(8,128)(2,1)S(1)}, u32[]{:S(2)}, u32[]{:S(2)}) collective-permute-start(bf16[2,48,1152]{2,1,0:T(8,128)(2,1)S(1)} %get-tuple-element.481), channel_id=1, source_target_pairs={{0,16},{2,18},{4,20},{6,22},{8,24},{10,26},{12,28},{14,30},{16,0},... | collective-permute-start | bytes 663560 | tf_op jit(solution)/shard_map/ppermute | solution.py:220
  196.9 11.4 %collective-permute-start.23 = (bf16[2,48,1152]{2,1,0:T(8,128)(2,1)S(1)}, bf16[2,48,1152]{2,1,0:T(8,128)(2,1)S(1)}, u32[]{:S(2)}, u32[]{:S(2)}) collective-permute-start(bf16[2,48,1152]{2,1,0:T(8,128)(2,1)S(1)} %get-tuple-element.482), channel_id=1, source_target_pairs={{0,8},{2,10},{4,12},{6,14},{8,0},{10,2},{12,4},{14,6},{16,24},{18,... | collective-permute-start | bytes 663560 | tf_op jit(solution)/shard_map/ppermute | solution.py:220
  209.0 89.7 %all-to-all-start.1 = ((bf16[16,128,768]{2,1,0:T(8,128)(2,1)}), bf16[16,128,768]{2,1,0:T(8,128)(2,1)S(1)}, u32[]{:S(2)}, u32[]{:S(2)}) async-start(bf16[16,128,768]{2,1,0:T(8,128)(2,1)} %get-tuple-element.530), calls=%async_computation.1 | async-start | bytes 6291456 | tf_op jit(solution)/shard_map/all_to_all | solution.py:1553
  214.2 30.9 %collective-permute-start.24 = (f32[512,768]{1,0:T(8,128)}, f32[512,768]{1,0:T(8,128)}, u32[]{:S(2)}, u32[]{:S(2)}) collective-permute-start(f32[512,768]{1,0:T(8,128)} %product.1), channel_id=1, source_target_pairs={{0,1},{1,0},{2,3},{3,2},{4,5},{5,4},{6,7},{7,6},{8,9},{9,8},{10,11... | collective-permute-start | bytes 4718600 | tf_op jit(solution)/shard_map/ppermute | solution.py:59
  220.5 48.8 %collective-permute-start.26 = (bf16[1,48,1152]{2,1,0:T(8,128)(2,1)}, bf16[1,48,1152]{2,1,0:T(8,128)(2,1)S(1)}, u32[]{:S(2)}, u32[]{:S(2)}) collective-permute-start(bf16[1,48,1152]{2,1,0:T(8,128)(2,1)} %get-tuple-element.522), channel_id=1, source_target_pairs={{0,4},{2,6},{4,0},{6,2},{8,12},{10,14},{12,8},{14,10},{16,20},{18,... | collective-permute-start | bytes 331784 | tf_op jit(solution)/shard_map/ppermute | solution.py:220
  222.4 46.9 %collective-permute-start.27 = (bf16[1,48,1152]{2,1,0:T(8,128)(2,1)}, bf16[1,48,1152]{2,1,0:T(8,128)(2,1)S(1)}, u32[]{:S(2)}, u32[]{:S(2)}) collective-permute-start(bf16[1,48,1152]{2,1,0:T(8,128)(2,1)} %get-tuple-element.523), channel_id=1, source_target_pairs={{0,4},{2,6},{4,0},{6,2},{8,12},{10,14},{12,8},{14,10},{16,20},{18,... | collective-permute-start | bytes 331784 | tf_op jit(solution)/shard_map/ppermute | solution.py:220
  223.9 21.1 %copy-start.48 = (f32[768]{0:T(1024)S(1)}, f32[768]{0:T(1024)}, u32[]{:S(2)}) copy-start(f32[768]{0:T(1024)} %param.33) | copy-start | bytes 9220
  224.6 3.6 %collective-permute-start = (f32[512,768]{1,0:T(8,128)S(1)}, f32[512,768]{1,0:T(8,128)S(1)}, u32[]{:S(2)}, u32[]{:S(2)}) collective-permute-start(f32[512,768]{1,0:T(8,128)S(1)} %get-tuple-element.78.own), channel_id=1, source_target_pairs={{0,1},{1,0},{2,3},{3,2},{4,5},{5,4},{6,7},{7,6},{8,9},{9,8},{10,11... | collective-permute-start | bytes 4718600 | tf_op jit(solution)/shard_map/cond/branch_1_fun/ppermute | solution.py:59
  238.0 6.8 %collective-permute-start.1 = (f32[512,768]{1,0:T(8,128)}, f32[512,768]{1,0:T(8,128)}, u32[]{:S(2)}, u32[]{:S(2)}) collective-permute-start(f32[512,768]{1,0:T(8,128)} %get-tuple-element.635), channel_id=1, source_target_pairs={{0,1},{1,0},{2,3},{3,2},{4,5},{5,4},{6,7},{7,6},{8,9},{9,8},{10,11... | collective-permute-start | bytes 4718600 | tf_op jit(solution)/shard_map/cond/branch_1_fun/ppermute | solution.py:59
  238.3 3.0 collective-permute-start.2
  245.7 12.7 %copy-start.41 = (f32[512,768]{1,0:T(8,128)S(1)}, f32[512,768]{1,0:T(8,128)}, u32[]{:S(2)}) copy-start(f32[512,768]{1,0:T(8,128)} %get-tuple-element.113.grad_first) | copy-start | bytes 4718596 | tf_op jit(solution)/shard_map/cond
  245.7 12.7 %copy-start.56 = (f32[512,768]{1,0:T(8,128)S(1)}, f32[512,768]{1,0:T(8,128)}, u32[]{:S(2)}) copy-start(f32[512,768]{1,0:T(8,128)} %get-tuple-element.115.result_own) | copy-start | bytes 4718596 | tf_op jit(solution)/shard_map/cond
  245.7 12.7 %copy-start.57 = (bf16[512,768]{1,0:T(8,128)(2,1)S(1)}, bf16[512,768]{1,0:T(8,128)(2,1)}, u32[]{:S(2)}) copy-start(bf16[512,768]{1,0:T(8,128)(2,1)} %get-tuple-element.100.values) | copy-start | bytes 2359300 | tf_op jit(solution)/shard_map/cond
  245.7 12.7 %copy-start.62 = (f32[512,768]{1,0:T(8,128)S(1)}, f32[512,768]{1,0:T(8,128)}, u32[]{:S(2)}) copy-start(f32[512,768]{1,0:T(8,128)} %get-tuple-element.114.second) | copy-start | bytes 4718596 | tf_op jit(solution)/shard_map/cond
  245.7 12.7 %copy-start.72 = (f32[8,768]{1,0:T(8,128)S(1)}, f32[8,768]{1,0:T(8,128)}, u32[]{:S(2)}) copy-start(f32[8,768]{1,0:T(8,128)} %get-tuple-element.117.act_sums) | copy-start | bytes 73732 | tf_op jit(solution)/shard_map/cond
  245.7 12.7 %copy-start.73 = (f32[8,768]{1,0:T(8,128)S(1)}, f32[8,768]{1,0:T(8,128)}, u32[]{:S(2)}) copy-start(f32[8,768]{1,0:T(8,128)} %get-tuple-element.119.ffn_gain_grad) | copy-start | bytes 73732 | tf_op jit(solution)/shard_map/cond
  258.2 5.0 %collective-permute-start.3 = (bf16[768,384]{1,0:T(8,128)(2,1)S(1)}, bf16[768,384]{1,0:T(8,128)(2,1)S(1)}, u32[]{:S(2)}, u32[]{:S(2)}) collective-permute-start(bf16[768,384]{1,0:T(8,128)(2,1)S(1)} %get-tuple-element.121), channel_id=1, source_target_pairs={{0,1},{1,0},{2,3},{3,2},{4,5},{5,4},{6,7},{7,6},{8,9},{9,8},{10,11... | collective-permute-start | bytes 1769480 | tf_op jit(solution)/shard_map/cond/branch_1_fun/ppermute | solution.py:59
  263.2 1.2 collective-permute-start.4
  264.4 31.6 %copy-start.38 = (bf16[4,2,2,48,1152]{4,3,2,1,0:T(8,128)(2,1)}, bf16[4,2,2,48,1152]{4,3,2,1,0:T(8,128)(2,1)S(1)}, u32[]{:S(2)}) copy-start(bf16[4,2,2,48,1152]{4,3,2,1,0:T(8,128)(2,1)S(1)} %get-tuple-element.520.refs_3_) | copy-start | bytes 5308420
  265.5 33.2 %collective-permute-start.30 = (bf16[8,48,1152]{2,1,0:T(8,128)(2,1)}, bf16[8,48,1152]{2,1,0:T(8,128)(2,1)}, u32[]{:S(2)}, u32[]{:S(2)}) collective-permute-start(bf16[8,48,1152]{2,1,0:T(8,128)(2,1)} %bitcast.35), channel_id=1, source_target_pairs={{0,4},{2,6},{4,0},{6,2},{8,12},{10,14},{12,8},{14,10},{16,20},{18,... | collective-permute-start | bytes 2654216 | tf_op jit(solution)/shard_map/ppermute | solution.py:220
  269.3 29.4 %collective-permute-start.28 = (bf16[8,48,1024]{2,1,0:T(8,128)(2,1)}, bf16[8,48,1024]{2,1,0:T(8,128)(2,1)}, u32[]{:S(2)}, u32[]{:S(2)}) collective-permute-start(bf16[8,48,1024]{2,1,0:T(8,128)(2,1)} %dynamic-slice_bitcast_fusion.1), channel_id=1, source_target_pairs={{0,2},{2,0},{4,6},{6,4},{8,10},{10,8},{12,14},{14,12},{16,18},{18,... | collective-permute-start | bytes 2359304 | tf_op jit(solution)/shard_map/ppermute | solution.py:220
  270.8 27.9 %collective-permute-start.29 = (bf16[8,48,896]{2,1,0:T(8,128)(2,1)}, bf16[8,48,896]{2,1,0:T(8,128)(2,1)}, u32[]{:S(2)}, u32[]{:S(2)}) collective-permute-start(bf16[8,48,896]{2,1,0:T(8,128)(2,1)} %bitcast.34), channel_id=1, source_target_pairs={{0,8},{2,10},{4,12},{6,14},{8,0},{10,2},{12,4},{14,6},{16,24},{18,... | collective-permute-start | bytes 2064392 | tf_op jit(solution)/shard_map/ppermute | solution.py:220
  272.2 26.5 %collective-permute-start.25 = (bf16[1,48,1152]{2,1,0:T(8,128)(2,1)S(1)}, bf16[1,48,1152]{2,1,0:T(8,128)(2,1)}, u32[]{:S(2)}, u32[]{:S(2)}) collective-permute-start(bf16[1,48,1152]{2,1,0:T(8,128)(2,1)S(1)} %get-tuple-element.521), channel_id=1, source_target_pairs={{0,16},{2,18},{4,20},{6,22},{8,24},{10,26},{12,28},{14,30},{16,0},... | collective-permute-start | bytes 331784 | tf_op jit(solution)/shard_map/ppermute | solution.py:220
  274.6 20.3 %collective-permute-start.32 = (f32[16,8,128]{2,1,0:T(8,128)S(1)}, f32[16,8,128]{2,1,0:T(8,128)S(1)}, u32[]{:S(2)}, u32[]{:S(2)}) collective-permute-start(f32[16,8,128]{2,1,0:T(8,128)S(1)} %copy-done.44), channel_id=1, source_target_pairs={{0,2},{2,0},{4,6},{6,4},{8,10},{10,8},{12,14},{14,12},{16,18},{18,... | collective-permute-start | bytes 196616 | tf_op jit(solution)/shard_map/ppermute | solution.py:1548
  294.9 3.8 %collective-permute-start.31 = (f32[6,8,128]{2,1,0:T(8,128)S(1)}, f32[6,8,128]{2,1,0:T(8,128)S(1)}, u32[]{:S(2)}, u32[]{:S(2)}) collective-permute-start(f32[6,8,128]{2,1,0:T(8,128)S(1)} %get-tuple-element.531), channel_id=1, source_target_pairs={{0,2},{2,0},{4,6},{6,4},{8,10},{10,8},{12,14},{14,12},{16,18},{18,... | collective-permute-start | bytes 73736 | tf_op jit(solution)/shard_map/ppermute | solution.py:1548
  299.6 11.6 %copy-start.42 = (f32[16,8,128]{2,1,0:T(8,128)S(1)}, f32[16,8,128]{2,1,0:T(8,128)}, u32[]{:S(2)}) copy-start(f32[16,8,128]{2,1,0:T(8,128)} %add.143) | copy-start | bytes 196612
  302.6 20.6 %collective-permute-start.35 = (bf16[4,48,1152]{2,1,0:T(8,128)(2,1)S(1)}, bf16[4,48,1152]{2,1,0:T(8,128)(2,1)S(1)}, u32[]{:S(2)}, u32[]{:S(2)}) collective-permute-start(bf16[4,48,1152]{2,1,0:T(8,128)(2,1)S(1)} %get-tuple-element.548), channel_id=1, source_target_pairs={{0,8},{2,10},{4,12},{6,14},{8,0},{10,2},{12,4},{14,6},{16,24},{18,... | collective-permute-start | bytes 1327112 | tf_op jit(solution)/shard_map/ppermute | solution.py:220
  308.3 14.9 %collective-permute-start.33 = (bf16[4,48,1024]{2,1,0:T(8,128)(2,1)S(1)}, bf16[4,48,1024]{2,1,0:T(8,128)(2,1)S(1)}, u32[]{:S(2)}, u32[]{:S(2)}) collective-permute-start(bf16[4,48,1024]{2,1,0:T(8,128)(2,1)S(1)} %get-tuple-element.546), channel_id=1, source_target_pairs={{0,4},{2,6},{4,0},{6,2},{8,12},{10,14},{12,8},{14,10},{16,20},{18,... | collective-permute-start | bytes 1179656 | tf_op jit(solution)/shard_map/ppermute | solution.py:220
  309.7 13.4 %collective-permute-start.34 = (bf16[4,48,896]{2,1,0:T(8,128)(2,1)S(1)}, bf16[4,48,896]{2,1,0:T(8,128)(2,1)S(1)}, u32[]{:S(2)}, u32[]{:S(2)}) collective-permute-start(bf16[4,48,896]{2,1,0:T(8,128)(2,1)S(1)} %get-tuple-element.547), channel_id=1, source_target_pairs={{0,2},{2,0},{4,6},{6,4},{8,10},{10,8},{12,14},{14,12},{16,18},{18,... | collective-permute-start | bytes 1032200 | tf_op jit(solution)/shard_map/ppermute | solution.py:220
  311.2 7.6 %collective-permute-start.37 = (f32[16,8,128]{2,1,0:T(8,128)S(1)}, f32[16,8,128]{2,1,0:T(8,128)S(1)}, u32[]{:S(2)}, u32[]{:S(2)}) collective-permute-start(f32[16,8,128]{2,1,0:T(8,128)S(1)} %copy-done.42), channel_id=1, source_target_pairs={{0,4},{2,6},{4,0},{6,2},{8,12},{10,14},{12,8},{14,10},{16,20},{18,... | collective-permute-start | bytes 196616 | tf_op jit(solution)/shard_map/ppermute | solution.py:1548
  318.8 4.3 %collective-permute-start.38 = (f32[16,8,128]{2,1,0:T(8,128)S(1)}, f32[16,8,128]{2,1,0:T(8,128)S(1)}, u32[]{:S(2)}, u32[]{:S(2)}) collective-permute-start(f32[16,8,128]{2,1,0:T(8,128)S(1)} %add.145), channel_id=1, source_target_pairs={{0,8},{2,10},{4,12},{6,14},{8,0},{10,2},{12,4},{14,6},{16,24},{18,... | collective-permute-start | bytes 196616 | tf_op jit(solution)/shard_map/ppermute | solution.py:1548
  319.2 3.9 %collective-permute-start.36 = (f32[6,8,128]{2,1,0:T(8,128)S(1)}, f32[6,8,128]{2,1,0:T(8,128)S(1)}, u32[]{:S(2)}, u32[]{:S(2)}) collective-permute-start(f32[6,8,128]{2,1,0:T(8,128)S(1)} %add.144), channel_id=1, source_target_pairs={{0,4},{2,6},{4,0},{6,2},{8,12},{10,14},{12,8},{14,10},{16,20},{18,... | collective-permute-start | bytes 73736 | tf_op jit(solution)/shard_map/ppermute | solution.py:1548
  323.5 6.5 %collective-permute-start.43 = (f32[16,8,128]{2,1,0:T(8,128)S(1)}, f32[16,8,128]{2,1,0:T(8,128)S(1)}, u32[]{:S(2)}, u32[]{:S(2)}) collective-permute-start(f32[16,8,128]{2,1,0:T(8,128)S(1)} %add.146), channel_id=1, source_target_pairs={{0,16},{2,18},{4,20},{6,22},{8,24},{10,26},{12,28},{14,30},{16,0},... | collective-permute-start | bytes 196616 | tf_op jit(solution)/shard_map/ppermute | solution.py:1548
  326.7 7.9 %collective-permute-start.39 = (bf16[2,48,1024]{2,1,0:T(8,128)(2,1)S(1)}, bf16[2,48,1024]{2,1,0:T(8,128)(2,1)S(1)}, u32[]{:S(2)}, u32[]{:S(2)}) collective-permute-start(bf16[2,48,1024]{2,1,0:T(8,128)(2,1)S(1)} %get-tuple-element.562), channel_id=1, source_target_pairs={{0,8},{2,10},{4,12},{6,14},{8,0},{10,2},{12,4},{14,6},{16,24},{18,... | collective-permute-start | bytes 589832 | tf_op jit(solution)/shard_map/ppermute | solution.py:220
  327.9 6.7 %collective-permute-start.40 = (bf16[2,48,896]{2,1,0:T(8,128)(2,1)S(1)}, bf16[2,48,896]{2,1,0:T(8,128)(2,1)S(1)}, u32[]{:S(2)}, u32[]{:S(2)}) collective-permute-start(bf16[2,48,896]{2,1,0:T(8,128)(2,1)S(1)} %get-tuple-element.563), channel_id=1, source_target_pairs={{0,4},{2,6},{4,0},{6,2},{8,12},{10,14},{12,8},{14,10},{16,20},{18,... | collective-permute-start | bytes 516104 | tf_op jit(solution)/shard_map/ppermute | solution.py:220
  327.9 6.7 %collective-permute-start.41 = (bf16[2,48,1152]{2,1,0:T(8,128)(2,1)S(1)}, bf16[2,48,1152]{2,1,0:T(8,128)(2,1)S(1)}, u32[]{:S(2)}, u32[]{:S(2)}) collective-permute-start(bf16[2,48,1152]{2,1,0:T(8,128)(2,1)S(1)} %get-tuple-element.564), channel_id=1, source_target_pairs={{0,2},{2,0},{4,6},{6,4},{8,10},{10,8},{12,14},{14,12},{16,18},{18,... | collective-permute-start | bytes 663560 | tf_op jit(solution)/shard_map/ppermute | solution.py:220
  329.1 5.5 %collective-permute-start.42 = (f32[6,8,128]{2,1,0:T(8,128)S(1)}, f32[6,8,128]{2,1,0:T(8,128)S(1)}, u32[]{:S(2)}, u32[]{:S(2)}) collective-permute-start(f32[6,8,128]{2,1,0:T(8,128)S(1)} %add.147), channel_id=1, source_target_pairs={{0,8},{2,10},{4,12},{6,14},{8,0},{10,2},{12,4},{14,6},{16,24},{18,... | collective-permute-start | bytes 73736 | tf_op jit(solution)/shard_map/ppermute | solution.py:1548
  334.8 13.7 %collective-permute-start.44 = (bf16[1,48,1024]{2,1,0:T(8,128)(2,1)S(1)}, bf16[1,48,1024]{2,1,0:T(8,128)(2,1)S(1)}, u32[]{:S(2)}, u32[]{:S(2)}) collective-permute-start(bf16[1,48,1024]{2,1,0:T(8,128)(2,1)S(1)} %get-tuple-element.575), channel_id=1, source_target_pairs={{0,16},{2,18},{4,20},{6,22},{8,24},{10,26},{12,28},{14,30},{16,0},... | collective-permute-start | bytes 294920 | tf_op jit(solution)/shard_map/ppermute | solution.py:220
  336.8 11.6 %collective-permute-start.45 = (bf16[1,48,896]{2,1,0:T(8,128)(2,1)S(1)}, bf16[1,48,896]{2,1,0:T(8,128)(2,1)S(1)}, u32[]{:S(2)}, u32[]{:S(2)}) collective-permute-start(bf16[1,48,896]{2,1,0:T(8,128)(2,1)S(1)} %get-tuple-element.576), channel_id=1, source_target_pairs={{0,16},{2,18},{4,20},{6,22},{8,24},{10,26},{12,28},{14,30},{16,0},... | collective-permute-start | bytes 258056 | tf_op jit(solution)/shard_map/ppermute | solution.py:220
  337.8 10.7 %collective-permute-start.46 = (bf16[1,48,1152]{2,1,0:T(8,128)(2,1)S(1)}, bf16[1,48,1152]{2,1,0:T(8,128)(2,1)S(1)}, u32[]{:S(2)}, u32[]{:S(2)}) collective-permute-start(bf16[1,48,1152]{2,1,0:T(8,128)(2,1)S(1)} %get-tuple-element.577), channel_id=1, source_target_pairs={{0,16},{2,18},{4,20},{6,22},{8,24},{10,26},{12,28},{14,30},{16,0},... | collective-permute-start | bytes 331784 | tf_op jit(solution)/shard_map/ppermute | solution.py:220
  339.8 8.6 %collective-permute-start.47 = (f32[6,8,128]{2,1,0:T(8,128)S(1)}, f32[6,8,128]{2,1,0:T(8,128)S(1)}, u32[]{:S(2)}, u32[]{:S(2)}) collective-permute-start(f32[6,8,128]{2,1,0:T(8,128)S(1)} %add.149), channel_id=1, source_target_pairs={{0,16},{2,18},{4,20},{6,22},{8,24},{10,26},{12,28},{14,30},{16,0},... | collective-permute-start | bytes 73736 | tf_op jit(solution)/shard_map/ppermute | solution.py:1548
  348.6 1.5 collective-permute-start.48
  (62 other events, 251.8 us)
